TPU v7x, 128 devices: a whole 4x4x4 slice. The times are simulated.
128 devices in a mesh: row: 16 (over x, y_lo, core), col: 8 (over z, y_hi).
Axes of the slice: x: 4, y: 4 (y_hi: 2, y_lo: 2; y = y_hi * 2 + y_lo), z: 4, core: 2. Of those that a mesh axis runs over, the one named last changes fastest.
Arguments:
- features: float32 [8, 64, 128, 1280], P('col', 'row'), may hold values from -256 to 256
- timestep: int32 [8], P('col'), may hold values from 0 to 999
- w_time: float32 [320, 1280], replicated, may hold values from -0.3125 to 0.3125
- w_emb: float32 [1280, 1280], replicated, may hold values from -0.15625 to 0.15625
- b_emb: float32 [1280], replicated, may hold values from -4 to 4
- gn_gain: float32 [1280], replicated, may hold values from 0.5 to 1.5
- gn_bias: float32 [1280], replicated, may hold values from -3 to 3
- w_query: bfloat16 [1280, 640], P('col'), may hold values from -0.5 to 0.5
- w_key: bfloat16 [1280, 640], P('col'), may hold values from -0.5 to 0.5
- w_value: bfloat16 [1280, 640], P('col'), may hold values from -0.15625 to 0.15625
- w_out: bfloat16 [640, 1280], P(None, 'col'), may hold values from -0.25 to 0.25
Outputs:
- block_out: float32 [8, 64, 128, 1280], P('col', 'row')
All inputs are finite; a program needn't handle non-finite values.
Results may differ from a plain program's by a relative error of at most 0.0035.
The roundings to bfloat16 on the way count: a program that leaves them out, or rounds other values in their place, can miss the bound.
Values may be sent and summed in bfloat16 or wider, within the bound.
No kernel may reach another device: no remote copies, remote signals or barrier semaphores. Data moves between devices by JAX's collectives and lax.ppermute only.
A program may use at most 128 MiB of HBM per device.

v0:
```python
import math

import jax
import jax.numpy as jnp
from jax import lax
from jax.sharding import PartitionSpec as P

GROUPS = 32
HEADS = 10
HEAD = 64


def time_shift(step_value, w_time, w_emb, b_emb):
    half = w_time.shape[0] // 2
    freqs = jnp.exp(-math.log(10000.0) * jnp.arange(half, dtype=jnp.float32) / half)
    angles = step_value.astype(jnp.float32) * freqs
    table = jnp.concatenate([jnp.cos(angles), jnp.sin(angles)])[None, :]
    hidden = jax.nn.silu(jnp.dot(table, w_time, precision=lax.Precision.HIGHEST))
    return jnp.dot(hidden, w_emb, precision=lax.Precision.HIGHEST) + b_emb[None, :]


def attend_block(query3, carry, keys, values):
    count = keys.shape[0]
    heads = query3.shape[1]
    size = query3.shape[2]
    key3 = keys.reshape(count, heads, size)
    value3 = values.reshape(count, heads, size)
    scores = jnp.einsum("qhd,khd->hqk", query3, key3, preferred_element_type=jnp.float32) * (
        1.0 / math.sqrt(size)
    )
    top, total, accum = carry
    new_top = jnp.maximum(top, jnp.max(scores, axis=-1))
    factor = jnp.exp(top - new_top)
    weights = jnp.exp(scores - new_top[:, :, None])
    total = total * factor + jnp.sum(weights, axis=-1)
    update = jnp.einsum(
        "hqk,khd->qhd", weights.astype(jnp.bfloat16), value3, preferred_element_type=jnp.float32
    )
    accum = accum * jnp.transpose(factor)[:, :, None] + update
    return (new_top, total, accum)


def attend_piece(query3, carry, piece):
    keys, values = piece
    count = keys.shape[0]
    width = keys.shape[1]
    key_blocks = keys.reshape(count // 1024, 1024, width)
    value_blocks = values.reshape(count // 1024, 1024, width)

    def step(state, pair):
        return (attend_block(query3, state, pair[0], pair[1]), 0)

    carry, unused = lax.scan(step, carry, (key_blocks, value_blocks))
    return carry


def start_state(pixels, heads, size):
    return (
        jnp.full((heads, pixels), -1e30, jnp.float32),
        jnp.zeros((heads, pixels), jnp.float32),
        jnp.zeros((pixels, heads, size), jnp.float32),
    )


def finish(state, pixels, width):
    top, total, accum = state
    return (accum / jnp.transpose(total)[:, :, None]).astype(jnp.bfloat16).reshape(pixels, width)


def local(
    features, timestep, w_time, w_emb, b_emb, gn_gain, gn_bias, w_query, w_key, w_value, w_out
):
    unused_one, rows_here, cols_here, channels = features.shape
    pixels = rows_here * cols_here
    groups = GROUPS
    heads = HEADS
    size = HEAD
    inner = heads * size
    full_query, full_key, full_value = (
        lax.all_gather(w_query, "col", axis=0, tiled=True),
        lax.all_gather(w_key, "col", axis=0, tiled=True),
        lax.all_gather(w_value, "col", axis=0, tiled=True),
    )
    full_out = lax.all_gather(w_out, "col", axis=1, tiled=True)
    shift = time_shift(timestep[0], w_time, w_emb, b_emb)
    lifted = features.reshape(pixels, channels) + shift
    grouped = lifted.reshape(pixels, groups, channels // groups)
    entries = float(pixels * lax.axis_size("row") * (channels // groups))
    mean = lax.psum(jnp.sum(grouped, axis=(0, 2)), "row") / entries
    centred = grouped - mean[None, :, None]
    var = lax.psum(jnp.sum(centred * centred, axis=(0, 2)), "row") / entries
    normed = (centred / jnp.sqrt(var + 1e-06)[None, :, None]).reshape(
        pixels, channels
    ) * gn_gain + gn_bias
    normed = normed.astype(jnp.bfloat16)
    query = jnp.dot(normed, full_query, preferred_element_type=jnp.float32).astype(jnp.bfloat16)
    keys = jnp.dot(normed, full_key, preferred_element_type=jnp.float32).astype(jnp.bfloat16)
    values = jnp.dot(normed, full_value, preferred_element_type=jnp.float32).astype(jnp.bfloat16)
    query3 = query.reshape(pixels, heads, size)
    state = attend_piece(
        query3,
        start_state(pixels, heads, size),
        (
            lax.all_gather(keys, "row", axis=0, tiled=True),
            lax.all_gather(values, "row", axis=0, tiled=True),
        ),
    )
    attended = finish(state, pixels, inner)
    block_out = lifted + jnp.dot(attended, full_out, preferred_element_type=jnp.float32)
    return block_out.reshape(1, rows_here, cols_here, channels)


def solution(mesh):
    return jax.shard_map(
        local,
        mesh=mesh,
        in_specs=(
            P("col", "row", None, None),
            P("col"),
            P(),
            P(),
            P(),
            P(),
            P(),
            P("col", None),
            P("col", None),
            P("col", None),
            P(None, "col"),
        ),
        out_specs=P("col", "row", None, None),
        check_vma=False,
    )
```

profile of v0, /device:TPU:2, one launch (start us, length us, event | category | flops | bytes accessed | tf_op | source)
XLA Modules:
  0.0 579.9 jit_solution(12418883745088037709)
XLA Ops:
  6.5 0.7 all-gather.7.cloned.1.call-update
  7.3 0.7 all-gather.13.cloned.1.call-update
  8.1 0.7 all-gather.11.cloned.1.call-update
  9.6 0.9 convolution_reduce_fusion.1
  10.5 6.1 %convolution_reduce_fusion = f32[1280]{0:T(1024)S(1)} fusion(f32[1280,1]{0,1:T(1,128)S(1)} %reshape.77, f32[1280,1280]{1,0:T(8,128)} %param.16), kind=kOutput, calls=%fused_computation.26 | convolution fusion | flops 19660800 | bytes 6563840 | tf_op jit(solution)/shard_map/dot_general | solution.py:19
  17.1 23.6 %psum.14 = f32[32]{0:T(128)S(1)} all-reduce(f32[32]{0:T(128)S(1)} %reduce_sum.36), channel_id=1, replica_groups=mesh['row'=16,'col'=8] {'row'}, use_global_device_ids=true, to_apply=%region_2.3 | all-reduce | flops 32 | bytes 256 | tf_op jit(solution)/shard_map/psum | solution.py:89
  40.9 2.1 multiply_reduce_fusion
  43.2 27.2 %psum.15 = f32[32]{0:T(128)S(1)} all-reduce(f32[32]{0:T(128)S(1)} %reduce_sum.46), channel_id=1, replica_groups=mesh['row'=16,'col'=8] {'row'}, use_global_device_ids=true, to_apply=%region_5.6 | all-reduce | flops 32 | bytes 256 | tf_op jit(solution)/shard_map/psum | solution.py:91
  70.6 3.8 add_convert_fusion
  74.4 3.5 convolution_convert_fusion.2
  77.9 35.6 %all-gather.13.cloned.1.call-done = bf16[1280,640]{1,0:T(8,128)(2,1)} async-done(((bf16[160,640]{1,0:T(8,128)(2,1)}), bf16[1280,640]{1,0:T(8,128)(2,1)}) %all-gather.13.cloned.1.call-update) | async-done | bytes 1638416 | tf_op jit(solution)/shard_map/all_gather | solution.py:82
  113.6 3.4 convolution_convert_fusion
  117.7 47.0 %all-gather.11.cloned.1.call-done = bf16[1280,640]{1,0:T(8,128)(2,1)} async-done(((bf16[160,640]{1,0:T(8,128)(2,1)}), bf16[1280,640]{1,0:T(8,128)(2,1)}) %all-gather.11.cloned.1.call-update) | async-done | bytes 1638416 | tf_op jit(solution)/shard_map/all_gather | solution.py:80
  164.6 2.6 convolution_convert_fusion.1
  167.3 1.1 copy.21
  168.3 58.2 %all-gather.9.cloned.1.call-done = bf16[8192,640]{1,0:T(8,128)(2,1)} async-done(((bf16[512,640]{1,0:T(8,128)(2,1)}), bf16[8192,640]{1,0:T(8,128)(2,1)}) %all-gather.9.cloned.1.call-update) | async-done | bytes 10485776 | tf_op jit(solution)/shard_map/all_gather | solution.py:104
  226.6 64.4 %all-gather.15.cloned.1.call-done = bf16[8192,640]{1,0:T(8,128)(2,1)} async-done(((bf16[512,640]{1,0:T(8,128)(2,1)}), bf16[8192,640]{1,0:T(8,128)(2,1)}) %all-gather.15.cloned.1.call-update) | async-done | bytes 10485776 | tf_op jit(solution)/shard_map/all_gather | solution.py:105
  291.0 275.5 %while.15 = (s32[]{:T(128)}, f32[10,512]{1,0:T(8,128)S(1)}, f32[10,512]{1,0:T(8,128)S(1)}, f32[512,10,64]{0,2,1:T(8,128)}, bf16[8,1024,640]{2,1,0:T(8,128)(2,1)}...) while((s32[]{:T(128)}, f32[10,512]{1,0:T(8,128)S(1)}, ...), condition=%wide.region_9.10_spmd.clone, body=%wide.region_6.9_spmd.clone.sunk | while | flops 1385134080 | bytes 79626344 | solution.py:53
  291.0 3.0 constant_dynamic-slice_fusion.3
  294.0 1.6 copy.29
  295.6 9.9 %bitcast_reduce_fusion.2 = (f32[10,512]{1,0:T(8,128)S(1)}, f32[10,1024,512]{2,1,0:T(8,128)}) fusion(bf16[1024,10,64]{0,2,1:T(8,128)(2,1)S(1)} %bitcast.67, bf16[512,10,64]{0,2,1:T(8,128)(2,1)} %get-tuple-element.192), kind=kOutput, calls=%fused_computation.1.clone.1 | convolution fusion | flops 681569280 | bytes 22958080 | tf_op jit(solution)/shard_map/while/body/eval_jaxpr/qhd,khd->hqk/dot_general | solution.py:28
  305.5 0.7 copy.30
  306.2 10.1 %fusion.46 = f32[512,10,64]{0,2,1:T(8,128)} fusion(bf16[1024,10,64]{0,2,1:T(8,128)(2,1)S(1)} %bitcast.68, f32[10,1024,512]{2,1,0:T(8,128)} %get-tuple-element.166, f32[10,512]{1,0:T(8,128)S(1)} %get-tuple-element.188, f32[512,10,64]{0,2,1:T(8,128)} %get-tuple-element.181, f32[512,10]{0,1:T(8,128)S(1)} %get-tuple-element.168, pred[]{:T(512)S(6)} %compare.3), kind=kOutput, calls=%fused_computation.7.clone.1 | convolution fusion | flops 687800320 | bytes 24944640 | tf_op jit(solution)/shard_map/while/body/eval_jaxpr/hqk,khd->qhd/dot_general | solution.py:36
  316.3 9.0 %fusion.44 = f32[10,512]{1,0:T(8,128)S(1)} fusion(f32[10,1024,512]{2,1,0:T(8,128)} %get-tuple-element.166, f32[10,512]{1,0:T(8,128)S(1)} %get-tuple-element.188), kind=kLoop, calls=%fused_computation.4.clone.1 | loop fusion | flops 15723520 | bytes 21012480 | tf_op jit(solution)/shard_map/while/body/eval_jaxpr/reduce_sum | solution.py:35
  325.3 3.0 constant_dynamic-slice_fusion.3
  328.3 1.6 copy.29
  329.9 9.8 %bitcast_reduce_fusion.2 = (f32[10,512]{1,0:T(8,128)S(1)}, f32[10,1024,512]{2,1,0:T(8,128)}) fusion(bf16[1024,10,64]{0,2,1:T(8,128)(2,1)S(1)} %bitcast.67, bf16[512,10,64]{0,2,1:T(8,128)(2,1)} %get-tuple-element.192), kind=kOutput, calls=%fused_computation.1.clone.1 | convolution fusion | flops 681569280 | bytes 22958080 | tf_op jit(solution)/shard_map/while/body/eval_jaxpr/qhd,khd->hqk/dot_general | solution.py:28
  339.7 0.7 copy.30
  340.4 10.4 %fusion.46 = f32[512,10,64]{0,2,1:T(8,128)} fusion(bf16[1024,10,64]{0,2,1:T(8,128)(2,1)S(1)} %bitcast.68, f32[10,1024,512]{2,1,0:T(8,128)} %get-tuple-element.166, f32[10,512]{1,0:T(8,128)S(1)} %get-tuple-element.188, f32[512,10,64]{0,2,1:T(8,128)} %get-tuple-element.181, f32[512,10]{0,1:T(8,128)S(1)} %get-tuple-element.168, pred[]{:T(512)S(6)} %compare.3), kind=kOutput, calls=%fused_computation.7.clone.1 | convolution fusion | flops 687800320 | bytes 24944640 | tf_op jit(solution)/shard_map/while/body/eval_jaxpr/hqk,khd->qhd/dot_general | solution.py:36
  350.8 9.0 %fusion.44 = f32[10,512]{1,0:T(8,128)S(1)} fusion(f32[10,1024,512]{2,1,0:T(8,128)} %get-tuple-element.166, f32[10,512]{1,0:T(8,128)S(1)} %get-tuple-element.188), kind=kLoop, calls=%fused_computation.4.clone.1 | loop fusion | flops 15723520 | bytes 21012480 | tf_op jit(solution)/shard_map/while/body/eval_jaxpr/reduce_sum | solution.py:35
  359.9 3.0 constant_dynamic-slice_fusion.3
  362.9 1.6 copy.29
  364.5 9.7 %bitcast_reduce_fusion.2 = (f32[10,512]{1,0:T(8,128)S(1)}, f32[10,1024,512]{2,1,0:T(8,128)}) fusion(bf16[1024,10,64]{0,2,1:T(8,128)(2,1)S(1)} %bitcast.67, bf16[512,10,64]{0,2,1:T(8,128)(2,1)} %get-tuple-element.192), kind=kOutput, calls=%fused_computation.1.clone.1 | convolution fusion | flops 681569280 | bytes 22958080 | tf_op jit(solution)/shard_map/while/body/eval_jaxpr/qhd,khd->hqk/dot_general | solution.py:28
  374.2 0.7 copy.30
  374.9 10.4 %fusion.46 = f32[512,10,64]{0,2,1:T(8,128)} fusion(bf16[1024,10,64]{0,2,1:T(8,128)(2,1)S(1)} %bitcast.68, f32[10,1024,512]{2,1,0:T(8,128)} %get-tuple-element.166, f32[10,512]{1,0:T(8,128)S(1)} %get-tuple-element.188, f32[512,10,64]{0,2,1:T(8,128)} %get-tuple-element.181, f32[512,10]{0,1:T(8,128)S(1)} %get-tuple-element.168, pred[]{:T(512)S(6)} %compare.3), kind=kOutput, calls=%fused_computation.7.clone.1 | convolution fusion | flops 687800320 | bytes 24944640 | tf_op jit(solution)/shard_map/while/body/eval_jaxpr/hqk,khd->qhd/dot_general | solution.py:36
  385.3 9.0 %fusion.44 = f32[10,512]{1,0:T(8,128)S(1)} fusion(f32[10,1024,512]{2,1,0:T(8,128)} %get-tuple-element.166, f32[10,512]{1,0:T(8,128)S(1)} %get-tuple-element.188), kind=kLoop, calls=%fused_computation.4.clone.1 | loop fusion | flops 15723520 | bytes 21012480 | tf_op jit(solution)/shard_map/while/body/eval_jaxpr/reduce_sum | solution.py:35
  394.3 3.0 constant_dynamic-slice_fusion.3
  397.3 1.6 copy.29
  398.9 9.7 %bitcast_reduce_fusion.2 = (f32[10,512]{1,0:T(8,128)S(1)}, f32[10,1024,512]{2,1,0:T(8,128)}) fusion(bf16[1024,10,64]{0,2,1:T(8,128)(2,1)S(1)} %bitcast.67, bf16[512,10,64]{0,2,1:T(8,128)(2,1)} %get-tuple-element.192), kind=kOutput, calls=%fused_computation.1.clone.1 | convolution fusion | flops 681569280 | bytes 22958080 | tf_op jit(solution)/shard_map/while/body/eval_jaxpr/qhd,khd->hqk/dot_general | solution.py:28
  408.6 0.7 copy.30
  409.3 10.4 %fusion.46 = f32[512,10,64]{0,2,1:T(8,128)} fusion(bf16[1024,10,64]{0,2,1:T(8,128)(2,1)S(1)} %bitcast.68, f32[10,1024,512]{2,1,0:T(8,128)} %get-tuple-element.166, f32[10,512]{1,0:T(8,128)S(1)} %get-tuple-element.188, f32[512,10,64]{0,2,1:T(8,128)} %get-tuple-element.181, f32[512,10]{0,1:T(8,128)S(1)} %get-tuple-element.168, pred[]{:T(512)S(6)} %compare.3), kind=kOutput, calls=%fused_computation.7.clone.1 | convolution fusion | flops 687800320 | bytes 24944640 | tf_op jit(solution)/shard_map/while/body/eval_jaxpr/hqk,khd->qhd/dot_general | solution.py:36
  419.7 9.0 %fusion.44 = f32[10,512]{1,0:T(8,128)S(1)} fusion(f32[10,1024,512]{2,1,0:T(8,128)} %get-tuple-element.166, f32[10,512]{1,0:T(8,128)S(1)} %get-tuple-element.188), kind=kLoop, calls=%fused_computation.4.clone.1 | loop fusion | flops 15723520 | bytes 21012480 | tf_op jit(solution)/shard_map/while/body/eval_jaxpr/reduce_sum | solution.py:35
  428.7 3.0 constant_dynamic-slice_fusion.3
  431.8 1.6 copy.29
  433.4 9.7 %bitcast_reduce_fusion.2 = (f32[10,512]{1,0:T(8,128)S(1)}, f32[10,1024,512]{2,1,0:T(8,128)}) fusion(bf16[1024,10,64]{0,2,1:T(8,128)(2,1)S(1)} %bitcast.67, bf16[512,10,64]{0,2,1:T(8,128)(2,1)} %get-tuple-element.192), kind=kOutput, calls=%fused_computation.1.clone.1 | convolution fusion | flops 681569280 | bytes 22958080 | tf_op jit(solution)/shard_map/while/body/eval_jaxpr/qhd,khd->hqk/dot_general | solution.py:28
  443.7 10.4 %fusion.46 = f32[512,10,64]{0,2,1:T(8,128)} fusion(bf16[1024,10,64]{0,2,1:T(8,128)(2,1)S(1)} %bitcast.68, f32[10,1024,512]{2,1,0:T(8,128)} %get-tuple-element.166, f32[10,512]{1,0:T(8,128)S(1)} %get-tuple-element.188, f32[512,10,64]{0,2,1:T(8,128)} %get-tuple-element.181, f32[512,10]{0,1:T(8,128)S(1)} %get-tuple-element.168, pred[]{:T(512)S(6)} %compare.3), kind=kOutput, calls=%fused_computation.7.clone.1 | convolution fusion | flops 687800320 | bytes 24944640 | tf_op jit(solution)/shard_map/while/body/eval_jaxpr/hqk,khd->qhd/dot_general | solution.py:36
  454.1 9.0 %fusion.44 = f32[10,512]{1,0:T(8,128)S(1)} fusion(f32[10,1024,512]{2,1,0:T(8,128)} %get-tuple-element.166, f32[10,512]{1,0:T(8,128)S(1)} %get-tuple-element.188), kind=kLoop, calls=%fused_computation.4.clone.1 | loop fusion | flops 15723520 | bytes 21012480 | tf_op jit(solution)/shard_map/while/body/eval_jaxpr/reduce_sum | solution.py:35
  463.2 3.0 constant_dynamic-slice_fusion.3
  466.2 1.6 copy.29
  467.8 9.7 %bitcast_reduce_fusion.2 = (f32[10,512]{1,0:T(8,128)S(1)}, f32[10,1024,512]{2,1,0:T(8,128)}) fusion(bf16[1024,10,64]{0,2,1:T(8,128)(2,1)S(1)} %bitcast.67, bf16[512,10,64]{0,2,1:T(8,128)(2,1)} %get-tuple-element.192), kind=kOutput, calls=%fused_computation.1.clone.1 | convolution fusion | flops 681569280 | bytes 22958080 | tf_op jit(solution)/shard_map/while/body/eval_jaxpr/qhd,khd->hqk/dot_general | solution.py:28
  478.2 10.4 %fusion.46 = f32[512,10,64]{0,2,1:T(8,128)} fusion(bf16[1024,10,64]{0,2,1:T(8,128)(2,1)S(1)} %bitcast.68, f32[10,1024,512]{2,1,0:T(8,128)} %get-tuple-element.166, f32[10,512]{1,0:T(8,128)S(1)} %get-tuple-element.188, f32[512,10,64]{0,2,1:T(8,128)} %get-tuple-element.181, f32[512,10]{0,1:T(8,128)S(1)} %get-tuple-element.168, pred[]{:T(512)S(6)} %compare.3), kind=kOutput, calls=%fused_computation.7.clone.1 | convolution fusion | flops 687800320 | bytes 24944640 | tf_op jit(solution)/shard_map/while/body/eval_jaxpr/hqk,khd->qhd/dot_general | solution.py:36
  488.6 9.0 %fusion.44 = f32[10,512]{1,0:T(8,128)S(1)} fusion(f32[10,1024,512]{2,1,0:T(8,128)} %get-tuple-element.166, f32[10,512]{1,0:T(8,128)S(1)} %get-tuple-element.188), kind=kLoop, calls=%fused_computation.4.clone.1 | loop fusion | flops 15723520 | bytes 21012480 | tf_op jit(solution)/shard_map/while/body/eval_jaxpr/reduce_sum | solution.py:35
  497.6 3.0 constant_dynamic-slice_fusion.3
  500.6 1.6 copy.29
  502.2 9.7 %bitcast_reduce_fusion.2 = (f32[10,512]{1,0:T(8,128)S(1)}, f32[10,1024,512]{2,1,0:T(8,128)}) fusion(bf16[1024,10,64]{0,2,1:T(8,128)(2,1)S(1)} %bitcast.67, bf16[512,10,64]{0,2,1:T(8,128)(2,1)} %get-tuple-element.192), kind=kOutput, calls=%fused_computation.1.clone.1 | convolution fusion | flops 681569280 | bytes 22958080 | tf_op jit(solution)/shard_map/while/body/eval_jaxpr/qhd,khd->hqk/dot_general | solution.py:28
  512.6 10.4 %fusion.46 = f32[512,10,64]{0,2,1:T(8,128)} fusion(bf16[1024,10,64]{0,2,1:T(8,128)(2,1)S(1)} %bitcast.68, f32[10,1024,512]{2,1,0:T(8,128)} %get-tuple-element.166, f32[10,512]{1,0:T(8,128)S(1)} %get-tuple-element.188, f32[512,10,64]{0,2,1:T(8,128)} %get-tuple-element.181, f32[512,10]{0,1:T(8,128)S(1)} %get-tuple-element.168, pred[]{:T(512)S(6)} %compare.3), kind=kOutput, calls=%fused_computation.7.clone.1 | convolution fusion | flops 687800320 | bytes 24944640 | tf_op jit(solution)/shard_map/while/body/eval_jaxpr/hqk,khd->qhd/dot_general | solution.py:36
  523.0 9.0 %fusion.44 = f32[10,512]{1,0:T(8,128)S(1)} fusion(f32[10,1024,512]{2,1,0:T(8,128)} %get-tuple-element.166, f32[10,512]{1,0:T(8,128)S(1)} %get-tuple-element.188), kind=kLoop, calls=%fused_computation.4.clone.1 | loop fusion | flops 15723520 | bytes 21012480 | tf_op jit(solution)/shard_map/while/body/eval_jaxpr/reduce_sum | solution.py:35
  532.1 3.0 constant_dynamic-slice_fusion.3
  535.1 1.6 copy.29
  536.7 9.7 %bitcast_reduce_fusion.2 = (f32[10,512]{1,0:T(8,128)S(1)}, f32[10,1024,512]{2,1,0:T(8,128)}) fusion(bf16[1024,10,64]{0,2,1:T(8,128)(2,1)S(1)} %bitcast.67, bf16[512,10,64]{0,2,1:T(8,128)(2,1)} %get-tuple-element.192), kind=kOutput, calls=%fused_computation.1.clone.1 | convolution fusion | flops 681569280 | bytes 22958080 | tf_op jit(solution)/shard_map/while/body/eval_jaxpr/qhd,khd->hqk/dot_general | solution.py:28
  547.1 10.4 %fusion.46 = f32[512,10,64]{0,2,1:T(8,128)} fusion(bf16[1024,10,64]{0,2,1:T(8,128)(2,1)S(1)} %bitcast.68, f32[10,1024,512]{2,1,0:T(8,128)} %get-tuple-element.166, f32[10,512]{1,0:T(8,128)S(1)} %get-tuple-element.188, f32[512,10,64]{0,2,1:T(8,128)} %get-tuple-element.181, f32[512,10]{0,1:T(8,128)S(1)} %get-tuple-element.168, pred[]{:T(512)S(6)} %compare.3), kind=kOutput, calls=%fused_computation.7.clone.1 | convolution fusion | flops 687800320 | bytes 24944640 | tf_op jit(solution)/shard_map/while/body/eval_jaxpr/hqk,khd->qhd/dot_general | solution.py:36
  557.5 9.0 %fusion.44 = f32[10,512]{1,0:T(8,128)S(1)} fusion(f32[10,1024,512]{2,1,0:T(8,128)} %get-tuple-element.166, f32[10,512]{1,0:T(8,128)S(1)} %get-tuple-element.188), kind=kLoop, calls=%fused_computation.4.clone.1 | loop fusion | flops 15723520 | bytes 21012480 | tf_op jit(solution)/shard_map/while/body/eval_jaxpr/reduce_sum | solution.py:35
  566.5 1.5 divide_convert_fusion
  568.0 5.1 convolution_add_fusion
  (71 shorter events, 4.9 us)
Async XLA Ops:
  6.5 3.0 copy-start
  6.5 67.9 %all-gather.7.cloned.1.call-start = ((), (), s32[]{:S(2)}) async-start(), calls=%async_computation | async-start | bytes 1843200 | tf_op jit(solution)/shard_map/all_gather | solution.py:81
  7.3 106.3 %all-gather.13.cloned.1.call-start = ((), (), s32[]{:S(2)}) async-start(), calls=%async_computation.3 | async-start | bytes 1843200 | tf_op jit(solution)/shard_map/all_gather | solution.py:82
  8.0 156.6 %all-gather.11.cloned.1.call-start = ((), (), s32[]{:S(2)}) async-start(), calls=%async_computation.2 | async-start | bytes 1843200 | tf_op jit(solution)/shard_map/all_gather | solution.py:80
  8.7 217.8 %all-gather.9.cloned.1.call-start = ((), (), s32[]{:S(2)}) async-start(), calls=%async_computation.1 | async-start | bytes 11141120 | tf_op jit(solution)/shard_map/all_gather | solution.py:104
  10.5 6.1 %copy-start.5 = (f32[1280]{0:T(1024)S(1)}, f32[1280]{0:T(1024)}, u32[]{:S(2)}) copy-start(f32[1280]{0:T(1024)} %param.17) | copy-start | bytes 15364
  10.5 6.1 %copy-start.2 = (f32[1,4,128,1280]{3,2,1,0:T(8,128)S(1)}, f32[1,4,128,1280]{3,2,1,0:T(8,128)}, u32[]{:S(2)}) copy-start(f32[1,4,128,1280]{3,2,1,0:T(8,128)} %param.13) | copy-start | bytes 7864324
  16.9 53.7 %copy-start.3 = (f32[1280]{0:T(1024)S(1)}, f32[1280]{0:T(1024)}, u32[]{:S(2)}) copy-start(f32[1280]{0:T(1024)} %param.19) | copy-start | bytes 15364
  16.9 53.8 %copy-start.4 = (f32[1280]{0:T(1024)S(1)}, f32[1280]{0:T(1024)}, u32[]{:S(2)}) copy-start(f32[1280]{0:T(1024)} %param.18) | copy-start | bytes 15364
  77.9 213.1 %all-gather.15.cloned.1.call-start = ((), (), s32[]{:S(2)}) async-start(), calls=%async_computation.4 | async-start | bytes 11141120 | tf_op jit(solution)/shard_map/all_gather | solution.py:105
  117.1 450.9 %all-gather.17.cloned.1.call-start = ((), (), s32[]{:S(2)}) async-start(), calls=%async_computation.5 | async-start | bytes 1843200 | tf_op jit(solution)/shard_map/all_gather | solution.py:84
  568.0 5.1 copy-start.1
Sparse Core Ops, SparseCore 0:
  9.7 52.8 all-gather.6
  64.8 48.7 all-gather.12
  115.9 48.7 all-gather.10
  166.2 60.3 all-gather.8
  228.1 62.8 all-gather.14
  293.1 51.1 all-gather.16
where the time goes:
time: 583 us; the launch traced here: 580 us
  waiting for transfers between devices  208 us (36%)
  matrix products  182 us (31%)
  other arithmetic  80.1 us (14%)
  blocking collectives  50.9 us (9%)
  local copies, waits for them, and re-layouts  43.8 us (8%)
  between operations  14.3 us (2%)
    dot_general x8, matrix products, attend_block(): jnp.einsum('hqk,khd->qhd', weights.astype(jnp.bfloat16), value3, preferre...  82.9 us
    dot_general x8, matrix products, attend_block(): jnp.einsum('qhd,khd->hqk', query3, key3, preferred_element_type=jnp.float32)  77.9 us
    reduce_sum x8, other arithmetic, attend_block(): total = total * factor + jnp.sum(weights, axis=-1)  71.8 us
    all_gather x1, waiting for transfers between devices, local(): lax.all_gather(values, 'row', axis=0, tiled=True)  64.4 us
    all_gather x1, waiting for transfers between devices, local(): lax.all_gather(keys, 'row', axis=0, tiled=True)  58.2 us
    all_gather x1, waiting for transfers between devices, local(): lax.all_gather(w_query, 'col', axis=0, tiled=True)  47 us
    dynamic_slice x24, local copies, waits for them, and re-layouts, attend_piece(): carry, unused = lax.scan(step, carry, (key_blocks, value_blocks))  42.2 us
    all_gather x1, waiting for transfers between devices, local(): lax.all_gather(w_value, 'col', axis=0, tiled=True)  35.6 us
  transfers between devices with their start and end apart: 6, of which 4 were waited for; matrix products, arithmetic and copies ran while one was open for 52% of the time, Pallas kernels for 0%

commit v1 on v0

v1 whole, which is shorter than its diff:
```python
import functools
import math

import jax
import jax.numpy as jnp
from jax import lax
from jax.experimental import pallas as pl
from jax.experimental.pallas import tpu as pltpu
from jax.sharding import PartitionSpec as P

GROUPS = 32
HEADS = 10
HEAD = 64
CHIPS = 8
F32 = jnp.float32
BF16 = jnp.bfloat16
SCALE = math.log2(math.e) / math.sqrt(HEAD)


def time_shift(step_value, w_time, w_emb, b_emb):
    half = w_time.shape[0] // 2
    freqs = jnp.exp(-math.log(10000.0) * jnp.arange(half, dtype=F32) / half)
    angles = step_value.astype(F32) * freqs
    table = jnp.concatenate([jnp.cos(angles), jnp.sin(angles)])[None, :]
    hidden = jax.nn.silu(jnp.dot(table, w_time, precision=lax.Precision.HIGHEST))
    return jnp.dot(hidden, w_emb, precision=lax.Precision.HIGHEST) + b_emb[None, :]


def move_row(value, target):
    return lax.ppermute(value, "row", [(r, target(r)) for r in range(16)])


def move_col(value, target):
    return lax.ppermute(value, "col", [(c, target(c)) for c in range(8)])


def along_x(step):
    return lambda r: ((r // 4 + step) % 4) * 4 + r % 4


def along_z(step):
    return lambda c: ((c // 2 + step) % 4) * 2 + c % 2


def other_core(value):
    return move_row(value, lambda r: r ^ 1)


def across_chips(value):
    groups = [list(range(0, 16, 2)), list(range(1, 16, 2))]
    return lax.all_to_all(value, "row", 0, 0, tiled=True, axis_index_groups=groups)


def pooled(parts, count):
    mean = sum(p[0] for p in parts) / len(parts)
    spread = sum(p[1] for p in parts) + count * sum((p[0] - mean) ** 2 for p in parts)
    return jnp.stack([mean, spread])


def pooled_over_row(stat, count):
    parts = [stat] + [move_row(stat, along_x(d)) for d in (1, 2, 3)]
    stat = pooled(parts, count)
    parts = [stat] + [move_row(stat, lambda r, k=k: r ^ k) for k in (1, 2, 3)]
    return pooled(parts, 4 * count)


def gathered_weights(w_query, w_key, w_value):
    core = lax.axis_index("row") % 2
    z = lax.axis_index("col") // 2
    y_hi = lax.axis_index("col") % 2
    half = w_key.shape[1] // 2
    first = jnp.concatenate([w_query, w_key[:, :half]], axis=1)
    second = jnp.concatenate([w_key[:, half:], w_value], axis=1)
    mine = jnp.where(core == 0, first, second)
    depth, width = mine.shape
    theirs = move_col(mine, lambda c: c ^ 1)
    slab = jnp.where(y_hi == 0, jnp.stack([mine, theirs]), jnp.stack([theirs, mine]))
    below = move_col(slab, along_z(1))
    above = move_col(slab, along_z(-1))
    far_0 = move_col(below[0], along_z(1))
    far_1 = move_col(above[1], along_z(-1))
    whole = jnp.zeros((2, 4, 2, depth, width), BF16)

    def put(whole, piece, where_z, where_y):
        at = (core, where_z % 4, where_y, 0, 0)
        whole = lax.dynamic_update_slice(whole, piece[None, None], at)
        at = (1 - core, where_z % 4, where_y, 0, 0)
        return lax.dynamic_update_slice(whole, other_core(piece)[None, None], at)

    whole = put(whole, slab, z, 0)
    whole = put(whole, below, z + 3, 0)
    whole = put(whole, above, z + 1, 0)
    whole = put(whole, far_0[None], z + 2, 0)
    whole = put(whole, far_1[None], z + 2, 1)
    return whole.reshape(2, 8 * depth, width)


def split3(value):
    high = value.astype(BF16)
    rest = value - high.astype(F32)
    middle = rest.astype(BF16)
    low = (rest - middle.astype(F32)).astype(BF16)
    return high, middle, low


def product(a, b):
    return lax.dot_general(a, b, (((1,), (0,)), ((), ())), preferred_element_type=F32)


def put_keys(keys, vals, place, key_t, value_t):
    count = key_t.shape[1]
    row = lax.broadcasted_iota(jnp.int32, (HEAD, count), 0)
    ones = jnp.where(row < 3, 1.0, 0.0).astype(BF16)
    wide = jnp.concatenate([key_t, key_t, key_t, ones], axis=0)
    keys[place : place + count, :] = wide.T
    vals[:, place : place + count] = value_t


def put_top(query, top):
    width = top.shape[1]
    row = lax.broadcasted_iota(jnp.int32, (HEAD, width), 0)
    high, middle, low = split3(-top)
    wide = [jnp.broadcast_to(part, (HEAD, width)).astype(F32) for part in (high, middle, low)]
    rows = jnp.where(row == 0, wide[0], jnp.where(row == 1, wide[1], jnp.where(row == 2, wide[2], 0.0)))
    query[3 * HEAD :, :] = rows.astype(BF16)


def attend_rows(query, keys, vals, total_ref, accum_ref, query_t, chunk):
    width = query_t.shape[1]
    count = keys.shape[0]
    for at, part in enumerate(split3(query_t.astype(F32) * SCALE)):
        query[at * HEAD : (at + 1) * HEAD, :] = part

    def scores(start, size):
        return product(keys[pl.ds(start, size), :], query[...])

    def run(top):
        put_top(query, top)

        def step(i, state):
            total, accum = state
            start = pl.multiple_of(i * chunk, chunk)
            weights = jnp.exp2(scores(start, chunk))
            total = total + jnp.sum(weights.reshape(chunk // 8, 8, width), axis=0)
            accum = accum + product(vals[:, pl.ds(start, chunk)], weights.astype(BF16))
            return total, accum

        state = (jnp.zeros((8, width), F32), jnp.zeros((HEAD, width), F32))
        total, accum = lax.fori_loop(0, count // chunk, step, state)
        total_ref[...] = jnp.sum(total, axis=0, keepdims=True)
        accum_ref[...] = accum

    query[3 * HEAD :, :] = jnp.zeros((HEAD, width), BF16)
    run(jnp.max(scores(0, 256), axis=0, keepdims=True))
    small = jnp.max(jnp.where(total_ref[...] < 1e30, 0.0, 1.0))

    @pl.when(small > 0.5)
    def _():
        query[3 * HEAD :, :] = jnp.zeros((HEAD, width), BF16)

        def step(i, top):
            start = pl.multiple_of(i * 512, 512)
            return jnp.maximum(top, jnp.max(scores(start, 512), axis=0, keepdims=True))

        run(lax.fori_loop(0, count // 512, step, jnp.full((1, width), -jnp.inf, F32)))

    return (accum_ref[...] / total_ref[...]).astype(BF16)


def attention_scratch(count, width):
    return [
        pltpu.VMEM((4 * HEAD, width), BF16),
        pltpu.VMEM((count, 4 * HEAD), BF16),
        pltpu.VMEM((HEAD, count), BF16),
        pltpu.VMEM((1, width), F32),
        pltpu.VMEM((HEAD, width), F32),
    ]


def cost(queries, count):
    return pl.CostEstimate(
        flops=4 * queries * count * HEAD, bytes_accessed=8 * 1024 * 1024, transcendentals=queries * count
    )


def one_head_kernel(query_ref, mine_ref, theirs_ref, out_ref, *scratch):
    query, keys, vals, total, accum = scratch
    sources, unused, pixels = mine_ref.shape
    per_step = query_ref.shape[0]

    @pl.when(pl.program_id(0) == 0)
    def _():
        for s in range(sources):
            put_keys(keys, vals, s * pixels, mine_ref[s, HEAD : 2 * HEAD], mine_ref[s, 2 * HEAD :])
            put_keys(keys, vals, (sources + s) * pixels, theirs_ref[s, :HEAD], theirs_ref[s, HEAD:])

    query_t = jnp.concatenate([query_ref[s] for s in range(per_step)], axis=1)
    attended = attend_rows(query, keys, vals, total, accum, query_t, 1024)
    for s in range(per_step):
        out_ref[s] = attended[:, s * pixels : (s + 1) * pixels]


def one_head(mine, theirs):
    sources, unused, pixels = mine.shape
    per_step = 2
    count = 2 * sources * pixels
    return pl.pallas_call(
        one_head_kernel,
        grid=(sources // per_step,),
        in_specs=[
            pl.BlockSpec((per_step, HEAD, pixels), lambda i: (i, 0, 0)),
            pl.BlockSpec(mine.shape, lambda i: (0, 0, 0)),
            pl.BlockSpec(theirs.shape, lambda i: (0, 0, 0)),
        ],
        out_specs=pl.BlockSpec((per_step, HEAD, pixels), lambda i: (i, 0, 0)),
        out_shape=jax.ShapeDtypeStruct((sources, HEAD, pixels), BF16),
        scratch_shapes=attention_scratch(count, per_step * pixels),
        compiler_params=pltpu.CompilerParams(vmem_limit_bytes=56 * 2**20),
        cost_estimate=cost(sources * pixels, count),
    )(mine, mine, theirs)


def own_rows_kernel(query_ref, key_ref, value_ref, out_ref, *scratch):
    query, keys, vals, total, accum = scratch
    sources, unused, pixels = key_ref.shape
    for s in range(sources):
        put_keys(keys, vals, s * pixels, key_ref[s], value_ref[s])
    out_ref[...] = attend_rows(query, keys, vals, total, accum, query_ref[...], 2048)


def own_rows(query_t, pairs):
    heads = query_t.shape[0] // HEAD
    sources, unused, pixels = pairs.shape
    count = sources * pixels
    return pl.pallas_call(
        own_rows_kernel,
        grid=(heads,),
        in_specs=[
            pl.BlockSpec((HEAD, pixels), lambda h: (h, 0)),
            pl.BlockSpec((sources, HEAD, pixels), lambda h: (0, h, 0)),
            pl.BlockSpec((sources, HEAD, pixels), lambda h: (0, heads + h, 0)),
        ],
        out_specs=pl.BlockSpec((HEAD, pixels), lambda h: (h, 0)),
        out_shape=jax.ShapeDtypeStruct(query_t.shape, BF16),
        scratch_shapes=attention_scratch(count, pixels),
        compiler_params=pltpu.CompilerParams(vmem_limit_bytes=56 * 2**20),
        cost_estimate=cost(heads * pixels, count),
    )(query_t, pairs, pairs)


def local(
    features, timestep, w_time, w_emb, b_emb, gn_gain, gn_bias, w_query, w_key, w_value, w_out
):
    unused_one, rows_here, cols_here, channels = features.shape
    pixels = rows_here * cols_here
    per_group = channels // GROUPS
    inner = HEADS * HEAD
    weights = gathered_weights(w_query, w_key, w_value)
    full_out = lax.all_gather(w_out, "col", axis=1, tiled=True)

    shift = time_shift(timestep[0], w_time, w_emb, b_emb)
    lifted = features.reshape(pixels, channels) + shift
    count = float(pixels * per_group)

    def by_group(value):
        return jnp.sum(jnp.sum(value, axis=0).reshape(GROUPS, per_group), axis=1)

    def by_channel(value):
        return jnp.repeat(value, per_group)[None, :]

    mean_here = by_group(lifted) / count
    spread_here = by_group((lifted - by_channel(mean_here)) ** 2)
    mean, spread = pooled_over_row(jnp.stack([mean_here, spread_here]), count)
    var = spread / (count * lax.axis_size("row"))
    normed = (lifted - by_channel(mean)) / by_channel(jnp.sqrt(var + 1e-06)) * gn_gain + gn_bias
    normed = normed.astype(BF16)

    rows = lax.dot_general(weights, normed, (((1,), (1,)), ((), ())), preferred_element_type=F32)
    rows = rows.astype(BF16).reshape(3, inner, pixels)
    first = CHIPS * HEAD
    by_head = rows[:, :first].reshape(3, CHIPS, HEAD, pixels).transpose(1, 0, 2, 3)
    mine = across_chips(by_head.reshape(CHIPS, 3 * HEAD, pixels))
    theirs = other_core(mine[:, HEAD:])
    pairs, mine = lax.optimization_barrier((rows[1:, first:], mine))
    pairs = lax.all_gather(pairs.reshape(2 * (inner - first), pixels), "row", axis=0, tiled=False)
    attended = across_chips(one_head(mine, theirs)).reshape(first, pixels)
    others = own_rows(rows[0, first:], pairs)
    attended = jnp.concatenate([attended, others], axis=0)
    added = lax.dot_general(attended, full_out, (((0,), (0,)), ((), ())), preferred_element_type=F32)
    return (lifted + added).reshape(1, rows_here, cols_here, channels)


def solution(mesh):
    return jax.shard_map(
        local,
        mesh=mesh,
        in_specs=(
            P("col", "row", None, None),
            P("col"),
            P(),
            P(),
            P(),
            P(),
            P(),
            P("col", None),
            P("col", None),
            P("col", None),
            P(None, "col"),
        ),
        out_specs=P("col", "row", None, None),
        check_vma=False,
    )
```

time: 583 us -> 261 us (0.45)
  matrix products: 182 us -> 15 us
  waiting for transfers between devices: 208 us -> 49.5 us
  Pallas kernels: 0 us -> 134 us
  other arithmetic: 80.1 us -> 9.06 us
  blocking collectives: 50.9 us -> 0 us
  local copies, waits for them, and re-layouts: 43.8 us -> 8.8 us
  starting transfers between devices: 0.38 us -> 28.8 us
    all_gather x5 -> x1, waiting for transfers between devices: 205 us -> 0.01 us  [local(): lax.all_gather(pairs.reshape(2 * (inner - first), pixels), 'row', axis=0,...]
    dot_general x20 -> x2, matrix products: 175 us -> 8.11 us  [the longest x1 5 us: local(): lax.dot_general(attended, full_out, (((0,), (0,)), ((), ())), preferred_e...]
    pallas_call x0 -> x2, Pallas kernels: none -> 134 us  [the longest x1 103 us: one_head(): pl.pallas_call(one_head_kernel, grid=(sources // per_step,), in_specs=[pl...]
    reduce_sum x12 -> x4, other arithmetic: 74.4 us -> 2.63 us  [by_group(): return jnp.sum(jnp.sum(value, axis=0).reshape(GROUPS, per_group), axis=1)]
    psum x2 -> x0, blocking collectives: 50.9 us -> none  [the longest x1 27.2 us: local(): var = lax.psum(jnp.sum(centred * centred, axis=(0, 2)), 'row') / entries]
    dynamic_slice x24 -> x0, local copies, waits for them, and re-layouts: 42.2 us -> none  [attend_piece(): carry, unused = lax.scan(step, carry, (key_blocks, value_blocks))]
    ppermute x0 -> x17, waiting for transfers between devices: none -> 28.7 us  [the longest x5 19.4 us: move_col(): return lax.ppermute(value, 'col', [(c, target(c)) for c in range(8)])]
    all_to_all x0 -> x2, waiting for transfers between devices: none -> 20.7 us  [across_chips(): lax.all_to_all(value, 'row', 0, 0, tiled=True, axis_index_groups=groups)]
  transfers between devices with their start and end apart: 6 -> 21, of which waited for: 4 -> 8; matrix products, arithmetic and copies ran while one was open for 52% -> 5% of each run, Pallas kernels for 0% -> 52%
where the time goes in v1:
time: 261 us; the launch traced here: 260 us
  Pallas kernels  134 us (51%)
  waiting for transfers between devices  49.5 us (19%)
  starting transfers between devices  28.8 us (11%)
  matrix products  15 us (6%)
  between operations  14.6 us (6%)
  other arithmetic  9.06 us (3%)
  local copies, waits for them, and re-layouts  8.8 us (3%)
    pallas_call x1, Pallas kernels, one_head(): pl.pallas_call(one_head_kernel, grid=(sources // per_step,), in_specs=[pl...  103 us
    pallas_call x1, Pallas kernels, own_rows(): pl.pallas_call(own_rows_kernel, grid=(heads,), in_specs=[pl.BlockSpec((HE...  31.6 us
    all_to_all x2, waiting for transfers between devices, across_chips(): lax.all_to_all(value, 'row', 0, 0, tiled=True, axis_index_groups=groups)  20.7 us
    ppermute x5, waiting for transfers between devices, move_col(): return lax.ppermute(value, 'col', [(c, target(c)) for c in range(8)])  19.4 us
    all_to_all x2, starting transfers between devices, across_chips(): lax.all_to_all(value, 'row', 0, 0, tiled=True, axis_index_groups=groups)  10.7 us
    ppermute x5, starting transfers between devices, move_col(): return lax.ppermute(value, 'col', [(c, target(c)) for c in range(8)])  10.6 us
    ppermute x12, waiting for transfers between devices, move_row(): return lax.ppermute(value, 'row', [(r, target(r)) for r in range(16)])  9.33 us
    ppermute x12, starting transfers between devices, move_row(): return lax.ppermute(value, 'row', [(r, target(r)) for r in range(16)])  7.46 us
  transfers between devices with their start and end apart: 21, of which 8 were waited for; matrix products, arithmetic and copies ran while one was open for 5% of the time, Pallas kernels for 52%

profile of v1, /device:TPU:2, one launch (start us, length us, event | category | flops | bytes accessed | tf_op | source)
XLA Modules:
  0.0 260.2 jit_solution(3860024460588187962)
XLA Ops:
  7.4 0.1 pad_maximum_fusion
  7.4 0.5 copy-done
  8.0 0.9 convolution_reduce_fusion.1
  8.9 6.1 %convolution_reduce_fusion = f32[1280]{0:T(1024)S(1)} fusion(f32[1280,1]{0,1:T(1,128)S(1)} %reshape.279, f32[1280,1280]{1,0:T(8,128)} %param.14), kind=kOutput, calls=%fused_computation.6 | convolution fusion | flops 19660800 | bytes 6563840 | tf_op jit(solution)/shard_map/dot_general | solution.py:26
  15.0 0.3 add_reduce_fusion
  15.3 0.1 reshape.270
  15.4 0.1 reduce_sum.37
  15.5 0.1 broadcast_in_dim.54
  15.6 0.1 sub.71
  15.7 2.1 multiply_reduce_fusion
  17.8 0.1 reshape.271
  17.9 0.1 reduce_sum.39
  18.0 1.6 collective-permute-start.10
  19.6 1.0 collective-permute-start.11
  20.6 2.2 collective-permute-start.12
  22.9 0.1 slice_bitcast_fusion.3
  23.0 0.1 maximum_select_fusion.3
  23.2 3.3 %collective-permute-start = (bf16[160,960]{1,0:T(8,128)(2,1)S(1)}, bf16[160,960]{1,0:T(8,128)(2,1)S(1)}, u32[]{:S(2)}, u32[]{:S(2)}) collective-permute-start(bf16[160,960]{1,0:T(8,128)(2,1)S(1)} %maximum_select_fusion.3), channel_id=1, source_target_pairs={{0,1},{1,0},{2,3},{3,2},{4,5},{5,4},{6,7},{7,6},{8,9},{9,8},{10,11... | collective-permute-start | bytes 921608 | tf_op jit(solution)/shard_map/ppermute | solution.py:34
  26.4 0.1 maximum_select_fusion.2
  26.7 0.1 collective-permute-start.13
  26.8 0.8 collective-permute-start.14
  27.5 1.1 collective-permute-start.15
  28.6 5.1 %collective-permute-done.14 = f32[2,32]{1,0:T(2,128)S(1)} collective-permute-done((f32[2,32]{1,0:T(2,128)S(1)}, f32[2,32]{1,0:T(2,128)S(1)}, u32[]{:S(2)}, u32[]{:S(2)}) %collective-permute-start.14) | collective-permute-done | bytes 288 | tf_op jit(solution)/shard_map/ppermute | solution.py:30
  33.8 0.1 broadcast_in_dim.56
  33.8 0.1 div.62
  33.9 0.1 broadcast_in_dim.55
  34.0 0.1 sub.78
  34.1 0.1 maximum_select_fusion.1
  34.2 0.2 collective-permute-start.1
  34.4 1.9 collective-permute-start.2
  36.3 2.2 collective-permute-start.4
  38.5 2.2 add_convert_fusion
  40.7 0.7 broadcast_in_dim.44
  41.4 0.2 fusion
  41.6 12.2 %collective-permute-done.2 = bf16[2,160,960]{2,1,0:T(8,128)(2,1)S(1)} collective-permute-done((bf16[2,160,960]{2,1,0:T(8,128)(2,1)S(1)}, bf16[2,160,960]{2,1,0:T(8,128)(2,1)S(1)}, u32[]{:S(2)}, u32[]{:S(2)}) %collective-permute-start.2) | collective-permute-done | bytes 614432 | tf_op jit(solution)/shard_map/ppermute | solution.py:34
  53.8 0.1 collective-permute-start.6
  53.8 0.1 collective-permute-start.3
  54.0 3.2 %collective-permute-start.8 = (bf16[160,960]{1,0:T(8,128)(2,1)S(1)}, bf16[160,960]{1,0:T(8,128)(2,1)S(1)}, u32[]{:S(2)}, u32[]{:S(2)}) collective-permute-start(bf16[160,960]{1,0:T(8,128)(2,1)S(1)} %slice_bitcast_fusion), channel_id=1, source_target_pairs={{0,6},{1,7},{2,0},{3,1},{4,2},{5,3},{6,4},{7,5},{8,14},{9,15},{10,... | collective-permute-start | bytes 921608 | tf_op jit(solution)/shard_map/ppermute | solution.py:34
  57.2 0.2 collective-permute-start.5
  57.4 0.1 bitcast_dynamic-update-slice_fusion.4
  57.5 0.1 bitcast_dynamic-update-slice_fusion.3
  57.5 6.9 %collective-permute-done.6 = bf16[160,960]{1,0:T(8,128)(2,1)S(1)} collective-permute-done((bf16[160,960]{1,0:T(8,128)(2,1)S(1)}, bf16[160,960]{1,0:T(8,128)(2,1)S(1)}, u32[]{:S(2)}, u32[]{:S(2)}) %collective-permute-start.6) | collective-permute-done | bytes 307232 | tf_op jit(solution)/shard_map/ppermute | solution.py:34
  64.5 0.3 collective-permute-done.8
  64.8 0.2 collective-permute-start.9
  65.0 0.1 bitcast_dynamic-update-slice_fusion.2
  65.1 0.1 bitcast_dynamic-update-slice_fusion.1
  65.1 0.1 bitcast_dynamic-update-slice_fusion
  65.2 0.9 collective-permute-done.7
  66.2 0.4 collective-permute-done.9
  66.6 3.1 %convolution_convert_fusion = bf16[2,960,512]{2,1,0:T(8,128)(2,1)S(1)} fusion(bf16[2,1280,960]{2,1,0:T(8,128)(2,1)S(1)} %bitcast.209, bf16[512,1280,1]{1,0,2:T(8,128)(2,1)S(1)} %bitcast.215), kind=kOutput, calls=%fused_computation.5 | convolution fusion | flops 2517565440 | bytes 8192000 | tf_op jit(solution)/shard_map/dot_general | solution.py:278
  69.7 0.1 slice.89
  69.8 1.4 copy.20
  71.3 0.3 copy-done.3
  71.6 4.9 %all-to-all-start = ((bf16[8,192,512]{2,1,0:T(8,128)(2,1)}), bf16[8,192,512]{2,1,0:T(8,128)(2,1)S(1)}, u32[]{:S(2)}, u32[]{:S(2)}) async-start(bf16[8,192,512]{2,1,0:T(8,128)(2,1)} %bitcast.42), calls=%async_computation | async-start | bytes 3145728 | tf_op jit(solution)/shard_map/all_to_all | solution.py:51
  76.5 1.7 slice.88
  78.2 20.7 %all-to-all-done.query_ref.mine_ref = bf16[8,192,512]{2,1,0:T(8,128)(2,1)S(1)} async-done(((bf16[8,192,512]{2,1,0:T(8,128)(2,1)}), bf16[8,192,512]{2,1,0:T(8,128)(2,1)S(1)}, u32[]{:S(2)}, u32[]{:S(2)}) %all-to-all-start) | async-done | bytes 1572896 | tf_op jit(solution)/shard_map/all_to_all | solution.py:51
  99.0 1.3 slice.90
  100.3 3.0 %collective-permute-done.16.theirs_ref = bf16[8,128,512]{2,1,0:T(8,128)(2,1)} collective-permute-done((bf16[8,128,512]{2,1,0:T(8,128)(2,1)}, bf16[8,128,512]{2,1,0:T(8,128)(2,1)}, u32[]{:S(2)}, u32[]{:S(2)}) %collective-permute-start.16) | collective-permute-done | bytes 1048608 | tf_op jit(solution)/shard_map/ppermute | solution.py:30
  103.2 102.8 %shard_map.109 = bf16[8,64,512]{2,1,0:T(8,128)(2,1)} custom-call(bf16[8,192,512]{2,1,0:T(8,128)(2,1)} %copy-done.2, bf16[8,192,512]{2,1,0:T(8,128)(2,1)} %copy-done.2, bf16[8,128,512]{2,1,0:T(8,128)(2,1)} %collective-permute-done.16.theirs_ref), custom_call_target="tpu_custom_call" | custom-call | flops 8589934592 | bytes 8388608 | tf_op jit(solution)/shard_map/pallas_call | solution.py:207
  206.0 5.8 %all-to-all-start.1 = ((bf16[8,64,512]{2,1,0:T(8,128)(2,1)}), bf16[8,64,512]{2,1,0:T(8,128)(2,1)S(1)}, u32[]{:S(2)}, u32[]{:S(2)}) async-start(bf16[8,64,512]{2,1,0:T(8,128)(2,1)} %shard_map.109), calls=%async_computation.1 | async-start | bytes 1048576 | tf_op jit(solution)/shard_map/all_to_all | solution.py:51
  211.8 3.4 %bitcast_add_fusion = f32[512,1280]{1,0:T(8,128)} fusion(f32[1,4,128,1280]{3,2,1,0:T(8,128)} %param.11, f32[1280]{0:T(1024)S(1)} %add.205), kind=kLoop, calls=%fused_computation.1 | loop fusion | flops 655360 | bytes 5248000 | tf_op jit(solution)/shard_map/add | solution.py:262
  215.2 1.6 slice_bitcast_fusion.2.query_ref
  216.8 31.6 %shard_map.110 = bf16[128,512]{1,0:T(8,128)(2,1)} custom-call(bf16[128,512]{1,0:T(8,128)(2,1)} %slice_bitcast_fusion.2.query_ref, bf16[16,256,512]{2,1,0:T(8,128)(2,1)} %all-gather.3.cloned.1.call-done.key_ref.value_ref, bf16[16,256,512]{2,1,0:T(8,128)(2,1)} %all-gather.3.cloned.1.call-done.key_ref.value_ref), custom_call_target="tpu_custom_call" | custom-call | flops 2147483648 | bytes 8388608 | tf_op jit(solution)/shard_map/pallas_call | solution.py:235
  248.4 5.0 %convolution_add_fusion = f32[512,1280]{1,0:T(8,128)} fusion(f32[512,1280]{1,0:T(8,128)} %bitcast_add_fusion, bf16[640,1280]{0,1:T(8,128)(2,1)} %all-gather.5.cloned.1.call-done, bf16[128,512]{1,0:T(8,128)(2,1)} %shard_map.110, bf16[512,512]{1,0:T(8,128)(2,1)S(1)} %bitcast.211), kind=kOutput, calls=%fused_computation | convolution fusion | flops 840826880 | bytes 7536640 | tf_op jit(solution)/shard_map/dot_general | solution.py:289
  (53 shorter events, 0.5 us)
Async XLA Ops:
  6.5 1.4 copy-start
  8.9 6.1 %copy-start.9 = (f32[1280]{0:T(1024)S(1)}, f32[1280]{0:T(1024)}, u32[]{:S(2)}) copy-start(f32[1280]{0:T(1024)} %param.15) | copy-start | bytes 15364
  8.9 6.1 %copy-start.1 = (f32[1,4,128,1280]{3,2,1,0:T(8,128)S(1)}, f32[1,4,128,1280]{3,2,1,0:T(8,128)}, u32[]{:S(2)}) copy-start(f32[1,4,128,1280]{3,2,1,0:T(8,128)} %param.11) | copy-start | bytes 7864324
  15.0 7.9 %copy-start.6 = (bf16[160,640]{1,0:T(8,128)(2,1)S(1)}, bf16[160,640]{1,0:T(8,128)(2,1)}, u32[]{:S(2)}) copy-start(bf16[160,640]{1,0:T(8,128)(2,1)} %param.19) | copy-start | bytes 614404
  15.0 8.0 %copy-start.4 = (bf16[160,640]{1,0:T(8,128)(2,1)S(1)}, bf16[160,640]{1,0:T(8,128)(2,1)}, u32[]{:S(2)}) copy-start(bf16[160,640]{1,0:T(8,128)(2,1)} %param.18) | copy-start | bytes 614404
  15.0 8.0 %copy-start.5 = (bf16[160,640]{1,0:T(8,128)(2,1)S(1)}, bf16[160,640]{1,0:T(8,128)(2,1)}, u32[]{:S(2)}) copy-start(bf16[160,640]{1,0:T(8,128)(2,1)} %param.20) | copy-start | bytes 614404
  17.8 20.7 %copy-start.7 = (f32[1280]{0:T(1024)S(1)}, f32[1280]{0:T(1024)}, u32[]{:S(2)}) copy-start(f32[1280]{0:T(1024)} %param.17) | copy-start | bytes 15364
  17.8 20.7 %copy-start.8 = (f32[1280]{0:T(1024)S(1)}, f32[1280]{0:T(1024)}, u32[]{:S(2)}) copy-start(f32[1280]{0:T(1024)} %param.16) | copy-start | bytes 15364
  18.0 8.6 %collective-permute-start.10 = (f32[2,32]{1,0:T(2,128)S(1)}, f32[2,32]{1,0:T(2,128)S(1)}, u32[]{:S(2)}, u32[]{:S(2)}) collective-permute-start(f32[2,32]{1,0:T(2,128)S(1)} %pad_maximum_fusion.1), channel_id=1, source_target_pairs={{0,32},{8,40},{16,48},{24,56},{32,64},{40,72},{48,80},{56,88},{64,... | collective-permute-start | bytes 776 | tf_op jit(solution)/shard_map/ppermute | solution.py:30
  19.6 7.0 %collective-permute-start.11 = (f32[2,32]{1,0:T(2,128)S(1)}, f32[2,32]{1,0:T(2,128)S(1)}, u32[]{:S(2)}, u32[]{:S(2)}) collective-permute-start(f32[2,32]{1,0:T(2,128)S(1)} %pad_maximum_fusion.1), channel_id=1, source_target_pairs={{0,64},{8,72},{16,80},{24,88},{32,96},{40,104},{48,112},{56,120},{... | collective-permute-start | bytes 776 | tf_op jit(solution)/shard_map/ppermute | solution.py:30
  20.6 6.0 %collective-permute-start.12 = (f32[2,32]{1,0:T(2,128)S(1)}, f32[2,32]{1,0:T(2,128)S(1)}, u32[]{:S(2)}, u32[]{:S(2)}) collective-permute-start(f32[2,32]{1,0:T(2,128)S(1)} %pad_maximum_fusion.1), channel_id=1, source_target_pairs={{0,96},{8,104},{16,112},{24,120},{32,0},{40,8},{48,16},{56,24},{64... | collective-permute-start | bytes 776 | tf_op jit(solution)/shard_map/ppermute | solution.py:30
  23.2 10.9 %collective-permute-start = (bf16[160,960]{1,0:T(8,128)(2,1)S(1)}, bf16[160,960]{1,0:T(8,128)(2,1)S(1)}, u32[]{:S(2)}, u32[]{:S(2)}) collective-permute-start(bf16[160,960]{1,0:T(8,128)(2,1)S(1)} %maximum_select_fusion.3), channel_id=1, source_target_pairs={{0,1},{1,0},{2,3},{3,2},{4,5},{5,4},{6,7},{7,6},{8,9},{9,8},{10,11... | collective-permute-start | bytes 921608 | tf_op jit(solution)/shard_map/ppermute | solution.py:34
  26.7 2.0 collective-permute-start.13
  26.8 6.9 %collective-permute-start.14 = (f32[2,32]{1,0:T(2,128)S(1)}, f32[2,32]{1,0:T(2,128)S(1)}, u32[]{:S(2)}, u32[]{:S(2)}) collective-permute-start(f32[2,32]{1,0:T(2,128)S(1)} %pad_maximum_fusion.2), channel_id=1, source_target_pairs={{0,16},{8,24},{16,0},{24,8},{32,48},{40,56},{48,32},{56,40},{64,80... | collective-permute-start | bytes 776 | tf_op jit(solution)/shard_map/ppermute | solution.py:30
  27.5 6.2 %collective-permute-start.15 = (f32[2,32]{1,0:T(2,128)S(1)}, f32[2,32]{1,0:T(2,128)S(1)}, u32[]{:S(2)}, u32[]{:S(2)}) collective-permute-start(f32[2,32]{1,0:T(2,128)S(1)} %pad_maximum_fusion.2), channel_id=1, source_target_pairs={{0,24},{8,16},{16,8},{24,0},{32,56},{40,48},{48,40},{56,32},{64,88... | collective-permute-start | bytes 776 | tf_op jit(solution)/shard_map/ppermute | solution.py:30
  34.2 23.2 %collective-permute-start.1 = (bf16[2,160,960]{2,1,0:T(8,128)(2,1)S(1)}, bf16[2,160,960]{2,1,0:T(8,128)(2,1)S(1)}, u32[]{:S(2)}, u32[]{:S(2)}) collective-permute-start(bf16[2,160,960]{2,1,0:T(8,128)(2,1)S(1)} %maximum_select_fusion.1), channel_id=1, source_target_pairs={{0,8},{8,0},{16,24},{24,16},{32,40},{40,32},{48,56},{56,48},{64,72... | collective-permute-start | bytes 1843208 | tf_op jit(solution)/shard_map/ppermute | solution.py:30
  34.4 19.3 %collective-permute-start.2 = (bf16[2,160,960]{2,1,0:T(8,128)(2,1)S(1)}, bf16[2,160,960]{2,1,0:T(8,128)(2,1)S(1)}, u32[]{:S(2)}, u32[]{:S(2)}) collective-permute-start(bf16[2,160,960]{2,1,0:T(8,128)(2,1)S(1)} %maximum_select_fusion.1), channel_id=1, source_target_pairs={{0,2},{1,3},{2,4},{3,5},{4,6},{5,7},{6,0},{7,1},{8,10},{9,11},{10,... | collective-permute-start | bytes 1843208 | tf_op jit(solution)/shard_map/ppermute | solution.py:34
  36.3 17.6 %collective-permute-start.4 = (bf16[2,160,960]{2,1,0:T(8,128)(2,1)S(1)}, bf16[2,160,960]{2,1,0:T(8,128)(2,1)S(1)}, u32[]{:S(2)}, u32[]{:S(2)}) collective-permute-start(bf16[2,160,960]{2,1,0:T(8,128)(2,1)S(1)} %maximum_select_fusion.1), channel_id=1, source_target_pairs={{0,6},{1,7},{2,0},{3,1},{4,2},{5,3},{6,4},{7,5},{8,14},{9,15},{10,... | collective-permute-start | bytes 1843208 | tf_op jit(solution)/shard_map/ppermute | solution.py:34
  53.8 10.7 %collective-permute-start.6 = (bf16[160,960]{1,0:T(8,128)(2,1)S(1)}, bf16[160,960]{1,0:T(8,128)(2,1)S(1)}, u32[]{:S(2)}, u32[]{:S(2)}) collective-permute-start(bf16[160,960]{1,0:T(8,128)(2,1)S(1)} %slice_bitcast_fusion.1), channel_id=1, source_target_pairs={{0,2},{1,3},{2,4},{3,5},{4,6},{5,7},{6,0},{7,1},{8,10},{9,11},{10,... | collective-permute-start | bytes 921608 | tf_op jit(solution)/shard_map/ppermute | solution.py:34
  53.8 11.2 %collective-permute-start.3 = (bf16[2,160,960]{2,1,0:T(8,128)(2,1)S(1)}, bf16[2,160,960]{2,1,0:T(8,128)(2,1)S(1)}, u32[]{:S(2)}, u32[]{:S(2)}) collective-permute-start(bf16[2,160,960]{2,1,0:T(8,128)(2,1)S(1)} %collective-permute-done.2), channel_id=1, source_target_pairs={{0,8},{8,0},{16,24},{24,16},{32,40},{40,32},{48,56},{56,48},{64,72... | collective-permute-start | bytes 1843208 | tf_op jit(solution)/shard_map/ppermute | solution.py:30
  54.0 10.8 %collective-permute-start.8 = (bf16[160,960]{1,0:T(8,128)(2,1)S(1)}, bf16[160,960]{1,0:T(8,128)(2,1)S(1)}, u32[]{:S(2)}, u32[]{:S(2)}) collective-permute-start(bf16[160,960]{1,0:T(8,128)(2,1)S(1)} %slice_bitcast_fusion), channel_id=1, source_target_pairs={{0,6},{1,7},{2,0},{3,1},{4,2},{5,3},{6,4},{7,5},{8,14},{9,15},{10,... | collective-permute-start | bytes 921608 | tf_op jit(solution)/shard_map/ppermute | solution.py:34
  57.2 8.0 %collective-permute-start.5 = (bf16[2,160,960]{2,1,0:T(8,128)(2,1)S(1)}, bf16[2,160,960]{2,1,0:T(8,128)(2,1)S(1)}, u32[]{:S(2)}, u32[]{:S(2)}) collective-permute-start(bf16[2,160,960]{2,1,0:T(8,128)(2,1)S(1)} %collective-permute-done.4), channel_id=1, source_target_pairs={{0,8},{8,0},{16,24},{24,16},{32,40},{40,32},{48,56},{56,48},{64,72... | collective-permute-start | bytes 1843208 | tf_op jit(solution)/shard_map/ppermute | solution.py:30
  64.5 1.6 collective-permute-start.7
  64.8 1.8 collective-permute-start.9
  69.7 1.9 copy-start.3
  71.6 27.3 %all-to-all-start = ((bf16[8,192,512]{2,1,0:T(8,128)(2,1)}), bf16[8,192,512]{2,1,0:T(8,128)(2,1)S(1)}, u32[]{:S(2)}, u32[]{:S(2)}) async-start(bf16[8,192,512]{2,1,0:T(8,128)(2,1)} %bitcast.42), calls=%async_computation | async-start | bytes 3145728 | tf_op jit(solution)/shard_map/all_to_all | solution.py:51
  76.5 140.3 %all-gather.3.cloned.1.call-start = ((), (), s32[]{:S(2)}) async-start(), calls=%async_computation.2 | async-start | bytes 4456448 | tf_op jit(solution)/shard_map/all_gather | solution.py:285
  98.9 4.3 %copy-start.2 = (bf16[8,192,512]{2,1,0:T(8,128)(2,1)}, bf16[8,192,512]{2,1,0:T(8,128)(2,1)S(1)}, u32[]{:S(2)}) copy-start(bf16[8,192,512]{2,1,0:T(8,128)(2,1)S(1)} %all-to-all-done.query_ref.mine_ref) | copy-start | bytes 4718596
  98.9 149.5 %all-gather.5.cloned.1.call-start = ((), (), s32[]{:S(2)}) async-start(), calls=%async_computation.3 | async-start | bytes 1843200 | tf_op jit(solution)/shard_map/all_gather | solution.py:259
  100.2 3.0 %collective-permute-start.16 = (bf16[8,128,512]{2,1,0:T(8,128)(2,1)}, bf16[8,128,512]{2,1,0:T(8,128)(2,1)}, u32[]{:S(2)}, u32[]{:S(2)}) collective-permute-start(bf16[8,128,512]{2,1,0:T(8,128)(2,1)} %slice.90), channel_id=1, source_target_pairs={{0,8},{8,0},{16,24},{24,16},{32,40},{40,32},{48,56},{56,48},{64,72... | collective-permute-start | bytes 3145736 | tf_op jit(solution)/shard_map/ppermute | solution.py:30
  206.0 42.4 %all-to-all-start.1 = ((bf16[8,64,512]{2,1,0:T(8,128)(2,1)}), bf16[8,64,512]{2,1,0:T(8,128)(2,1)S(1)}, u32[]{:S(2)}, u32[]{:S(2)}) async-start(bf16[8,64,512]{2,1,0:T(8,128)(2,1)} %shard_map.109), calls=%async_computation.1 | async-start | bytes 1048576 | tf_op jit(solution)/shard_map/all_to_all | solution.py:51
Sparse Core Ops, SparseCore 0:
  99.0 37.7 all-gather.2
  139.1 50.6 all-gather.4

commit v2 on v1

--- a/solution.py
+++ b/solution.py
@@ -64,16 +64,19 @@
     return pooled(parts, 4 * count)
 
 
-def gathered_weights(w_query, w_key, w_value):
+def half_weights(w_query, w_key, w_value):
+    core = lax.axis_index("row") % 2
+    half = w_key.shape[1] // 2
+    first = jnp.concatenate([w_query, w_key[:, :half]], axis=1)
+    second = jnp.concatenate([w_key[:, half:], w_value], axis=1)
+    return jnp.where(core == 0, first, second)
+
+
+def gathered_weights(mine, theirs):
     core = lax.axis_index("row") % 2
     z = lax.axis_index("col") // 2
     y_hi = lax.axis_index("col") % 2
-    half = w_key.shape[1] // 2
-    first = jnp.concatenate([w_query, w_key[:, :half]], axis=1)
-    second = jnp.concatenate([w_key[:, half:], w_value], axis=1)
-    mine = jnp.where(core == 0, first, second)
     depth, width = mine.shape
-    theirs = move_col(mine, lambda c: c ^ 1)
     slab = jnp.where(y_hi == 0, jnp.stack([mine, theirs]), jnp.stack([theirs, mine]))
     below = move_col(slab, along_z(1))
     above = move_col(slab, along_z(-1))
@@ -183,15 +186,16 @@
     )
 
 
-def one_head_kernel(query_ref, mine_ref, theirs_ref, out_ref, *scratch):
+def attend_kernel(query_ref, mine_ref, theirs_ref, out_ref, *scratch):
     query, keys, vals, total, accum = scratch
     sources, unused, pixels = mine_ref.shape
     per_step = query_ref.shape[0]
+    first = mine_ref.shape[1] - 2 * HEAD
 
     @pl.when(pl.program_id(0) == 0)
     def _():
         for s in range(sources):
-            put_keys(keys, vals, s * pixels, mine_ref[s, HEAD : 2 * HEAD], mine_ref[s, 2 * HEAD :])
+            put_keys(keys, vals, s * pixels, mine_ref[s, first : first + HEAD], mine_ref[s, first + HEAD :])
             put_keys(keys, vals, (sources + s) * pixels, theirs_ref[s, :HEAD], theirs_ref[s, HEAD:])
 
     query_t = jnp.concatenate([query_ref[s] for s in range(per_step)], axis=1)
@@ -200,52 +204,25 @@
         out_ref[s] = attended[:, s * pixels : (s + 1) * pixels]
 
 
-def one_head(mine, theirs):
+def attend(query, mine, theirs):
     sources, unused, pixels = mine.shape
+    blocks = query.shape[0]
     per_step = 2
     count = 2 * sources * pixels
     return pl.pallas_call(
-        one_head_kernel,
-        grid=(sources // per_step,),
+        attend_kernel,
+        grid=(blocks // per_step,),
         in_specs=[
             pl.BlockSpec((per_step, HEAD, pixels), lambda i: (i, 0, 0)),
             pl.BlockSpec(mine.shape, lambda i: (0, 0, 0)),
             pl.BlockSpec(theirs.shape, lambda i: (0, 0, 0)),
         ],
         out_specs=pl.BlockSpec((per_step, HEAD, pixels), lambda i: (i, 0, 0)),
-        out_shape=jax.ShapeDtypeStruct((sources, HEAD, pixels), BF16),
+        out_shape=jax.ShapeDtypeStruct((blocks, HEAD, pixels), BF16),
         scratch_shapes=attention_scratch(count, per_step * pixels),
         compiler_params=pltpu.CompilerParams(vmem_limit_bytes=56 * 2**20),
-        cost_estimate=cost(sources * pixels, count),
-    )(mine, mine, theirs)
-
-
-def own_rows_kernel(query_ref, key_ref, value_ref, out_ref, *scratch):
-    query, keys, vals, total, accum = scratch
-    sources, unused, pixels = key_ref.shape
-    for s in range(sources):
-        put_keys(keys, vals, s * pixels, key_ref[s], value_ref[s])
-    out_ref[...] = attend_rows(query, keys, vals, total, accum, query_ref[...], 2048)
-
-
-def own_rows(query_t, pairs):
-    heads = query_t.shape[0] // HEAD
-    sources, unused, pixels = pairs.shape
-    count = sources * pixels
-    return pl.pallas_call(
-        own_rows_kernel,
-        grid=(heads,),
-        in_specs=[
-            pl.BlockSpec((HEAD, pixels), lambda h: (h, 0)),
-            pl.BlockSpec((sources, HEAD, pixels), lambda h: (0, h, 0)),
-            pl.BlockSpec((sources, HEAD, pixels), lambda h: (0, heads + h, 0)),
-        ],
-        out_specs=pl.BlockSpec((HEAD, pixels), lambda h: (h, 0)),
-        out_shape=jax.ShapeDtypeStruct(query_t.shape, BF16),
-        scratch_shapes=attention_scratch(count, pixels),
-        compiler_params=pltpu.CompilerParams(vmem_limit_bytes=56 * 2**20),
-        cost_estimate=cost(heads * pixels, count),
-    )(query_t, pairs, pairs)
+        cost_estimate=cost(blocks * pixels, count),
+    )(query, mine, theirs)
 
 
 def local(
@@ -255,10 +232,12 @@
     pixels = rows_here * cols_here
     per_group = channels // GROUPS
     inner = HEADS * HEAD
-    weights = gathered_weights(w_query, w_key, w_value)
-    full_out = lax.all_gather(w_out, "col", axis=1, tiled=True)
+    half = half_weights(w_query, w_key, w_value)
+    half_theirs = move_col(half, lambda c: c ^ 1)
+    weights = gathered_weights(half, half_theirs)
 
     shift = time_shift(timestep[0], w_time, w_emb, b_emb)
+    features, unused = lax.optimization_barrier((features, half_theirs))
     lifted = features.reshape(pixels, channels) + shift
     count = float(pixels * per_group)
 
@@ -281,11 +260,32 @@
     by_head = rows[:, :first].reshape(3, CHIPS, HEAD, pixels).transpose(1, 0, 2, 3)
     mine = across_chips(by_head.reshape(CHIPS, 3 * HEAD, pixels))
     theirs = other_core(mine[:, HEAD:])
-    pairs, mine = lax.optimization_barrier((rows[1:, first:], mine))
-    pairs = lax.all_gather(pairs.reshape(2 * (inner - first), pixels), "row", axis=0, tiled=False)
-    attended = across_chips(one_head(mine, theirs)).reshape(first, pixels)
-    others = own_rows(rows[0, first:], pairs)
-    attended = jnp.concatenate([attended, others], axis=0)
+    upper = lax.axis_index("row") // CHIPS
+    rest = rows[:, first:].reshape(3, 2, HEAD, pixels)
+    by_head, unused = lax.optimization_barrier((rest[1:].transpose(1, 0, 2, 3), mine))
+    by_head = jnp.repeat(by_head.reshape(2, 2 * HEAD, pixels), CHIPS // 2, axis=0)
+    pairs = across_chips(by_head)
+    pairs_theirs = other_core(pairs)
+    opposite = lambda r: (r + 8) % 16
+    query = lax.dynamic_index_in_dim(rest[0], upper, 0, keepdims=False)
+    query_far = move_row(lax.dynamic_index_in_dim(rest[0], 1 - upper, 0, keepdims=False), opposite)
+    core = lax.axis_index("row") % 2
+    out_half = lax.dynamic_slice_in_dim(w_out, core * (inner // 2), inner // 2, 0)
+    out_half, unused = lax.optimization_barrier((out_half, mine))
+    out_half = lax.all_to_all(jnp.broadcast_to(out_half[None], (8,) + out_half.shape), "col", 0, 0, tiled=True)
+    out_half = out_half.transpose(1, 0, 2).reshape(inner // 2, channels)
+    out_theirs = other_core(out_half)
+    out_low = jnp.where(core == 0, out_half, out_theirs)
+    out_high = jnp.where(core == 0, out_theirs, out_half)
+    full_out = jnp.concatenate([out_low, out_high], axis=0)
+
+    attended = attend(mine, mine, theirs)
+    query, attended = lax.optimization_barrier((jnp.stack([query, query_far]), attended))
+    attended = across_chips(attended).reshape(first, pixels)
+    both = attend(query, pairs, pairs_theirs)
+    returned = move_row(both[1], opposite)
+    others = jnp.where(upper == 0, jnp.stack([both[0], returned]), jnp.stack([returned, both[0]]))
+    attended = jnp.concatenate([attended, others.reshape(inner - first, pixels)], axis=0)
     added = lax.dot_general(attended, full_out, (((0,), (0,)), ((), ())), preferred_element_type=F32)
     return (lifted + added).reshape(1, rows_here, cols_here, channels)
 

time: 261 us -> 299 us (1.15)
  the two profiles are of different devices: /device:TPU:2 before, /device:TPU:34 now
where the time goes in v2:
time: 299 us; the launch traced here: 297 us
  Pallas kernels  131 us (44%)
  waiting for transfers between devices  65.5 us (22%)
  starting transfers between devices  45 us (15%)
  local copies, waits for them, and re-layouts  24.6 us (8%)
  matrix products  18 us (6%)
  other arithmetic  11.5 us (4%)
    pallas_call x2, Pallas kernels, attend(): pl.pallas_call(attend_kernel, grid=(blocks // per_step,), in_specs=[pl.Bl...  131 us
    all_to_all x3, waiting for transfers between devices, across_chips(): lax.all_to_all(value, 'row', 0, 0, tiled=True, axis_index_groups=groups)  34.5 us
    ppermute x5, waiting for transfers between devices, move_col(): return lax.ppermute(value, 'col', [(c, target(c)) for c in range(8)])  18.2 us
    all_to_all x3, starting transfers between devices, across_chips(): lax.all_to_all(value, 'row', 0, 0, tiled=True, axis_index_groups=groups)  16.8 us
    all_to_all x1, waiting for transfers between devices, local(): lax.all_to_all(jnp.broadcast_to(out_half[None], (8,) + out_half.shape), '...  10.7 us
    all_to_all x1, starting transfers between devices, local(): lax.all_to_all(jnp.broadcast_to(out_half[None], (8,) + out_half.shape), '...  10.4 us
    ppermute x16, starting transfers between devices, move_row(): return lax.ppermute(value, 'row', [(r, target(r)) for r in range(16)])  10.3 us
    ppermute x5, starting transfers between devices, move_col(): return lax.ppermute(value, 'col', [(c, target(c)) for c in range(8)])  7.59 us
  transfers between devices with their start and end apart: 25, of which 7 were waited for; matrix products, arithmetic and copies ran while one was open for 11% of the time, Pallas kernels for 44%

profile of v2, /device:TPU:34, one launch (start us, length us, event | category | flops | bytes accessed | tf_op | source)
XLA Modules:
  0.0 296.6 jit_solution(930245145517721315)
XLA Ops:
  0.0 1.2 slice_bitcast_fusion.3
  1.2 1.2 maximum_select_fusion.2
  2.4 3.3 %collective-permute-start = (bf16[160,960]{1,0:T(8,128)(2,1)S(1)}, bf16[160,960]{1,0:T(8,128)(2,1)S(1)}, u32[]{:S(2)}, u32[]{:S(2)}) collective-permute-start(bf16[160,960]{1,0:T(8,128)(2,1)S(1)} %maximum_select_fusion.2), channel_id=1, source_target_pairs={{0,1},{1,0},{2,3},{3,2},{4,5},{5,4},{6,7},{7,6},{8,9},{9,8},{10,11... | collective-permute-start | bytes 921608 | tf_op jit(solution)/shard_map/ppermute | solution.py:34
  6.5 0.9 convolution_reduce_fusion.1
  7.4 6.1 %convolution_reduce_fusion = f32[1280]{0:T(1024)S(1)} fusion(f32[1280,1]{0,1:T(1,128)S(1)} %reshape.301, f32[1280,1280]{1,0:T(8,128)} %param.14), kind=kOutput, calls=%fused_computation.10 | convolution fusion | flops 19660800 | bytes 6563840 | tf_op jit(solution)/shard_map/dot_general | solution.py:26
  13.6 0.1 maximum_select_fusion.3
  13.7 0.3 add_reduce_fusion
  14.1 0.1 reduce_sum.37
  14.4 2.1 multiply_reduce_fusion
  16.6 0.1 reduce_sum.39
  16.7 0.6 collective-permute-start.12
  17.3 2.4 collective-permute-start.11
  19.7 1.8 collective-permute-start.10
  21.5 0.9 maximum_select_fusion.1
  22.5 1.9 collective-permute-start.2
  24.5 1.2 collective-permute-start.15
  25.7 0.7 collective-permute-start.14
  26.4 3.0 %broadcast_in_dim.53 = bf16[2,4,2,160,960]{4,3,2,1,0:T(8,128)(2,1)} broadcast(bf16[]{:T(256)} %constant.112.clone.1), dimensions={} | broadcast | bytes 4915202 | tf_op jit(solution)/shard_map/broadcast_in_dim | solution.py:85
  29.4 1.1 fusion.7
  30.9 2.2 add_convert_fusion
  33.2 6.7 %collective-permute-done.2 = bf16[2,160,960]{2,1,0:T(8,128)(2,1)S(1)} collective-permute-done((bf16[2,160,960]{2,1,0:T(8,128)(2,1)}, bf16[2,160,960]{2,1,0:T(8,128)(2,1)S(1)}, u32[]{:S(2)}, u32[]{:S(2)}) %collective-permute-start.2) | collective-permute-done | bytes 614432 | tf_op jit(solution)/shard_map/ppermute | solution.py:34
  39.9 2.0 collective-permute-start.6
  41.9 5.9 %collective-permute-done.4 = bf16[2,160,960]{2,1,0:T(8,128)(2,1)S(1)} collective-permute-done((bf16[2,160,960]{2,1,0:T(8,128)(2,1)}, bf16[2,160,960]{2,1,0:T(8,128)(2,1)S(1)}, u32[]{:S(2)}, u32[]{:S(2)}) %collective-permute-start.4) | collective-permute-done | bytes 614432 | tf_op jit(solution)/shard_map/ppermute | solution.py:34
  47.8 0.4 collective-permute-start.8
  48.2 2.0 bitcast_dynamic-update-slice_fusion.4
  50.1 0.9 bitcast_dynamic-update-slice_fusion.3
  51.0 0.6 collective-permute-start.7
  51.6 5.6 %collective-permute-done.8 = bf16[160,960]{1,0:T(8,128)(2,1)S(1)} collective-permute-done((bf16[160,960]{1,0:T(8,128)(2,1)S(1)}, bf16[160,960]{1,0:T(8,128)(2,1)S(1)}, u32[]{:S(2)}, u32[]{:S(2)}) %collective-permute-start.8) | collective-permute-done | bytes 307232 | tf_op jit(solution)/shard_map/ppermute | solution.py:34
  57.1 0.9 bitcast_dynamic-update-slice_fusion.2
  58.0 0.9 bitcast_dynamic-update-slice_fusion.1
  58.9 0.9 bitcast_dynamic-update-slice_fusion
  59.8 0.7 bitcast_dynamic-update-slice_fusion.8
  60.6 0.8 bitcast_dynamic-update-slice_fusion.7
  61.3 0.8 bitcast_dynamic-update-slice_fusion.6
  62.1 0.8 bitcast_dynamic-update-slice_fusion.5
  62.9 5.5 %convolution_convert_fusion = bf16[2,960,512]{2,1,0:T(8,128)(2,1)S(1)} fusion(bf16[2,1280,960]{2,1,0:T(8,128)(2,1)} %bitcast.22, bf16[512,1280,1]{1,0,2:T(8,128)(2,1)S(1)} %bitcast.231), kind=kOutput, calls=%fused_computation.5 | convolution fusion | flops 2517565440 | bytes 8192000 | tf_op jit(solution)/shard_map/dot_general | solution.py:257
  68.4 0.1 slice.107
  68.5 1.4 copy.27
  70.0 0.2 copy-done.4
  70.2 4.6 %all-to-all-start = ((bf16[8,192,512]{2,1,0:T(8,128)(2,1)}), bf16[8,192,512]{2,1,0:T(8,128)(2,1)S(1)}, u32[]{:S(2)}, u32[]{:S(2)}) async-start(bf16[8,192,512]{2,1,0:T(8,128)(2,1)} %bitcast.45), calls=%async_computation | async-start | bytes 3145728 | tf_op jit(solution)/shard_map/all_to_all | solution.py:51
  74.8 1.0 slice.109
  75.7 21.5 %all-to-all-done.query_ref.mine_ref = bf16[8,192,512]{2,1,0:T(8,128)(2,1)S(1)} async-done(((bf16[8,192,512]{2,1,0:T(8,128)(2,1)}), bf16[8,192,512]{2,1,0:T(8,128)(2,1)S(1)}, u32[]{:S(2)}, u32[]{:S(2)}) %all-to-all-start) | async-done | bytes 1572896 | tf_op jit(solution)/shard_map/all_to_all | solution.py:51
  97.3 1.1 broadcast_in_dim.66
  98.4 6.6 %all-to-all-start.2 = ((bf16[8,128,512]{2,1,0:T(8,128)(2,1)}), bf16[8,128,512]{2,1,0:T(8,128)(2,1)}, u32[]{:S(2)}, u32[]{:S(2)}) async-start(bf16[8,128,512]{2,1,0:T(8,128)(2,1)} %bitcast.226), calls=%async_computation.2 | async-start | bytes 2097152 | tf_op jit(solution)/shard_map/all_to_all | solution.py:51
  104.9 1.1 slice.108
  106.1 0.1 constant_dynamic-slice_fusion
  106.2 13.0 %all-to-all-done.2.mine_ref = bf16[8,128,512]{2,1,0:T(8,128)(2,1)} async-done(((bf16[8,128,512]{2,1,0:T(8,128)(2,1)}), bf16[8,128,512]{2,1,0:T(8,128)(2,1)}, u32[]{:S(2)}, u32[]{:S(2)}) %all-to-all-start.2) | async-done | bytes 1048608 | tf_op jit(solution)/shard_map/all_to_all | solution.py:51
  119.1 1.1 broadcast_in_dim.67
  120.2 10.4 %all-to-all-start.3 = ((bf16[8,320,160]{1,2,0:T(8,128)(2,1)}), bf16[8,320,160]{1,2,0:T(8,128)(2,1)S(1)}, u32[]{:S(2)}, u32[]{:S(2)}) async-start(bf16[8,320,160]{1,2,0:T(8,128)(2,1)} %broadcast_in_dim.67), calls=%async_computation.3 | async-start | bytes 1966080 | tf_op jit(solution)/shard_map/all_to_all | solution.py:275
  130.6 0.9 slice.106
  131.6 0.6 constant_dynamic-slice_fusion.1
  132.2 0.7 collective-permute-start.16
  132.9 10.7 %all-to-all-done.3 = bf16[8,320,160]{1,2,0:T(8,128)(2,1)S(1)} async-done(((bf16[8,320,160]{1,2,0:T(8,128)(2,1)}), bf16[8,320,160]{1,2,0:T(8,128)(2,1)S(1)}, u32[]{:S(2)}, u32[]{:S(2)}) %all-to-all-start.3) | async-done | bytes 819232 | tf_op jit(solution)/shard_map/all_to_all | solution.py:275
  143.6 1.3 copy.29
  144.8 1.5 pad_maximum_fusion.query_ref
  146.3 102.8 %shard_map.109 = bf16[8,64,512]{2,1,0:T(8,128)(2,1)} custom-call(bf16[8,192,512]{2,1,0:T(8,128)(2,1)} %copy-done.2, bf16[8,192,512]{2,1,0:T(8,128)(2,1)} %copy-done.2, bf16[8,128,512]{2,1,0:T(8,128)(2,1)} %collective-permute-done.17.theirs_ref), custom_call_target="tpu_custom_call" | custom-call | flops 8589934592 | bytes 8388608 | tf_op jit(solution)/shard_map/pallas_call | solution.py:212
  249.1 5.7 %all-to-all-start.1 = ((bf16[8,64,512]{2,1,0:T(8,128)(2,1)}), bf16[8,64,512]{2,1,0:T(8,128)(2,1)}, u32[]{:S(2)}, u32[]{:S(2)}) async-start(bf16[8,64,512]{2,1,0:T(8,128)(2,1)} %shard_map.109), calls=%async_computation.1 | async-start | bytes 1048576 | tf_op jit(solution)/shard_map/all_to_all | solution.py:51
  254.8 1.3 copy.30
  256.1 28.2 %shard_map.110 = bf16[2,64,512]{2,1,0:T(8,128)(2,1)} custom-call(bf16[2,64,512]{2,1,0:T(8,128)(2,1)} %pad_maximum_fusion.query_ref, bf16[8,128,512]{2,1,0:T(8,128)(2,1)} %all-to-all-done.2.mine_ref, bf16[8,128,512]{2,1,0:T(8,128)(2,1)} %collective-permute-done.18.theirs_ref), custom_call_target="tpu_custom_call" | custom-call | flops 2147483648 | bytes 8388608 | tf_op jit(solution)/shard_map/pallas_call | solution.py:212
  284.3 0.9 fusion.33
  285.2 2.2 collective-permute-start.19
  287.4 1.6 broadcast_select_fusion.1
  288.9 2.1 collective-permute-done.19
  291.1 5.5 %fusion = f32[512,1280]{1,0:T(8,128)} fusion(f32[1,4,128,1280]{3,2,1,0:T(8,128)} %param.11, bf16[320,1280]{0,1:T(8,128)(2,1)} %get-tuple-element.20, bf16[320,1280]{0,1:T(8,128)(2,1)} %get-tuple-element.19, f32[1280]{0:T(1024)S(1)} %add.220, bf16[128,512]{1,0:T(8,128)(2,1)S(1)} %bitcast.241, bf16[512,512]{1,0:T(8,128)(2,1)} %bitcast.46), kind=kOutput, calls=%fused_computation.1 | convolution fusion | flops 844759040 | bytes 7541760 | tf_op jit(solution)/shard_map/dot_general | solution.py:289
  (71 shorter events, 1.2 us)
Async XLA Ops:
  0.0 6.5 %copy-start = (f32[320,1280]{1,0:T(8,128)S(1)}, f32[320,1280]{1,0:T(8,128)}, u32[]{:S(2)}) copy-start(f32[320,1280]{1,0:T(8,128)} %param.13) | copy-start | bytes 4915204
  2.4 11.3 %collective-permute-start = (bf16[160,960]{1,0:T(8,128)(2,1)S(1)}, bf16[160,960]{1,0:T(8,128)(2,1)S(1)}, u32[]{:S(2)}, u32[]{:S(2)}) collective-permute-start(bf16[160,960]{1,0:T(8,128)(2,1)S(1)} %maximum_select_fusion.2), channel_id=1, source_target_pairs={{0,1},{1,0},{2,3},{3,2},{4,5},{5,4},{6,7},{7,6},{8,9},{9,8},{10,11... | collective-permute-start | bytes 921608 | tf_op jit(solution)/shard_map/ppermute | solution.py:34
  7.4 6.1 %copy-start.10 = (f32[1280]{0:T(1024)S(1)}, f32[1280]{0:T(1024)}, u32[]{:S(2)}) copy-start(f32[1280]{0:T(1024)} %param.15) | copy-start | bytes 15364
  7.4 6.1 %copy-start.5 = (bf16[160,640]{1,0:T(8,128)(2,1)S(1)}, bf16[160,640]{1,0:T(8,128)(2,1)}, u32[]{:S(2)}) copy-start(bf16[160,640]{1,0:T(8,128)(2,1)} %param.18) | copy-start | bytes 614404
  7.4 6.1 %copy-start.6 = (bf16[160,640]{1,0:T(8,128)(2,1)S(1)}, bf16[160,640]{1,0:T(8,128)(2,1)}, u32[]{:S(2)}) copy-start(bf16[160,640]{1,0:T(8,128)(2,1)} %param.20) | copy-start | bytes 614404
  7.4 6.3 %copy-start.1 = (f32[1,4,128,1280]{3,2,1,0:T(8,128)S(1)}, f32[1,4,128,1280]{3,2,1,0:T(8,128)}, u32[]{:S(2)}) copy-start(f32[1,4,128,1280]{3,2,1,0:T(8,128)} %param.11) | copy-start | bytes 7864324
  16.7 7.7 %collective-permute-start.12 = (f32[2,32]{1,0:T(2,128)S(1)}, f32[2,32]{1,0:T(2,128)S(1)}, u32[]{:S(2)}, u32[]{:S(2)}) collective-permute-start(f32[2,32]{1,0:T(2,128)S(1)} %pad_maximum_fusion.2), channel_id=1, source_target_pairs={{0,96},{8,104},{16,112},{24,120},{32,0},{40,8},{48,16},{56,24},{64... | collective-permute-start | bytes 776 | tf_op jit(solution)/shard_map/ppermute | solution.py:30
  17.3 7.1 %collective-permute-start.11 = (f32[2,32]{1,0:T(2,128)S(1)}, f32[2,32]{1,0:T(2,128)S(1)}, u32[]{:S(2)}, u32[]{:S(2)}) collective-permute-start(f32[2,32]{1,0:T(2,128)S(1)} %pad_maximum_fusion.2), channel_id=1, source_target_pairs={{0,64},{8,72},{16,80},{24,88},{32,96},{40,104},{48,112},{56,120},{... | collective-permute-start | bytes 776 | tf_op jit(solution)/shard_map/ppermute | solution.py:30
  19.7 4.7 %collective-permute-start.10 = (f32[2,32]{1,0:T(2,128)S(1)}, f32[2,32]{1,0:T(2,128)S(1)}, u32[]{:S(2)}, u32[]{:S(2)}) collective-permute-start(f32[2,32]{1,0:T(2,128)S(1)} %pad_maximum_fusion.2), channel_id=1, source_target_pairs={{0,32},{8,40},{16,48},{24,56},{32,64},{40,72},{48,80},{56,88},{64,... | collective-permute-start | bytes 776 | tf_op jit(solution)/shard_map/ppermute | solution.py:30
  22.5 25.7 %collective-permute-start.1 = (bf16[2,160,960]{2,1,0:T(8,128)(2,1)}, bf16[2,160,960]{2,1,0:T(8,128)(2,1)}, u32[]{:S(2)}, u32[]{:S(2)}) collective-permute-start(bf16[2,160,960]{2,1,0:T(8,128)(2,1)} %maximum_select_fusion.1), channel_id=1, source_target_pairs={{0,8},{8,0},{16,24},{24,16},{32,40},{40,32},{48,56},{56,48},{64,72... | collective-permute-start | bytes 1843208 | tf_op jit(solution)/shard_map/ppermute | solution.py:30
  22.5 17.4 %collective-permute-start.2 = (bf16[2,160,960]{2,1,0:T(8,128)(2,1)}, bf16[2,160,960]{2,1,0:T(8,128)(2,1)S(1)}, u32[]{:S(2)}, u32[]{:S(2)}) collective-permute-start(bf16[2,160,960]{2,1,0:T(8,128)(2,1)} %maximum_select_fusion.1), channel_id=1, source_target_pairs={{0,2},{1,3},{2,4},{3,5},{4,6},{5,7},{6,0},{7,1},{8,10},{9,11},{10,... | collective-permute-start | bytes 1843208 | tf_op jit(solution)/shard_map/ppermute | solution.py:34
  24.5 6.0 %collective-permute-start.15 = (f32[2,32]{1,0:T(2,128)S(1)}, f32[2,32]{1,0:T(2,128)S(1)}, u32[]{:S(2)}, u32[]{:S(2)}) collective-permute-start(f32[2,32]{1,0:T(2,128)S(1)} %pad_maximum_fusion.3), channel_id=1, source_target_pairs={{0,24},{8,16},{16,8},{24,0},{32,56},{40,48},{48,40},{56,32},{64,88... | collective-permute-start | bytes 776 | tf_op jit(solution)/shard_map/ppermute | solution.py:30
  25.7 4.9 %collective-permute-start.14 = (f32[2,32]{1,0:T(2,128)S(1)}, f32[2,32]{1,0:T(2,128)S(1)}, u32[]{:S(2)}, u32[]{:S(2)}) collective-permute-start(f32[2,32]{1,0:T(2,128)S(1)} %pad_maximum_fusion.3), channel_id=1, source_target_pairs={{0,16},{8,24},{16,0},{24,8},{32,48},{40,56},{48,32},{56,40},{64,80... | collective-permute-start | bytes 776 | tf_op jit(solution)/shard_map/ppermute | solution.py:30
  26.4 4.1 %collective-permute-start.13 = (f32[2,32]{1,0:T(2,128)S(1)}, f32[2,32]{1,0:T(2,128)S(1)}, u32[]{:S(2)}, u32[]{:S(2)}) collective-permute-start(f32[2,32]{1,0:T(2,128)S(1)} %pad_maximum_fusion.3), channel_id=1, source_target_pairs={{0,8},{8,0},{16,24},{24,16},{32,40},{40,32},{48,56},{56,48},{64,72... | collective-permute-start | bytes 776 | tf_op jit(solution)/shard_map/ppermute | solution.py:30
  26.4 4.5 %copy-start.8 = (f32[1280]{0:T(1024)S(1)}, f32[1280]{0:T(1024)}, u32[]{:S(2)}) copy-start(f32[1280]{0:T(1024)} %param.17) | copy-start | bytes 15364
  26.4 4.5 %copy-start.9 = (f32[1280]{0:T(1024)S(1)}, f32[1280]{0:T(1024)}, u32[]{:S(2)}) copy-start(f32[1280]{0:T(1024)} %param.16) | copy-start | bytes 15364
  30.5 17.3 %collective-permute-start.4 = (bf16[2,160,960]{2,1,0:T(8,128)(2,1)}, bf16[2,160,960]{2,1,0:T(8,128)(2,1)S(1)}, u32[]{:S(2)}, u32[]{:S(2)}) collective-permute-start(bf16[2,160,960]{2,1,0:T(8,128)(2,1)} %maximum_select_fusion.1), channel_id=1, source_target_pairs={{0,6},{1,7},{2,0},{3,1},{4,2},{5,3},{6,4},{7,5},{8,14},{9,15},{10,... | collective-permute-start | bytes 1843208 | tf_op jit(solution)/shard_map/ppermute | solution.py:34
  39.9 11.1 %collective-permute-start.6 = (bf16[160,960]{1,0:T(8,128)(2,1)S(1)}, bf16[160,960]{1,0:T(8,128)(2,1)S(1)}, u32[]{:S(2)}, u32[]{:S(2)}) collective-permute-start(bf16[160,960]{1,0:T(8,128)(2,1)S(1)} %slice_bitcast_fusion.1), channel_id=1, source_target_pairs={{0,2},{1,3},{2,4},{3,5},{4,6},{5,7},{6,0},{7,1},{8,10},{9,11},{10,... | collective-permute-start | bytes 921608 | tf_op jit(solution)/shard_map/ppermute | solution.py:34
  41.9 15.3 %collective-permute-start.3 = (bf16[2,160,960]{2,1,0:T(8,128)(2,1)S(1)}, bf16[2,160,960]{2,1,0:T(8,128)(2,1)S(1)}, u32[]{:S(2)}, u32[]{:S(2)}) collective-permute-start(bf16[2,160,960]{2,1,0:T(8,128)(2,1)S(1)} %collective-permute-done.2), channel_id=1, source_target_pairs={{0,8},{8,0},{16,24},{24,16},{32,40},{40,32},{48,56},{56,48},{64,72... | collective-permute-start | bytes 1843208 | tf_op jit(solution)/shard_map/ppermute | solution.py:30
  47.8 9.3 %collective-permute-start.8 = (bf16[160,960]{1,0:T(8,128)(2,1)S(1)}, bf16[160,960]{1,0:T(8,128)(2,1)S(1)}, u32[]{:S(2)}, u32[]{:S(2)}) collective-permute-start(bf16[160,960]{1,0:T(8,128)(2,1)S(1)} %slice_bitcast_fusion), channel_id=1, source_target_pairs={{0,6},{1,7},{2,0},{3,1},{4,2},{5,3},{6,4},{7,5},{8,14},{9,15},{10,... | collective-permute-start | bytes 921608 | tf_op jit(solution)/shard_map/ppermute | solution.py:34
  48.1 10.8 %collective-permute-start.5 = (bf16[2,160,960]{2,1,0:T(8,128)(2,1)S(1)}, bf16[2,160,960]{2,1,0:T(8,128)(2,1)S(1)}, u32[]{:S(2)}, u32[]{:S(2)}) collective-permute-start(bf16[2,160,960]{2,1,0:T(8,128)(2,1)S(1)} %collective-permute-done.4), channel_id=1, source_target_pairs={{0,8},{8,0},{16,24},{24,16},{32,40},{40,32},{48,56},{56,48},{64,72... | collective-permute-start | bytes 1843208 | tf_op jit(solution)/shard_map/ppermute | solution.py:30
  51.0 9.6 %collective-permute-start.7 = (bf16[1,160,960]{2,1,0:T(8,128)(2,1)S(1)}, bf16[1,160,960]{2,1,0:T(8,128)(2,1)S(1)}, u32[]{:S(2)}, u32[]{:S(2)}) collective-permute-start(bf16[1,160,960]{2,1,0:T(8,128)(2,1)S(1)} %bitcast.239), channel_id=1, source_target_pairs={{0,8},{8,0},{16,24},{24,16},{32,40},{40,32},{48,56},{56,48},{64,72... | collective-permute-start | bytes 921608 | tf_op jit(solution)/shard_map/ppermute | solution.py:30
  57.1 5.0 %collective-permute-start.9 = (bf16[1,160,960]{2,1,0:T(8,128)(2,1)S(1)}, bf16[1,160,960]{2,1,0:T(8,128)(2,1)S(1)}, u32[]{:S(2)}, u32[]{:S(2)}) collective-permute-start(bf16[1,160,960]{2,1,0:T(8,128)(2,1)S(1)} %bitcast.240), channel_id=1, source_target_pairs={{0,8},{8,0},{16,24},{24,16},{32,40},{40,32},{48,56},{56,48},{64,72... | collective-permute-start | bytes 921608 | tf_op jit(solution)/shard_map/ppermute | solution.py:30
  68.4 1.8 copy-start.4
  70.2 27.1 %all-to-all-start = ((bf16[8,192,512]{2,1,0:T(8,128)(2,1)}), bf16[8,192,512]{2,1,0:T(8,128)(2,1)S(1)}, u32[]{:S(2)}, u32[]{:S(2)}) async-start(bf16[8,192,512]{2,1,0:T(8,128)(2,1)} %bitcast.45), calls=%async_computation | async-start | bytes 3145728 | tf_op jit(solution)/shard_map/all_to_all | solution.py:51
  97.3 8.8 %copy-start.2 = (bf16[8,192,512]{2,1,0:T(8,128)(2,1)}, bf16[8,192,512]{2,1,0:T(8,128)(2,1)S(1)}, u32[]{:S(2)}) copy-start(bf16[8,192,512]{2,1,0:T(8,128)(2,1)S(1)} %all-to-all-done.query_ref.mine_ref) | copy-start | bytes 4718596
  97.3 8.8 %copy-start.7 = (bf16[640,160]{0,1:T(8,128)(2,1)S(1)}, bf16[640,160]{0,1:T(8,128)(2,1)}, u32[]{:S(2)}) copy-start(bf16[640,160]{0,1:T(8,128)(2,1)} %param.21) | copy-start | bytes 614404
  98.4 20.8 %all-to-all-start.2 = ((bf16[8,128,512]{2,1,0:T(8,128)(2,1)}), bf16[8,128,512]{2,1,0:T(8,128)(2,1)}, u32[]{:S(2)}, u32[]{:S(2)}) async-start(bf16[8,128,512]{2,1,0:T(8,128)(2,1)} %bitcast.226), calls=%async_computation.2 | async-start | bytes 2097152 | tf_op jit(solution)/shard_map/all_to_all | solution.py:51
  106.0 40.3 %collective-permute-start.17 = (bf16[8,128,512]{2,1,0:T(8,128)(2,1)}, bf16[8,128,512]{2,1,0:T(8,128)(2,1)}, u32[]{:S(2)}, u32[]{:S(2)}) collective-permute-start(bf16[8,128,512]{2,1,0:T(8,128)(2,1)} %slice.108), channel_id=1, source_target_pairs={{0,8},{8,0},{16,24},{24,16},{32,40},{40,32},{48,56},{56,48},{64,72... | collective-permute-start | bytes 3145736 | tf_op jit(solution)/shard_map/ppermute | solution.py:30
  120.2 23.4 %all-to-all-start.3 = ((bf16[8,320,160]{1,2,0:T(8,128)(2,1)}), bf16[8,320,160]{1,2,0:T(8,128)(2,1)S(1)}, u32[]{:S(2)}, u32[]{:S(2)}) async-start(bf16[8,320,160]{1,2,0:T(8,128)(2,1)} %broadcast_in_dim.67), calls=%async_computation.3 | async-start | bytes 1966080 | tf_op jit(solution)/shard_map/all_to_all | solution.py:275
  131.5 124.6 %collective-permute-start.18 = (bf16[8,128,512]{2,1,0:T(8,128)(2,1)}, bf16[8,128,512]{2,1,0:T(8,128)(2,1)}, u32[]{:S(2)}, u32[]{:S(2)}) collective-permute-start(bf16[8,128,512]{2,1,0:T(8,128)(2,1)} %all-to-all-done.2.mine_ref), channel_id=1, source_target_pairs={{0,8},{8,0},{16,24},{24,16},{32,40},{40,32},{48,56},{56,48},{64,72... | collective-permute-start | bytes 3145736 | tf_op jit(solution)/shard_map/ppermute | solution.py:30
  132.2 12.6 %collective-permute-start.16 = (bf16[64,512]{1,0:T(8,128)(2,1)}, bf16[64,512]{1,0:T(8,128)(2,1)}, u32[]{:S(2)}, u32[]{:S(2)}) collective-permute-start(bf16[64,512]{1,0:T(8,128)(2,1)} %get-tuple-element.28), channel_id=1, source_target_pairs={{0,64},{8,72},{16,80},{24,88},{32,96},{40,104},{48,112},{56,120},{... | collective-permute-start | bytes 196616 | tf_op jit(solution)/shard_map/ppermute | solution.py:30
  144.8 110.0 %collective-permute-start.20 = (bf16[320,1280]{1,0:T(8,128)(2,1)}, bf16[320,1280]{1,0:T(8,128)(2,1)S(1)}, u32[]{:S(2)}, u32[]{:S(2)}) collective-permute-start(bf16[320,1280]{1,0:T(8,128)(2,1)} %copy.29), channel_id=1, source_target_pairs={{0,8},{8,0},{16,24},{24,16},{32,40},{40,32},{48,56},{56,48},{64,72... | collective-permute-start | bytes 2457608 | tf_op jit(solution)/shard_map/ppermute | solution.py:30
  249.1 41.9 %all-to-all-start.1 = ((bf16[8,64,512]{2,1,0:T(8,128)(2,1)}), bf16[8,64,512]{2,1,0:T(8,128)(2,1)}, u32[]{:S(2)}, u32[]{:S(2)}) async-start(bf16[8,64,512]{2,1,0:T(8,128)(2,1)} %shard_map.109), calls=%async_computation.1 | async-start | bytes 1048576 | tf_op jit(solution)/shard_map/all_to_all | solution.py:51
  256.1 31.3 %copy-start.3 = (bf16[320,1280]{0,1:T(8,128)(2,1)S(1)}, bf16[320,1280]{0,1:T(8,128)(2,1)}, u32[]{:S(2)}) copy-start(bf16[320,1280]{0,1:T(8,128)(2,1)} %copy.30) | copy-start | bytes 2457604
  285.2 5.8 %collective-permute-start.19 = (bf16[64,512]{1,0:T(8,128)(2,1)S(1)}, bf16[64,512]{1,0:T(8,128)(2,1)S(1)}, u32[]{:S(2)}, u32[]{:S(2)}) collective-permute-start(bf16[64,512]{1,0:T(8,128)(2,1)S(1)} %get-tuple-element.26), channel_id=1, source_target_pairs={{0,64},{8,72},{16,80},{24,88},{32,96},{40,104},{48,112},{56,120},{... | collective-permute-start | bytes 196616 | tf_op jit(solution)/shard_map/ppermute | solution.py:30

commit v3 on v2

v3 whole, which is shorter than its diff:
```python
import functools
import math

import jax
import jax.numpy as jnp
from jax import lax
from jax.experimental import pallas as pl
from jax.experimental.pallas import tpu as pltpu
from jax.sharding import PartitionSpec as P

GROUPS = 32
HEADS = 10
HEAD = 64
CHIPS = 8
F32 = jnp.float32
BF16 = jnp.bfloat16
SCALE = math.log2(math.e) / math.sqrt(HEAD)


def time_shift(step_value, w_time, w_emb, b_emb):
    half = w_time.shape[0] // 2
    freqs = jnp.exp(-math.log(10000.0) * jnp.arange(half, dtype=F32) / half)
    angles = step_value.astype(F32) * freqs
    table = jnp.concatenate([jnp.cos(angles), jnp.sin(angles)])[None, :]
    hidden = jax.nn.silu(jnp.dot(table, w_time, precision=lax.Precision.HIGHEST))
    return jnp.dot(hidden, w_emb, precision=lax.Precision.HIGHEST) + b_emb[None, :]


def move_row(value, target):
    return lax.ppermute(value, "row", [(r, target(r)) for r in range(16)])


def move_col(value, target):
    return lax.ppermute(value, "col", [(c, target(c)) for c in range(8)])


def along_x(step):
    return lambda r: ((r // 4 + step) % 4) * 4 + r % 4


def along_z(step):
    return lambda c: ((c // 2 + step) % 4) * 2 + c % 2


def after(value, *others):
    anywhere = pl.BlockSpec(memory_space=pl.ANY)
    return pl.pallas_call(
        lambda *refs: None,
        in_specs=[anywhere] * (1 + len(others)),
        out_specs=anywhere,
        out_shape=jax.ShapeDtypeStruct(value.shape, value.dtype),
        input_output_aliases={0: 0},
        cost_estimate=pl.CostEstimate(flops=0, bytes_accessed=0, transcendentals=0),
    )(value, *others)


def other_core(value):
    return move_row(value, lambda r: r ^ 1)


def across_chips(value):
    groups = [list(range(0, 16, 2)), list(range(1, 16, 2))]
    return lax.all_to_all(value, "row", 0, 0, tiled=True, axis_index_groups=groups)


def pooled(parts, count):
    mean = sum(p[0] for p in parts) / len(parts)
    spread = sum(p[1] for p in parts) + count * sum((p[0] - mean) ** 2 for p in parts)
    return jnp.stack([mean, spread])


def pooled_over_row(stat, count):
    parts = [stat] + [move_row(stat, along_x(d)) for d in (1, 2, 3)]
    stat = pooled(parts, count)
    parts = [stat] + [move_row(stat, lambda r, k=k: r ^ k) for k in (1, 2, 3)]
    return pooled(parts, 4 * count)


def half_columns_kernel(core_ref, query_ref, key_ref, value_ref, out_w_ref, out_ref, packed):
    def put(low, last, start):
        parts = []
        for ref in (query_ref, key_ref, value_ref):
            parts += [ref[:, low * HEAD : (low + 4) * HEAD], ref[:, last * HEAD : (last + 1) * HEAD]]
        half = out_w_ref.shape[1] // 2
        parts.append(out_w_ref[:, start : start + half])
        packed[...] = jnp.concatenate(parts, axis=1)

    @pl.when(pl.program_id(0) == 0)
    def _():
        @pl.when(core_ref[0] == 0)
        def _():
            put(0, 8, 0)

        @pl.when(core_ref[0] == 1)
        def _():
            put(4, 9, out_w_ref.shape[1] // 2)

    out_ref[0] = packed[...]


def half_columns(w_query, w_key, w_value, w_out):
    core = (lax.axis_index("row") % 2).astype(jnp.int32).reshape(1)
    size = lax.axis_size("col")
    depth = w_query.shape[0]
    width = (3 * w_query.shape[1] + w_out.shape[0]) // 2
    whole = pl.BlockSpec((depth, w_query.shape[1]), lambda i: (0, 0))
    return pl.pallas_call(
        half_columns_kernel,
        grid=(size,),
        in_specs=[pl.BlockSpec(memory_space=pltpu.SMEM)] + [whole] * 4,
        out_specs=pl.BlockSpec((1, depth, width), lambda i: (i, 0, 0)),
        out_shape=jax.ShapeDtypeStruct((size, depth, width), BF16),
        scratch_shapes=[pltpu.VMEM((depth, width), BF16)],
    )(core, w_query, w_key, w_value, w_out.T)


def by_core(mine, theirs):
    core = lax.axis_index("row") % 2
    return jnp.where(core == 0, jnp.stack([mine, theirs]), jnp.stack([theirs, mine]))


def project_kernel(normed_ref, weight_ref, first_ref, last_ref):
    heads = first_ref.shape[0] + 1
    for part in range(3):
        columns = weight_ref[:, :, part * heads * HEAD : (part + 1) * heads * HEAD]
        columns = columns.reshape(normed_ref.shape[1], heads * HEAD)
        out = lax.dot_general(
            normed_ref[...], columns, (((1,), (0,)), ((), ())), preferred_element_type=F32
        )
        out = out.T.astype(BF16)
        for head in range(heads):
            rows = out[head * HEAD : (head + 1) * HEAD]
            if head < heads - 1:
                first_ref[head, part * HEAD : (part + 1) * HEAD, :] = rows
            else:
                last_ref[part * HEAD : (part + 1) * HEAD, :] = rows


def project(normed, weight):
    heads = HEADS // 2
    pixels = normed.shape[0]
    width = -(-3 * heads * HEAD // 128) * 128
    return pl.pallas_call(
        project_kernel,
        grid=(1,),
        in_specs=[
            pl.BlockSpec(normed.shape, lambda i: (0, 0)),
            pl.BlockSpec(weight.shape[:2] + (width,), lambda i: (0, 0, 0)),
        ],
        out_specs=(
            pl.BlockSpec((heads - 1, 3 * HEAD, pixels), lambda i: (0, 0, 0)),
            pl.BlockSpec((3 * HEAD, pixels), lambda i: (0, 0)),
        ),
        out_shape=(
            jax.ShapeDtypeStruct((heads - 1, 3 * HEAD, pixels), BF16),
            jax.ShapeDtypeStruct((3 * HEAD, pixels), BF16),
        ),
        compiler_params=pltpu.CompilerParams(vmem_limit_bytes=48 * 2**20),
        cost_estimate=pl.CostEstimate(
            flops=6 * normed.size * heads * HEAD, bytes_accessed=2**22, transcendentals=0
        ),
    )(normed, weight)


def split3(value):
    high = value.astype(BF16)
    rest = value - high.astype(F32)
    middle = rest.astype(BF16)
    low = (rest - middle.astype(F32)).astype(BF16)
    return high, middle, low


def product(a, b):
    return lax.dot_general(a, b, (((1,), (0,)), ((), ())), preferred_element_type=F32)


def put_keys(keys, vals, place, key_t, value_t):
    count = key_t.shape[1]
    row = lax.broadcasted_iota(jnp.int32, (HEAD, count), 0)
    ones = jnp.where(row < 3, 1.0, 0.0).astype(BF16)
    wide = jnp.concatenate([key_t, key_t, key_t, ones], axis=0)
    keys[place : place + count, :] = wide.T
    vals[:, place : place + count] = value_t


def put_top(query, top):
    width = top.shape[1]
    row = lax.broadcasted_iota(jnp.int32, (HEAD, width), 0)
    high, middle, low = split3(-top)
    wide = [jnp.broadcast_to(part, (HEAD, width)).astype(F32) for part in (high, middle, low)]
    rows = jnp.where(row == 0, wide[0], jnp.where(row == 1, wide[1], jnp.where(row == 2, wide[2], 0.0)))
    query[3 * HEAD :, :] = rows.astype(BF16)


def attend_rows(query, keys, vals, total_ref, accum_ref, query_t, chunk):
    width = query_t.shape[1]
    count = keys.shape[0]
    for at, part in enumerate(split3(query_t.astype(F32) * SCALE)):
        query[at * HEAD : (at + 1) * HEAD, :] = part

    def scores(start, size):
        return product(keys[pl.ds(start, size), :], query[...])

    def run(top, chunk):
        put_top(query, top)

        def step(i, state):
            total, accum = state
            start = pl.multiple_of(i * chunk, chunk)
            weights = jnp.exp2(scores(start, chunk))
            total = total + jnp.sum(weights.reshape(chunk // 8, 8, width), axis=0)
            accum = accum + product(vals[:, pl.ds(start, chunk)], weights.astype(BF16))
            return total, accum

        state = (jnp.zeros((8, width), F32), jnp.zeros((HEAD, width), F32))
        total, accum = lax.fori_loop(0, count // chunk, step, state)
        total_ref[...] = jnp.sum(total, axis=0, keepdims=True)
        accum_ref[...] = accum

    query[3 * HEAD :, :] = jnp.zeros((HEAD, width), BF16)
    run(jnp.max(scores(0, 256), axis=0, keepdims=True), chunk)
    small = jnp.max(jnp.where(total_ref[...] < 1e30, 0.0, 1.0))

    @pl.when(small > 0.5)
    def _():
        query[3 * HEAD :, :] = jnp.zeros((HEAD, width), BF16)

        def step(i, top):
            start = pl.multiple_of(i * 512, 512)
            return jnp.maximum(top, jnp.max(scores(start, 512), axis=0, keepdims=True))

        run(lax.fori_loop(0, count // 512, step, jnp.full((1, width), -jnp.inf, F32)), 512)

    return (accum_ref[...] / total_ref[...]).astype(BF16)


def attention_scratch(count, width):
    return [
        pltpu.VMEM((4 * HEAD, width), BF16),
        pltpu.VMEM((count, 4 * HEAD), BF16),
        pltpu.VMEM((HEAD, count), BF16),
        pltpu.VMEM((1, width), F32),
        pltpu.VMEM((HEAD, width), F32),
    ]


def cost(queries, count):
    return pl.CostEstimate(
        flops=20 * queries * count * HEAD, bytes_accessed=8 * 1024 * 1024, transcendentals=queries * count
    )


def attend_kernel(places_ref, *refs):
    query_refs, (mine_ref, theirs_ref, out_ref), scratch = refs[:2], refs[2:5], refs[5:]
    query, keys, vals, total, accum = scratch
    sources, rows, pixels = mine_ref.shape
    first = rows - 2 * HEAD

    @pl.when(pl.program_id(0) == 0)
    def _():
        for s in range(sources):
            for at, ref in ((s, mine_ref), (sources + s, theirs_ref)):
                put_keys(keys, vals, at * pixels, ref[s, first : first + HEAD], ref[s, first + HEAD :])

    query_t = jnp.concatenate([ref[0] for ref in query_refs], axis=1)
    attended = attend_rows(query, keys, vals, total, accum, query_t, 4096)
    for at in range(2):
        out_ref[at] = attended[:, at * pixels : (at + 1) * pixels]


def attend(places, mine, theirs):
    sources, rows, pixels = mine.shape
    blocks = places.shape[0]
    count = 2 * sources * pixels
    return pl.pallas_call(
        attend_kernel,
        grid_spec=pltpu.PrefetchScalarGridSpec(
            num_scalar_prefetch=1,
            grid=(blocks // 2,),
            in_specs=[
                pl.BlockSpec((1, HEAD, pixels), lambda i, places: (places[2 * i], 0, 0)),
                pl.BlockSpec((1, HEAD, pixels), lambda i, places: (places[2 * i + 1], 0, 0)),
                pl.BlockSpec(mine.shape, lambda i, places: (0, 0, 0)),
                pl.BlockSpec(theirs.shape, lambda i, places: (0, 0, 0)),
            ],
            out_specs=pl.BlockSpec((2, HEAD, pixels), lambda i, places: (i, 0, 0)),
            scratch_shapes=attention_scratch(count, 2 * pixels),
        ),
        out_shape=jax.ShapeDtypeStruct((blocks, HEAD, pixels), BF16),
        compiler_params=pltpu.CompilerParams(vmem_limit_bytes=56 * 2**20),
        cost_estimate=cost(blocks * pixels, count),
    )(places, mine, mine, mine, theirs)


def add_attended_kernel(
    place_ref, features_ref, shift_ref, first_ref, near_ref, far_ref, mine_ref, theirs_ref,
    out_ref, rows, attended, weights,
):
    heads, size, pixels = first_ref.shape
    unused, channels, half = weights.shape
    here = features_ref.shape[2]

    @pl.when(pl.program_id(0) == 0)
    def _():
        upper, core = place_ref[0], place_ref[1]
        rows[: heads * size, :] = first_ref[...].reshape(heads * size, pixels)
        start = heads * size
        rows[pl.ds(pl.multiple_of(start + upper * size, size), size), :] = near_ref[...]
        rows[pl.ds(pl.multiple_of(start + (1 - upper) * size, size), size), :] = far_ref[...]
        for at in range(2):
            attended[at] = rows[at * half : (at + 1) * half, :].T
        weights[core] = mine_ref[:, :, -half:].reshape(channels, half)
        weights[1 - core] = theirs_ref[:, :, -half:].reshape(channels, half)

    here = pl.ds(pl.multiple_of(pl.program_id(0) * here, here), here)
    added = [
        lax.dot_general(
            attended[at, here, :], weights[at], (((1,), (1,)), ((), ())), preferred_element_type=F32
        )
        for at in range(2)
    ]
    out_ref[0, 0] = (features_ref[0, 0] + shift_ref[...]) + (added[0] + added[1])


def add_attended(place, features, shift, first, near, far, mine, theirs):
    unused_one, rows_here, cols_here, channels = features.shape
    pixels = rows_here * cols_here
    half = HEADS * HEAD // 2

    def whole(value):
        return pl.BlockSpec(value.shape, lambda i: (0,) * value.ndim)

    block = pl.BlockSpec((1, 1, cols_here, channels), lambda i: (0, i, 0, 0))
    last = pl.BlockSpec(mine.shape[:2] + (2 * half,), lambda i: (0, 0, mine.shape[2] // (2 * half) - 1))
    return pl.pallas_call(
        add_attended_kernel,
        grid=(rows_here,),
        in_specs=[pl.BlockSpec(memory_space=pltpu.SMEM), block]
        + [whole(value) for value in (shift, first, near, far)]
        + [last, last],
        out_specs=block,
        out_shape=jax.ShapeDtypeStruct(features.shape, F32),
        scratch_shapes=[
            pltpu.VMEM((2 * half, pixels), BF16),
            pltpu.VMEM((2, pixels, half), BF16),
            pltpu.VMEM((2, channels, half), BF16),
        ],
        compiler_params=pltpu.CompilerParams(vmem_limit_bytes=48 * 2**20),
        cost_estimate=pl.CostEstimate(
            flops=4 * features.size * half, bytes_accessed=8 * features.size, transcendentals=0
        ),
    )(place, features, shift, first, near, far, mine, theirs)


def local(
    features, timestep, w_time, w_emb, b_emb, gn_gain, gn_bias, w_query, w_key, w_value, w_out
):
    unused_one, rows_here, cols_here, channels = features.shape
    pixels = rows_here * cols_here
    per_group = channels // GROUPS
    inner = HEADS * HEAD
    mine = half_columns(w_query, w_key, w_value, w_out)
    mine = lax.all_to_all(mine, "col", 0, 0, tiled=True)
    shift = time_shift(timestep[0], w_time, w_emb, b_emb)
    lifted = features.reshape(pixels, channels) + shift
    count = float(pixels * per_group)

    def by_group(value):
        return jnp.sum(jnp.sum(value, axis=0).reshape(GROUPS, per_group), axis=1)

    def by_channel(value):
        return jnp.repeat(value, per_group)[None, :]

    mean_here = by_group(lifted) / count
    spread_here = by_group((lifted - by_channel(mean_here)) ** 2)
    mean, spread = pooled_over_row(jnp.stack([mean_here, spread_here]), count)
    var = spread / (count * lax.axis_size("row"))
    normed = (lifted - by_channel(mean)) / by_channel(jnp.sqrt(var + 1e-06)) * gn_gain + gn_bias
    normed = normed.astype(BF16)

    mine = after(mine, normed)
    theirs = other_core(mine)
    out_weights = (mine, theirs)
    first_mine, last_mine = project(normed, mine)
    first_theirs, last_theirs = project(normed, theirs)
    first = CHIPS * HEAD
    by_head = by_core(first_mine, first_theirs).reshape(CHIPS, 3 * HEAD, pixels)
    mine = across_chips(by_head)
    upper = lax.axis_index("row") // CHIPS
    rest = by_core(last_mine, last_theirs)
    by_head = jnp.repeat(rest, CHIPS // 2, axis=0)
    theirs = other_core(mine)
    pairs = across_chips(after(by_head, mine))

    attended = attend(jnp.arange(CHIPS, dtype=jnp.int32), mine, theirs)
    pairs = after(pairs, attended)
    pairs_theirs = other_core(pairs)
    chip = lax.axis_index("row") // 2
    opposite = lambda r: (r + 8) % 16
    attended = across_chips(attended)
    places = jnp.stack([chip, (chip + 4) % CHIPS]).astype(jnp.int32)
    near, far = attend(places, pairs, pairs_theirs)
    far = move_row(far, opposite)
    place = jnp.stack([upper, lax.axis_index("row") % 2]).astype(jnp.int32)
    return add_attended(place, features, shift, attended, near, far, *out_weights)


def solution(mesh):
    return jax.shard_map(
        local,
        mesh=mesh,
        in_specs=(
            P("col", "row", None, None),
            P("col"),
            P(),
            P(),
            P(),
            P(),
            P(),
            P("col", None),
            P("col", None),
            P("col", None),
            P(None, "col"),
        ),
        out_specs=P("col", "row", None, None),
        check_vma=False,
    )
```

time: 299 us -> 256 us (0.86)
  the two profiles are of different devices: /device:TPU:34 before, /device:TPU:2 now
where the time goes in v3:
time: 256 us; the launch traced here: 254 us
  Pallas kernels  155 us (61%)
  starting transfers between devices  27.5 us (11%)
  waiting for transfers between devices  25.3 us (10%)
  blocking collectives  24.4 us (10%)
  other arithmetic  7.12 us (3%)
  matrix products  6.92 us (3%)
  local copies, waits for them, and re-layouts  6.77 us (3%)
    pallas_call x2, Pallas kernels, attend(): pl.pallas_call(attend_kernel, grid_spec=pltpu.PrefetchScalarGridSpec(num_...  136 us
    ppermute x10, waiting for transfers between devices, move_row(): return lax.ppermute(value, 'row', [(r, target(r)) for r in range(16)])  24.4 us
    all_to_all x1, blocking collectives, across_chips(): lax.all_to_all(value, 'row', 0, 0, tiled=True, axis_index_groups=groups)  24.4 us
    all_to_all x2, starting transfers between devices, across_chips(): lax.all_to_all(value, 'row', 0, 0, tiled=True, axis_index_groups=groups)  10.7 us
    ppermute x10, starting transfers between devices, move_row(): return lax.ppermute(value, 'row', [(r, target(r)) for r in range(16)])  8.9 us
    pallas_call x2, Pallas kernels, project(): pl.pallas_call(project_kernel, grid=(1,), in_specs=[pl.BlockSpec(normed.s...  8.01 us
    all_to_all x1, starting transfers between devices, local(): mine = lax.all_to_all(mine, 'col', 0, 0, tiled=True)  7.94 us
    pallas_call x1, Pallas kernels, add_attended(): pl.pallas_call(add_attended_kernel, grid=(rows_here,), in_specs=[pl.Block...  6.87 us
  transfers between devices with their start and end apart: 13, of which 7 were waited for; matrix products, arithmetic and copies ran while one was open for 7% of the time, Pallas kernels for 55%

profile of v3, /device:TPU:2, one launch (start us, length us, event | category | flops | bytes accessed | tf_op | source)
XLA Modules:
  0.0 254.1 jit_solution(3309509582397254254)
XLA Ops:
  0.0 0.0 copy-start
  0.0 4.8 %shard_map.109 = bf16[8,160,1280]{2,1,0:T(8,128)(2,1)} custom-call(s32[1]{0:T(128)} %bitcast.1.core_ref, bf16[160,640]{1,0:T(8,128)(2,1)} %query_ref.1, bf16[160,640]{1,0:T(8,128)(2,1)} %key_ref.1, bf16[160,640]{1,0:T(8,128)(2,1)} %value_ref.1, bf16[160,640]{1,0:T(8,128)(2,1)} %bitcast.189), custom_call_target="tpu_custom_call" | custom-call | tf_op jit(solution)/shard_map/pallas_call | solution.py:107
  4.8 7.9 %all-to-all-start = ((bf16[8,160,1280]{2,1,0:T(8,128)(2,1)}), bf16[8,160,1280]{2,1,0:T(8,128)(2,1)}, u32[]{:S(2)}, u32[]{:S(2)}) async-start(bf16[8,160,1280]{2,1,0:T(8,128)(2,1)} %shard_map.109), calls=%async_computation | async-start | bytes 6553600 | tf_op jit(solution)/shard_map/all_to_all | solution.py:363
  13.5 0.1 pad_maximum_fusion
  13.5 0.9 convolution_reduce_fusion.1
  14.4 0.0 copy-start.7
  14.4 0.0 copy-start.1
  14.5 6.1 %convolution_reduce_fusion = f32[1280]{0:T(1024)S(1)} fusion(f32[1280,1]{0,1:T(1,128)S(1)} %reshape.68, f32[1280,1280]{1,0:T(8,128)} %param.14), kind=kOutput, calls=%fused_computation.9 | convolution fusion | flops 19660800 | bytes 6563840 | tf_op jit(solution)/shard_map/dot_general | solution.py:26
  20.5 0.0 copy-done.1
  20.6 0.0 copy-start.5
  20.6 0.0 copy-start.6
  20.6 0.3 add_reduce_fusion
  20.9 0.1 reshape.63
  21.0 0.1 reduce_sum.37
  21.1 0.1 broadcast_in_dim.16
  21.1 0.1 sub.65
  21.2 2.1 multiply_reduce_fusion
  23.4 0.1 reshape.64
  23.4 0.1 reduce_sum.39
  23.6 0.6 collective-permute-start.2
  24.2 2.4 collective-permute-start.1
  26.6 1.8 collective-permute-start
  28.4 0.0 collective-permute-done.2
  28.4 0.8 collective-permute-done.1
  29.3 0.9 collective-permute-done
  30.2 0.1 collective-permute-start.5
  30.3 0.8 collective-permute-start.4
  31.0 1.1 collective-permute-start.3
  32.1 16.2 %collective-permute-done.5 = f32[2,32]{1,0:T(2,128)S(1)} collective-permute-done((f32[2,32]{1,0:T(2,128)S(1)}, f32[2,32]{1,0:T(2,128)S(1)}, u32[]{:S(2)}, u32[]{:S(2)}) %collective-permute-start.5) | collective-permute-done | bytes 288 | tf_op jit(solution)/shard_map/ppermute | solution.py:30
  48.4 1.0 collective-permute-done.4
  49.4 0.0 collective-permute-done.3
  49.5 0.1 broadcast_in_dim.18
  49.5 0.1 div.68
  49.6 0.1 broadcast_in_dim.17
  49.7 0.1 sub.72
  49.8 3.3 %fusion.4.refs_1_.normed_ref = bf16[512,1280]{1,0:T(8,128)(2,1)} fusion(f32[1,4,128,1280]{3,2,1,0:T(8,128)} %features_ref.1, f32[1280]{0:T(1024)S(1)} %copy-done.5, f32[1280]{0:T(1024)S(1)} %copy-done.6, f32[1280]{0:T(1024)S(1)} %div.68, f32[1280]{0:T(1024)S(1)} %sub.72, f32[1280]{0:T(1024)S(1)} %add.148), kind=kLoop, calls=%fused_computation.6 | loop fusion | flops 3932160 | bytes 3957760 | tf_op jit(solution)/shard_map/convert_element_type | solution.py:379
  53.1 0.8 all-to-all-done.refs_0_
  53.9 0.0 collective-permute-start.6
  54.0 0.5 copy-done.3
  54.4 4.0 %shard_map.111 = (bf16[4,192,512]{2,1,0:T(8,128)(2,1)S(1)}, bf16[192,512]{1,0:T(8,128)(2,1)S(1)}) custom-call(bf16[512,1280]{1,0:T(8,128)(2,1)S(1)} %copy-done.3, bf16[8,160,1280]{2,1,0:T(8,128)(2,1)} %shard_map.110.weight_ref.mine_ref), custom_call_target="tpu_custom_call" | custom-call | flops 1258291200 | bytes 4194304 | tf_op jit(solution)/shard_map/pallas_call | solution.py:143
  58.4 1.7 collective-permute-done.6.weight_ref.theirs_ref
  60.1 4.0 %shard_map.112 = (bf16[4,192,512]{2,1,0:T(8,128)(2,1)S(1)}, bf16[192,512]{1,0:T(8,128)(2,1)S(1)}) custom-call(bf16[512,1280]{1,0:T(8,128)(2,1)S(1)} %copy-done.3, bf16[8,160,1280]{2,1,0:T(8,128)(2,1)} %collective-permute-done.6.weight_ref.theirs_ref), custom_call_target="tpu_custom_call" | custom-call | flops 1258291200 | bytes 4194304 | tf_op jit(solution)/shard_map/pallas_call | solution.py:143
  64.1 0.3 maximum_select_fusion
  64.4 24.4 %all_to_all.20.refs_0_.refs_1_.refs_2_ = bf16[8,192,512]{2,1,0:T(8,128)(2,1)} all-to-all(bf16[8,192,512]{2,1,0:T(8,128)(2,1)S(1)} %bitcast.188), channel_id=1, replica_groups={{0,16,32,48,64,80,96,112},{8,24,40,56,72,88,104,120},{1,17,33,49,65,81,..., dimensions={0} | all-to-all | bytes 3145728 | tf_op jit(solution)/shard_map/all_to_all | solution.py:63
  88.8 0.0 collective-permute-start.7
  88.9 1.3 broadcast_in_dim.19
  90.2 5.2 %all-to-all-start.3 = ((bf16[8,192,512]{2,1,0:T(8,128)(2,1)}), bf16[8,192,512]{2,1,0:T(8,128)(2,1)S(1)}, u32[]{:S(2)}, u32[]{:S(2)}) async-start(bf16[8,192,512]{2,1,0:T(8,128)(2,1)} %shard_map.114), calls=%async_computation.3 | async-start | bytes 3145728 | tf_op jit(solution)/shard_map/all_to_all | solution.py:63
  95.4 0.0 collective-permute-done.7.refs_3_
  95.4 0.6 iota.7.places_ref
  95.9 106.0 %shard_map.113.refs_1_ = bf16[8,64,512]{2,1,0:T(8,128)(2,1)} custom-call(s32[8]{0:T(128)} %iota.7.places_ref, bf16[8,192,512]{2,1,0:T(8,128)(2,1)} %all_to_all.20.refs_0_.refs_1_.refs_2_, bf16[8,192,512]{2,1,0:T(8,128)(2,1)} %all_to_all.20.refs_0_.refs_1_.refs_2_, bf16[8,192,512]{2,1,0:T(8,128)(2,1)} %all_to_all.20.refs_0_.refs_1_.refs_2_, ...), custom_call_target="tpu_custom_call" | custom-call | flops 42949672960 | bytes 8388608 | tf_op jit(solution)/shard_map/pallas_call | solution.py:275
  202.0 0.0 all-to-all-done.3.refs_0_
  202.0 1.1 copy-done.4
  203.1 0.0 collective-permute-start.8
  203.1 0.6 pad_add_fusion.1.places_ref
  203.8 5.4 %all-to-all-start.2 = ((bf16[8,64,512]{2,1,0:T(8,128)(2,1)}), bf16[8,64,512]{2,1,0:T(8,128)(2,1)S(1)}, u32[]{:S(2)}, u32[]{:S(2)}) async-start(bf16[8,64,512]{2,1,0:T(8,128)(2,1)} %shard_map.113.refs_1_), calls=%async_computation.2 | async-start | bytes 1048576 | tf_op jit(solution)/shard_map/all_to_all | solution.py:63
  209.2 0.0 collective-permute-done.8.refs_3_
  209.2 29.6 %shard_map.116 = bf16[2,64,512]{2,1,0:T(8,128)(2,1)} custom-call(s32[2]{0:T(128)} %pad_add_fusion.1.places_ref, bf16[8,192,512]{2,1,0:T(8,128)(2,1)} %shard_map.115.refs_0_.refs_1_.refs_2_, bf16[8,192,512]{2,1,0:T(8,128)(2,1)} %shard_map.115.refs_0_.refs_1_.refs_2_, bf16[8,192,512]{2,1,0:T(8,128)(2,1)} %shard_map.115.refs_0_.refs_1_.refs_2_, ...), custom_call_target="tpu_custom_call" | custom-call | flops 10737418240 | bytes 8388608 | tf_op jit(solution)/shard_map/pallas_call | solution.py:275
  238.8 0.9 slice_bitcast_fusion
  239.7 2.1 collective-permute-start.9
  241.8 0.1 pad_add_fusion.place_ref
  241.9 0.0 all-to-all-done.2.first_ref
  241.9 3.6 %collective-permute-done.9.far_ref = bf16[64,512]{1,0:T(8,128)(2,1)S(1)} collective-permute-done((bf16[64,512]{1,0:T(8,128)(2,1)S(1)}, bf16[64,512]{1,0:T(8,128)(2,1)S(1)}, u32[]{:S(2)}, u32[]{:S(2)}) %collective-permute-start.9) | collective-permute-done | bytes 65568 | tf_op jit(solution)/shard_map/ppermute | solution.py:30
  245.5 1.7 copy-done.2
  247.3 6.9 %shard_map.117 = f32[1,4,128,1280]{3,2,1,0:T(8,128)} custom-call(s32[2]{0:T(128)S(1)} %pad_add_fusion.place_ref, f32[1,4,128,1280]{3,2,1,0:T(8,128)S(1)} %copy-done.2, f32[1,1280]{1,0:T(1,128)S(1)} %add.149.shift_ref, bf16[8,64,512]{2,1,0:T(8,128)(2,1)S(1)} %all-to-all-done.2.first_ref, bf16[64,512]{1,0:T(8,128)(2,1)S(1)} %get-tuple-element.18.near_ref, ...), custom_call_target="tpu_custom_call" | custom-call | flops 838860800 | bytes 5242880 | tf_op jit(solution)/shard_map/pallas_call | solution.py:335
  (22 shorter events, 0.2 us)
Async XLA Ops:
  0.0 13.5 %copy-start = (f32[320,1280]{1,0:T(8,128)S(1)}, f32[320,1280]{1,0:T(8,128)}, u32[]{:S(2)}) copy-start(f32[320,1280]{1,0:T(8,128)} %param.13) | copy-start | bytes 4915204
  4.8 49.1 %all-to-all-start = ((bf16[8,160,1280]{2,1,0:T(8,128)(2,1)}), bf16[8,160,1280]{2,1,0:T(8,128)(2,1)}, u32[]{:S(2)}, u32[]{:S(2)}) async-start(bf16[8,160,1280]{2,1,0:T(8,128)(2,1)} %shard_map.109), calls=%async_computation | async-start | bytes 6553600 | tf_op jit(solution)/shard_map/all_to_all | solution.py:363
  14.4 6.1 %copy-start.7 = (f32[1280]{0:T(1024)S(1)}, f32[1280]{0:T(1024)}, u32[]{:S(2)}) copy-start(f32[1280]{0:T(1024)} %param.15) | copy-start | bytes 15364
  14.4 6.1 %copy-start.1 = (f32[1,4,128,1280]{3,2,1,0:T(8,128)S(1)}, f32[1,4,128,1280]{3,2,1,0:T(8,128)}, u32[]{:S(2)}) copy-start(f32[1,4,128,1280]{3,2,1,0:T(8,128)} %features_ref.1) | copy-start | bytes 7864324
  20.6 29.2 %copy-start.5 = (f32[1280]{0:T(1024)S(1)}, f32[1280]{0:T(1024)}, u32[]{:S(2)}) copy-start(f32[1280]{0:T(1024)} %param.17) | copy-start | bytes 15364
  20.6 29.2 %copy-start.6 = (f32[1280]{0:T(1024)S(1)}, f32[1280]{0:T(1024)}, u32[]{:S(2)}) copy-start(f32[1280]{0:T(1024)} %param.16) | copy-start | bytes 15364
  23.6 4.8 %collective-permute-start.2 = (f32[2,32]{1,0:T(2,128)S(1)}, f32[2,32]{1,0:T(2,128)S(1)}, u32[]{:S(2)}, u32[]{:S(2)}) collective-permute-start(f32[2,32]{1,0:T(2,128)S(1)} %pad_maximum_fusion.1), channel_id=1, source_target_pairs={{0,96},{8,104},{16,112},{24,120},{32,0},{40,8},{48,16},{56,24},{64... | collective-permute-start | bytes 776 | tf_op jit(solution)/shard_map/ppermute | solution.py:30
  24.2 5.1 %collective-permute-start.1 = (f32[2,32]{1,0:T(2,128)S(1)}, f32[2,32]{1,0:T(2,128)S(1)}, u32[]{:S(2)}, u32[]{:S(2)}) collective-permute-start(f32[2,32]{1,0:T(2,128)S(1)} %pad_maximum_fusion.1), channel_id=1, source_target_pairs={{0,64},{8,72},{16,80},{24,88},{32,96},{40,104},{48,112},{56,120},{... | collective-permute-start | bytes 776 | tf_op jit(solution)/shard_map/ppermute | solution.py:30
  26.6 3.6 %collective-permute-start = (f32[2,32]{1,0:T(2,128)S(1)}, f32[2,32]{1,0:T(2,128)S(1)}, u32[]{:S(2)}, u32[]{:S(2)}) collective-permute-start(f32[2,32]{1,0:T(2,128)S(1)} %pad_maximum_fusion.1), channel_id=1, source_target_pairs={{0,32},{8,40},{16,48},{24,56},{32,64},{40,72},{48,80},{56,88},{64,... | collective-permute-start | bytes 776 | tf_op jit(solution)/shard_map/ppermute | solution.py:30
  30.2 18.2 %collective-permute-start.5 = (f32[2,32]{1,0:T(2,128)S(1)}, f32[2,32]{1,0:T(2,128)S(1)}, u32[]{:S(2)}, u32[]{:S(2)}) collective-permute-start(f32[2,32]{1,0:T(2,128)S(1)} %pad_maximum_fusion.2), channel_id=1, source_target_pairs={{0,24},{8,16},{16,8},{24,0},{32,56},{40,48},{48,40},{56,32},{64,88... | collective-permute-start | bytes 776 | tf_op jit(solution)/shard_map/ppermute | solution.py:30
  30.3 19.1 %collective-permute-start.4 = (f32[2,32]{1,0:T(2,128)S(1)}, f32[2,32]{1,0:T(2,128)S(1)}, u32[]{:S(2)}, u32[]{:S(2)}) collective-permute-start(f32[2,32]{1,0:T(2,128)S(1)} %pad_maximum_fusion.2), channel_id=1, source_target_pairs={{0,16},{8,24},{16,0},{24,8},{32,48},{40,56},{48,32},{56,40},{64,80... | collective-permute-start | bytes 776 | tf_op jit(solution)/shard_map/ppermute | solution.py:30
  31.0 18.4 %collective-permute-start.3 = (f32[2,32]{1,0:T(2,128)S(1)}, f32[2,32]{1,0:T(2,128)S(1)}, u32[]{:S(2)}, u32[]{:S(2)}) collective-permute-start(f32[2,32]{1,0:T(2,128)S(1)} %pad_maximum_fusion.2), channel_id=1, source_target_pairs={{0,8},{8,0},{16,24},{24,16},{32,40},{40,32},{48,56},{56,48},{64,72... | collective-permute-start | bytes 776 | tf_op jit(solution)/shard_map/ppermute | solution.py:30
  53.1 1.3 copy-start.3
  53.9 6.2 %collective-permute-start.6 = (bf16[8,160,1280]{2,1,0:T(8,128)(2,1)}, bf16[8,160,1280]{2,1,0:T(8,128)(2,1)}, u32[]{:S(2)}, u32[]{:S(2)}) collective-permute-start(bf16[8,160,1280]{2,1,0:T(8,128)(2,1)} %shard_map.110.weight_ref.mine_ref), channel_id=1, source_target_pairs={{0,8},{8,0},{16,24},{24,16},{32,40},{40,32},{48,56},{56,48},{64,72... | collective-permute-start | bytes 9830408 | tf_op jit(solution)/shard_map/ppermute | solution.py:30
  88.8 6.5 %collective-permute-start.7 = (bf16[8,192,512]{2,1,0:T(8,128)(2,1)}, bf16[8,192,512]{2,1,0:T(8,128)(2,1)}, u32[]{:S(2)}, u32[]{:S(2)}) collective-permute-start(bf16[8,192,512]{2,1,0:T(8,128)(2,1)} %all_to_all.20.refs_0_.refs_1_.refs_2_), channel_id=1, source_target_pairs={{0,8},{8,0},{16,24},{24,16},{32,40},{40,32},{48,56},{56,48},{64,72... | collective-permute-start | bytes 4718600 | tf_op jit(solution)/shard_map/ppermute | solution.py:30
  90.2 111.8 %all-to-all-start.3 = ((bf16[8,192,512]{2,1,0:T(8,128)(2,1)}), bf16[8,192,512]{2,1,0:T(8,128)(2,1)S(1)}, u32[]{:S(2)}, u32[]{:S(2)}) async-start(bf16[8,192,512]{2,1,0:T(8,128)(2,1)} %shard_map.114), calls=%async_computation.3 | async-start | bytes 3145728 | tf_op jit(solution)/shard_map/all_to_all | solution.py:63
  202.0 1.1 copy-start.4
  203.1 6.1 %collective-permute-start.8 = (bf16[8,192,512]{2,1,0:T(8,128)(2,1)}, bf16[8,192,512]{2,1,0:T(8,128)(2,1)}, u32[]{:S(2)}, u32[]{:S(2)}) collective-permute-start(bf16[8,192,512]{2,1,0:T(8,128)(2,1)} %shard_map.115.refs_0_.refs_1_.refs_2_), channel_id=1, source_target_pairs={{0,8},{8,0},{16,24},{24,16},{32,40},{40,32},{48,56},{56,48},{64,72... | collective-permute-start | bytes 4718600 | tf_op jit(solution)/shard_map/ppermute | solution.py:30
  203.8 38.1 %all-to-all-start.2 = ((bf16[8,64,512]{2,1,0:T(8,128)(2,1)}), bf16[8,64,512]{2,1,0:T(8,128)(2,1)S(1)}, u32[]{:S(2)}, u32[]{:S(2)}) async-start(bf16[8,64,512]{2,1,0:T(8,128)(2,1)} %shard_map.113.refs_1_), calls=%async_computation.2 | async-start | bytes 1048576 | tf_op jit(solution)/shard_map/all_to_all | solution.py:63
  239.7 5.8 %collective-permute-start.9 = (bf16[64,512]{1,0:T(8,128)(2,1)S(1)}, bf16[64,512]{1,0:T(8,128)(2,1)S(1)}, u32[]{:S(2)}, u32[]{:S(2)}) collective-permute-start(bf16[64,512]{1,0:T(8,128)(2,1)S(1)} %get-tuple-element.17), channel_id=1, source_target_pairs={{0,64},{8,72},{16,80},{24,88},{32,96},{40,104},{48,112},{56,120},{... | collective-permute-start | bytes 196616 | tf_op jit(solution)/shard_map/ppermute | solution.py:30
  245.5 1.7 copy-start.2

commit v4 on v3

v4 whole, which is shorter than its diff:
```python
import functools
import math

import jax
import jax.numpy as jnp
from jax import lax
from jax.experimental import pallas as pl
from jax.experimental.pallas import tpu as pltpu
from jax.sharding import PartitionSpec as P

GROUPS = 32
HEADS = 10
HEAD = 64
CHIPS = 8
F32 = jnp.float32
BF16 = jnp.bfloat16
SCALE = math.log2(math.e) / math.sqrt(HEAD)


NO_COST = pl.CostEstimate(flops=0, bytes_accessed=0, transcendentals=0)


def time_shift_kernel(table_ref, time_ref, emb_ref, bias_ref, out_ref, hidden, total):
    step = pl.program_id(0)
    depth = emb_ref.shape[0]

    @pl.when(step == 0)
    def _():
        value = jnp.sum(table_ref[...] * time_ref[...], axis=0, keepdims=True)
        value = value / (1.0 + jnp.exp(-value))
        hidden[...] = jnp.broadcast_to(value, (8, value.shape[1])).T
        total[...] = jnp.zeros_like(total)

    part = hidden[pl.ds(pl.multiple_of(step * depth, depth), depth), 0:1] * emb_ref[...]
    total[...] += jnp.sum(part.reshape(depth // 8, 8, part.shape[1]), axis=0)

    @pl.when(step == pl.num_programs(0) - 1)
    def _():
        out_ref[...] = jnp.sum(total[...], axis=0, keepdims=True) + bias_ref[...]


def time_shift(step_value, w_time, w_emb, b_emb):
    half = w_time.shape[0] // 2
    channels = w_emb.shape[1]
    freqs = jnp.exp(-math.log(10000.0) * jnp.arange(half, dtype=F32) / half)
    angles = step_value.astype(F32) * freqs
    table = jnp.concatenate([jnp.cos(angles), jnp.sin(angles)])[:, None]
    steps = 4
    return pl.pallas_call(
        time_shift_kernel,
        grid=(steps,),
        in_specs=[
            pl.BlockSpec(table.shape, lambda i: (0, 0)),
            pl.BlockSpec(w_time.shape, lambda i: (0, 0)),
            pl.BlockSpec((w_emb.shape[0] // steps, channels), lambda i: (i, 0)),
            pl.BlockSpec((1, channels), lambda i: (0, 0)),
        ],
        out_specs=pl.BlockSpec((1, channels), lambda i: (0, 0)),
        out_shape=jax.ShapeDtypeStruct((1, channels), F32),
        scratch_shapes=[pltpu.VMEM((w_emb.shape[0], 8), F32), pltpu.VMEM((8, channels), F32)],
        compiler_params=pltpu.CompilerParams(vmem_limit_bytes=48 * 2**20),
        cost_estimate=NO_COST,
    )(table, w_time, w_emb, b_emb[None, :])


def spread_kernel(features_ref, out_ref):
    value = features_ref[...].reshape(-1, features_ref.shape[3])
    count = value.shape[0]
    mean = jnp.sum(value, axis=0, keepdims=True) / count
    out_ref[0:1, :] = mean
    out_ref[1:2, :] = jnp.sum((value - mean) ** 2, axis=0, keepdims=True)


def channel_spread(features):
    return pl.pallas_call(
        spread_kernel,
        out_shape=jax.ShapeDtypeStruct((2, features.shape[3]), F32),
        compiler_params=pltpu.CompilerParams(vmem_limit_bytes=48 * 2**20),
        cost_estimate=NO_COST,
    )(features)


def normalise_kernel(features_ref, group_ref, shift_ref, gain_ref, bias_ref, out_ref):
    lifted = features_ref[0, 0] + shift_ref[...]
    value = (lifted - group_ref[0:1, :]) * (1.0 / group_ref[1:2, :])
    out_ref[...] = (value * gain_ref[...] + bias_ref[...]).astype(BF16)


def normalise(features, group, *rows):
    unused, rows_here, cols_here, channels = features.shape
    row = pl.BlockSpec((1, channels), lambda i: (0, 0))
    return pl.pallas_call(
        normalise_kernel,
        grid=(rows_here,),
        in_specs=[
            pl.BlockSpec((1, 1, cols_here, channels), lambda i: (0, i, 0, 0)),
            pl.BlockSpec(group.shape, lambda i: (0, 0)),
        ]
        + [row] * len(rows),
        out_specs=pl.BlockSpec((cols_here, channels), lambda i: (i, 0)),
        out_shape=jax.ShapeDtypeStruct((rows_here * cols_here, channels), BF16),
        cost_estimate=NO_COST,
    )(features, group, *[value.reshape(1, channels) for value in rows])


def move_row(value, target):
    return lax.ppermute(value, "row", [(r, target(r)) for r in range(16)])


def move_col(value, target):
    return lax.ppermute(value, "col", [(c, target(c)) for c in range(8)])


def along_x(step):
    return lambda r: ((r // 4 + step) % 4) * 4 + r % 4


def along_z(step):
    return lambda c: ((c // 2 + step) % 4) * 2 + c % 2


def after(value, *others):
    anywhere = pl.BlockSpec(memory_space=pl.ANY)
    return pl.pallas_call(
        lambda *refs: None,
        in_specs=[anywhere] * (1 + len(others)),
        out_specs=anywhere,
        out_shape=jax.ShapeDtypeStruct(value.shape, value.dtype),
        input_output_aliases={0: 0},
        cost_estimate=pl.CostEstimate(flops=0, bytes_accessed=0, transcendentals=0),
    )(value, *others)


def other_core(value):
    return move_row(value, lambda r: r ^ 1)


def across_chips(value):
    groups = [list(range(0, 16, 2)), list(range(1, 16, 2))]
    return lax.all_to_all(value, "row", 0, 0, tiled=True, axis_index_groups=groups)


def pooled(parts, count):
    mean = sum(p[0] for p in parts) / len(parts)
    spread = sum(p[1] for p in parts) + count * sum((p[0] - mean) ** 2 for p in parts)
    return jnp.stack([mean, spread])


def pooled_over_row(stat, count):
    parts = [stat] + [move_row(stat, along_x(d)) for d in (1, 2, 3)]
    stat = pooled(parts, count)
    parts = [stat] + [move_row(stat, lambda r, k=k: r ^ k) for k in (1, 2, 3)]
    return pooled(parts, 4 * count)


def half_columns_kernel(core_ref, query_ref, key_ref, value_ref, out_w_ref, out_ref, packed, sems):
    def put(low, last, start):
        parts = [out_w_ref[:, start : start + out_w_ref.shape[1] // 2]]
        for head in (low, low + 1, low + 2, low + 3, last):
            parts += [ref[:, head * HEAD : (head + 1) * HEAD] for ref in (query_ref, key_ref, value_ref)]
        packed[...] = jnp.concatenate(parts, axis=1)

    @pl.when(core_ref[0] == 0)
    def _():
        put(0, 8, 0)

    @pl.when(core_ref[0] == 1)
    def _():
        put(4, 9, out_w_ref.shape[1] // 2)

    copies = [pltpu.make_async_copy(packed, out_ref.at[i], sems.at[i]) for i in range(out_ref.shape[0])]
    for copy in copies:
        copy.start()
    for copy in copies:
        copy.wait()


def half_columns(w_query, w_key, w_value, w_out):
    core = (lax.axis_index("row") % 2).astype(jnp.int32).reshape(1)
    size = lax.axis_size("col")
    depth = w_query.shape[0]
    width = (3 * w_query.shape[1] + w_out.shape[0]) // 2
    return pl.pallas_call(
        half_columns_kernel,
        in_specs=[pl.BlockSpec(memory_space=pltpu.SMEM)] + [pl.BlockSpec(memory_space=pltpu.VMEM)] * 4,
        out_specs=pl.BlockSpec(memory_space=pl.ANY),
        out_shape=jax.ShapeDtypeStruct((size, depth, width), BF16),
        scratch_shapes=[pltpu.VMEM((depth, width), BF16), pltpu.SemaphoreType.DMA((size,))],
        compiler_params=pltpu.CompilerParams(vmem_limit_bytes=62 * 2**20),
    )(core, w_query, w_key, w_value, w_out.T)


def by_core(mine, theirs):
    core = lax.axis_index("row") % 2
    return jnp.where(core == 0, jnp.stack([mine, theirs]), jnp.stack([theirs, mine]))


def project_kernel(normed_ref, weight_ref, out_ref):
    weight = weight_ref[...].reshape(normed_ref.shape[1], weight_ref.shape[2])
    out_ref[...] = product(normed_ref[...], weight).T.astype(BF16)


def project(normed, weight):
    pixels, channels = normed.shape
    size, depth, width = weight.shape
    rows = HEADS // 2 * 3 * HEAD
    lanes = 256
    skip = (width - rows) // lanes
    out = pl.pallas_call(
        project_kernel,
        grid=(width // lanes - skip,),
        in_specs=[
            pl.BlockSpec((pixels, channels), lambda i: (0, 0)),
            pl.BlockSpec((size, depth, lanes), lambda i: (0, 0, i + skip)),
        ],
        out_specs=pl.BlockSpec((lanes, pixels), lambda i: (i, 0)),
        out_shape=jax.ShapeDtypeStruct((width - skip * lanes, pixels), BF16),
        compiler_params=pltpu.CompilerParams(vmem_limit_bytes=48 * 2**20),
        cost_estimate=pl.CostEstimate(
            flops=2 * normed.size * rows, bytes_accessed=2**22, transcendentals=0
        ),
    )(normed, weight)
    out = out[-rows:]
    return out[: -3 * HEAD].reshape(HEADS // 2 - 1, 3 * HEAD, pixels), out[-3 * HEAD :]


def split3(value):
    high = value.astype(BF16)
    rest = value - high.astype(F32)
    middle = rest.astype(BF16)
    low = (rest - middle.astype(F32)).astype(BF16)
    return high, middle, low


def product(a, b):
    return lax.dot_general(a, b, (((1,), (0,)), ((), ())), preferred_element_type=F32)


def put_keys(keys, vals, place, key_t, value_t):
    count = key_t.shape[1]
    row = lax.broadcasted_iota(jnp.int32, (HEAD, count), 0)
    ones = jnp.where(row < 3, 1.0, 0.0).astype(BF16)
    wide = jnp.concatenate([key_t, key_t, key_t, ones], axis=0)
    keys[place : place + count, :] = wide.T
    vals[:, place : place + count] = value_t


def put_top(query, top):
    width = top.shape[1]
    row = lax.broadcasted_iota(jnp.int32, (HEAD, width), 0)
    high, middle, low = split3(-top)
    wide = [jnp.broadcast_to(part, (HEAD, width)).astype(F32) for part in (high, middle, low)]
    rows = jnp.where(row == 0, wide[0], jnp.where(row == 1, wide[1], jnp.where(row == 2, wide[2], 0.0)))
    query[3 * HEAD :, :] = rows.astype(BF16)


def attend_rows(query, keys, vals, total_ref, accum_ref, query_t, chunk):
    width = query_t.shape[1]
    count = keys.shape[0]
    for at, part in enumerate(split3(query_t.astype(F32) * SCALE)):
        query[at * HEAD : (at + 1) * HEAD, :] = part

    def scores(start, size):
        return product(keys[pl.ds(start, size), :], query[...])

    def run(top, chunk):
        put_top(query, top)

        def step(i, state):
            total, accum = state
            start = pl.multiple_of(i * chunk, chunk)
            weights = jnp.exp2(scores(start, chunk))
            total = total + jnp.sum(weights.reshape(chunk // 8, 8, width), axis=0)
            accum = accum + product(vals[:, pl.ds(start, chunk)], weights.astype(BF16))
            return total, accum

        state = (jnp.zeros((8, width), F32), jnp.zeros((HEAD, width), F32))
        total, accum = lax.fori_loop(0, count // chunk, step, state)
        total_ref[...] = jnp.sum(total, axis=0, keepdims=True)
        accum_ref[...] = accum

    query[3 * HEAD :, :] = jnp.zeros((HEAD, width), BF16)
    run(jnp.max(scores(0, 256), axis=0, keepdims=True), chunk)
    small = jnp.max(jnp.where(total_ref[...] < 1e30, 0.0, 1.0))

    @pl.when(small > 0.5)
    def _():
        query[3 * HEAD :, :] = jnp.zeros((HEAD, width), BF16)

        def step(i, top):
            start = pl.multiple_of(i * 512, 512)
            return jnp.maximum(top, jnp.max(scores(start, 512), axis=0, keepdims=True))

        run(lax.fori_loop(0, count // 512, step, jnp.full((1, width), -jnp.inf, F32)), 512)

    return (accum_ref[...] / total_ref[...]).astype(BF16)


def attention_scratch(count, width):
    return [
        pltpu.VMEM((4 * HEAD, width), BF16),
        pltpu.VMEM((count, 4 * HEAD), BF16),
        pltpu.VMEM((HEAD, count), BF16),
        pltpu.VMEM((1, width), F32),
        pltpu.VMEM((HEAD, width), F32),
    ]


def cost(queries, count):
    return pl.CostEstimate(
        flops=20 * queries * count * HEAD, bytes_accessed=8 * 1024 * 1024, transcendentals=queries * count
    )


def attend_kernel(stride, query_ref, *refs):
    sources, (out_ref, query, keys, vals, total, accum) = refs[:-6], refs[-6:]
    chips, rows, pixels = sources[0].shape

    @pl.when(pl.program_id(0) == 0)
    def _():
        place = 0
        for ref in sources:
            for chip in range(chips):
                for end in range(stride, rows + 1, stride):
                    key, value = ref[chip, end - 2 * HEAD : end - HEAD], ref[chip, end - HEAD : end]
                    put_keys(keys, vals, place, key, value)
                    place += pixels

    query_t = jnp.concatenate([query_ref[0], query_ref[1]], axis=1)
    attended = attend_rows(query, keys, vals, total, accum, query_t, 8192)
    for at in range(2):
        out_ref[at] = attended[:, at * pixels : (at + 1) * pixels]


def attend(queries, mine, theirs, stride):
    sources = [mine] if theirs is None else [mine, theirs]
    blocks, unused, pixels = queries.shape
    count = sum(source.shape[0] * source.shape[1] // stride * pixels for source in sources)
    return pl.pallas_call(
        functools.partial(attend_kernel, stride),
        grid=(blocks // 2,),
        in_specs=[pl.BlockSpec((2, HEAD, pixels), lambda i: (i, 0, 0))]
        + [pl.BlockSpec(source.shape, lambda i: (0, 0, 0)) for source in sources],
        out_specs=pl.BlockSpec((2, HEAD, pixels), lambda i: (i, 0, 0)),
        out_shape=jax.ShapeDtypeStruct((blocks, HEAD, pixels), BF16),
        scratch_shapes=attention_scratch(count, 2 * pixels),
        compiler_params=pltpu.CompilerParams(vmem_limit_bytes=56 * 2**20),
        cost_estimate=cost(blocks * pixels, count),
    )(queries, *sources)


def add_attended_kernel(
    core_ref, features_ref, shift_ref, first_ref, near_ref, far_ref, mine_ref, theirs_ref,
    out_ref, rows, attended, weights,
):
    heads, size, pixels = first_ref.shape
    unused, channels, half = weights.shape
    here = features_ref.shape[1] * features_ref.shape[2]

    @pl.when(pl.program_id(0) == 0)
    def _():
        core = core_ref[0]
        rows[: heads * size, :] = first_ref[...].reshape(heads * size, pixels)
        start = heads * size
        rows[pl.ds(pl.multiple_of(start + core * size, size), size), :] = near_ref[...]
        rows[pl.ds(pl.multiple_of(start + (1 - core) * size, size), size), :] = far_ref[...]
        for at in range(2):
            attended[at] = rows[at * half : (at + 1) * half, :].T
        weights[core] = mine_ref[:, :, :half].reshape(channels, half)
        weights[1 - core] = theirs_ref[:, :, :half].reshape(channels, half)

    here = pl.ds(pl.multiple_of(pl.program_id(0) * here, here), here)
    added = [
        lax.dot_general(
            attended[at, here, :], weights[at], (((1,), (1,)), ((), ())), preferred_element_type=F32
        )
        for at in range(2)
    ]
    lifted = features_ref[...].reshape(added[0].shape) + shift_ref[...]
    out_ref[...] = (lifted + (added[0] + added[1])).reshape(out_ref.shape)


def add_attended(core, features, shift, first, near, far, mine, theirs):
    unused_one, rows_here, cols_here, channels = features.shape
    pixels = rows_here * cols_here
    half = HEADS * HEAD // 2

    def whole(value):
        return pl.BlockSpec(value.shape, lambda i: (0,) * value.ndim)

    block = pl.BlockSpec((1, rows_here // 2, cols_here, channels), lambda i: (0, i, 0, 0))
    lanes = pl.BlockSpec(mine.shape[:2] + (-(-half // 128) * 128,), lambda i: (0, 0, 0))
    return pl.pallas_call(
        add_attended_kernel,
        grid=(2,),
        in_specs=[pl.BlockSpec(memory_space=pltpu.SMEM), block]
        + [whole(value) for value in (shift, first, near, far)]
        + [lanes, lanes],
        out_specs=block,
        out_shape=jax.ShapeDtypeStruct(features.shape, F32),
        scratch_shapes=[
            pltpu.VMEM((2 * half, pixels), BF16),
            pltpu.VMEM((2, pixels, half), BF16),
            pltpu.VMEM((2, channels, half), BF16),
        ],
        compiler_params=pltpu.CompilerParams(vmem_limit_bytes=48 * 2**20),
        cost_estimate=pl.CostEstimate(
            flops=4 * features.size * half, bytes_accessed=8 * features.size, transcendentals=0
        ),
    )(core, features, shift, first, near, far, mine, theirs)


def local(
    features, timestep, w_time, w_emb, b_emb, gn_gain, gn_bias, w_query, w_key, w_value, w_out
):
    unused_one, rows_here, cols_here, channels = features.shape
    pixels = rows_here * cols_here
    per_group = channels // GROUPS
    inner = HEADS * HEAD
    mine = half_columns(w_query, w_key, w_value, w_out)
    mine = lax.all_to_all(mine, "col", 0, 0, tiled=True)
    pooled_stat = pooled_over_row(channel_spread(features), float(pixels))
    mean, spread = pooled_stat
    shift = time_shift(timestep[0], w_time, w_emb, b_emb)
    count = float(pixels * lax.axis_size("row"))
    means = (mean[None, :] + shift).reshape(GROUPS, per_group)
    mean = jnp.sum(means, axis=1) / per_group
    spread = jnp.sum(spread.reshape(GROUPS, per_group) + count * (means - mean[:, None]) ** 2, axis=1)
    var = spread / (count * per_group)

    group = jnp.repeat(jnp.stack([mean, jnp.sqrt(var + 1e-06)]), per_group, axis=1)
    normed = normalise(features, group, shift, gn_gain, gn_bias)

    mine = after(mine, normed)
    theirs = other_core(mine)
    out_weights = (mine, theirs)
    first_mine, last_mine = project(normed, mine)
    first_theirs, last_theirs = project(normed, theirs)
    first = CHIPS * HEAD
    by_head = by_core(first_mine, first_theirs).reshape(CHIPS, 3 * HEAD, pixels)
    mine = across_chips(by_head)
    rest = jnp.stack([last_mine, other_core(last_theirs)])
    pairs = jnp.broadcast_to(rest[None, :, HEAD:], (CHIPS, 2, 2 * HEAD, pixels))
    theirs = other_core(mine)
    pairs = across_chips(after(pairs, mine))

    attended = attend(mine, mine, theirs, 3 * HEAD)
    pairs = after(pairs, attended)
    attended = across_chips(attended)
    near, far = attend(rest[:, :HEAD], pairs.reshape(CHIPS, 4 * HEAD, pixels), None, 2 * HEAD)
    core = (lax.axis_index("row") % 2).astype(jnp.int32).reshape(1)
    return add_attended(core, features, shift, attended, near, other_core(far), *out_weights)


def solution(mesh):
    return jax.shard_map(
        local,
        mesh=mesh,
        in_specs=(
            P("col", "row", None, None),
            P("col"),
            P(),
            P(),
            P(),
            P(),
            P(),
            P("col", None),
            P("col", None),
            P("col", None),
            P(None, "col"),
        ),
        out_specs=P("col", "row", None, None),
        check_vma=False,
    )
```

time: 256 us -> 246 us (0.961)
  matrix products: 6.92 us -> 0 us
  local copies, waits for them, and re-layouts: 6.77 us -> 12.3 us
  other arithmetic: 7.12 us -> 1.61 us
    dot_general x2 -> x0, matrix products: 6.92 us -> none  [the longest x1 6.05 us: time_shift(): jnp.dot(hidden, w_emb, precision=lax.Precision.HIGHEST) + b_emb[None, :]]
    unnamed x16 -> x26, local copies, waits for them, and re-layouts: 3.38 us -> 6.73 us
    convert_element_type x1 -> x0, other arithmetic: 3.29 us -> none  [local(): normed = normed.astype(BF16)]
    pallas_call x6 -> x9, Pallas kernels: 155 us -> 153 us  [the longest x2 132 us: attend(): pl.pallas_call(functools.partial(attend_kernel, stride), grid=(blocks //...]
  transfers between devices with their start and end apart: 13 -> 13, of which waited for: 7 -> 4; matrix products, arithmetic and copies ran while one was open for 7% -> 3% of each run, Pallas kernels for 55% -> 58%
where the time goes in v4:
time: 246 us; the launch traced here: 245 us
  Pallas kernels  153 us (62%)
  starting transfers between devices  26.6 us (11%)
  blocking collectives  25.2 us (10%)
  waiting for transfers between devices  24.9 us (10%)
  local copies, waits for them, and re-layouts  12.3 us (5%)
    pallas_call x2, Pallas kernels, attend(): pl.pallas_call(functools.partial(attend_kernel, stride), grid=(blocks //...  132 us
    all_to_all x1, blocking collectives, across_chips(): lax.all_to_all(value, 'row', 0, 0, tiled=True, axis_index_groups=groups)  25.2 us
    ppermute x10, waiting for transfers between devices, move_row(): return lax.ppermute(value, 'row', [(r, target(r)) for r in range(16)])  24.9 us
    all_to_all x2, starting transfers between devices, across_chips(): lax.all_to_all(value, 'row', 0, 0, tiled=True, axis_index_groups=groups)  11 us
    all_to_all x1, starting transfers between devices, local(): mine = lax.all_to_all(mine, 'col', 0, 0, tiled=True)  7.96 us
    ppermute x10, starting transfers between devices, move_row(): return lax.ppermute(value, 'row', [(r, target(r)) for r in range(16)])  7.67 us
    unnamed x26, local copies, waits for them, and re-layouts  6.73 us
    pallas_call x2, Pallas kernels, project(): pl.pallas_call(project_kernel, grid=(width // lanes - skip,), in_specs=[p...  5.1 us
  transfers between devices with their start and end apart: 13, of which 4 were waited for; matrix products, arithmetic and copies ran while one was open for 3% of the time, Pallas kernels for 58%

profile of v4, /device:TPU:2, one launch (start us, length us, event | category | flops | bytes accessed | tf_op | source)
XLA Modules:
  0.0 245.0 jit_solution(4945331919636078258)
XLA Ops:
  0.0 3.1 %shard_map.112 = bf16[8,160,1280]{2,1,0:T(8,128)(2,1)} custom-call(s32[1]{0:T(128)} %bitcast.core_ref, bf16[160,640]{1,0:T(8,128)(2,1)} %query_ref.1, bf16[160,640]{1,0:T(8,128)(2,1)} %key_ref.1, bf16[160,640]{1,0:T(8,128)(2,1)} %value_ref.1, bf16[160,640]{1,0:T(8,128)(2,1)} %bitcast.24), custom_call_target="tpu_custom_call" | custom-call | tf_op jit(solution)/shard_map/pallas_call | solution.py:183
  3.1 8.0 %all-to-all-start = ((bf16[8,160,1280]{2,1,0:T(8,128)(2,1)}), bf16[8,160,1280]{2,1,0:T(8,128)(2,1)S(1)}, u32[]{:S(2)}, u32[]{:S(2)}) async-start(bf16[8,160,1280]{2,1,0:T(8,128)(2,1)} %shard_map.112), calls=%async_computation | async-start | bytes 6553600 | tf_op jit(solution)/shard_map/all_to_all | solution.py:421
  11.1 1.7 copy-done.2
  12.8 0.6 shard_map.110
  13.4 1.6 collective-permute-start
  15.0 1.1 collective-permute-start.1
  16.1 2.2 collective-permute-start.2
  19.0 0.0 collective-permute-done
  19.0 1.2 collective-permute-done.1
  20.2 0.1 fusion.3
  20.3 0.1 collective-permute-start.3
  20.4 0.8 collective-permute-start.4
  21.2 1.1 collective-permute-start.5
  22.3 0.1 pad_maximum_fusion.3
  22.3 0.1 broadcast_in_dim.20.table_ref
  22.5 0.6 reshape.80.gain_ref
  23.1 0.6 reshape.81.bias_ref
  23.7 4.2 %shard_map.109.shift_ref = f32[1,1280]{1,0:T(1,128)S(1)} custom-call(f32[320,1]{1,0:T(8,128)S(1)} %broadcast_in_dim.20.table_ref, f32[320,1280]{1,0:T(8,128)S(1)} %copy-done.6, f32[1280,1280]{1,0:T(8,128)} %emb_ref.1, f32[1,1280]{1,0:T(1,128)S(1)} %broadcast_in_dim.17.bias_ref), custom_call_target="tpu_custom_call" | custom-call | tf_op jit(solution)/shard_map/pallas_call | solution.py:49
  27.9 0.1 add.249
  28.0 0.1 squeeze.20
  28.1 0.1 squeeze.21
  28.1 0.1 squeeze.44
  28.2 0.1 squeeze.45
  28.3 19.8 %collective-permute-done.4 = f32[2,1280]{1,0:T(2,128)S(1)} collective-permute-done((f32[2,1280]{1,0:T(2,128)S(1)}, f32[2,1280]{1,0:T(2,128)S(1)}, u32[]{:S(2)}, u32[]{:S(2)}) %collective-permute-start.4) | collective-permute-done | bytes 10272 | tf_op jit(solution)/shard_map/ppermute | solution.py:107
  48.1 0.0 collective-permute-done.5
  48.1 0.1 slice_reduce_fusion.2
  48.2 0.1 reshape.78
  48.3 0.1 squeeze.46
  48.4 0.1 squeeze.47
  48.5 0.1 squeeze.48
  48.6 0.1 squeeze.49
  48.6 0.1 squeeze.50
  48.7 0.1 squeeze.51
  48.8 0.1 reduce_sum.18
  48.9 0.2 add_reduce_fusion
  49.2 0.1 broadcast_in_dim.18
  49.2 0.7 reshape.79.group_ref
  49.9 3.9 %shard_map.111.refs_1_.normed_ref = bf16[512,1280]{1,0:T(8,128)(2,1)} custom-call(f32[1,4,128,1280]{3,2,1,0:T(8,128)} %features_ref.5, f32[2,1280]{1,0:T(2,128)} %reshape.79.group_ref, f32[1,1280]{1,0:T(1,128)} %copy-done.7, f32[1,1280]{1,0:T(1,128)} %reshape.80.gain_ref, f32[1,1280]{1,0:T(1,128)} %reshape.81.bias_ref), custom_call_target="tpu_custom_call" | custom-call | tf_op jit(solution)/shard_map/pallas_call | solution.py:92
  53.9 1.7 copy-done
  55.6 0.2 collective-permute-start.6
  55.8 1.9 copy-done.1
  57.7 1.3 copy-done.4
  59.0 2.5 %shard_map.114 = bf16[1024,512]{1,0:T(8,128)(2,1)S(1)} custom-call(bf16[512,1280]{1,0:T(8,128)(2,1)S(1)} %copy-done.4, bf16[8,160,1280]{2,1,0:T(8,128)(2,1)S(1)} %copy-done.1), custom_call_target="tpu_custom_call" | custom-call | flops 1258291200 | bytes 4194304 | tf_op jit(solution)/shard_map/pallas_call | solution.py:209
  61.6 0.1 slice.107
  61.7 0.0 collective-permute-done.6.weight_ref.theirs_ref
  61.7 2.6 %shard_map.115 = bf16[1024,512]{1,0:T(8,128)(2,1)S(1)} custom-call(bf16[512,1280]{1,0:T(8,128)(2,1)S(1)} %copy-done.4, bf16[8,160,1280]{2,1,0:T(8,128)(2,1)S(1)} %collective-permute-done.6.weight_ref.theirs_ref), custom_call_target="tpu_custom_call" | custom-call | flops 1258291200 | bytes 4194304 | tf_op jit(solution)/shard_map/pallas_call | solution.py:209
  64.3 0.1 slice.108
  64.3 0.3 maximum_select_fusion
  64.6 25.2 %all_to_all.20.query_ref.refs_0_.refs_1_ = bf16[8,192,512]{2,1,0:T(8,128)(2,1)} all-to-all(bf16[8,192,512]{2,1,0:T(8,128)(2,1)S(1)} %bitcast.19), channel_id=1, replica_groups={{0,16,32,48,64,80,96,112},{8,24,40,56,72,88,104,120},{1,17,33,49,65,81,..., dimensions={0} | all-to-all | bytes 3145728 | tf_op jit(solution)/shard_map/all_to_all | solution.py:140
  89.8 0.6 collective-permute-start.8
  90.4 2.7 %collective-permute-done.8 = bf16[192,512]{1,0:T(8,128)(2,1)S(1)} collective-permute-done((bf16[192,512]{1,0:T(8,128)(2,1)S(1)}, bf16[192,512]{1,0:T(8,128)(2,1)S(1)}, u32[]{:S(2)}, u32[]{:S(2)}) %collective-permute-start.8) | collective-permute-done | bytes 196640 | tf_op jit(solution)/shard_map/ppermute | solution.py:107
  93.1 0.7 pad_maximum_fusion.1.query_ref
  93.8 1.5 broadcast_in_dim.19.refs_0_
  95.3 5.2 %all-to-all-start.3 = ((bf16[8,2,128,512]{3,2,1,0:T(8,128)(2,1)}), bf16[8,2,128,512]{3,2,1,0:T(8,128)(2,1)S(1)}, u32[]{:S(2)}, u32[]{:S(2)}) async-start(bf16[8,2,128,512]{3,2,1,0:T(8,128)(2,1)} %shard_map.117), calls=%async_computation.3 | async-start | bytes 4194304 | tf_op jit(solution)/shard_map/all_to_all | solution.py:140
  100.6 0.0 collective-permute-done.7.refs_1_
  100.6 103.9 %shard_map.116.refs_1_ = bf16[8,64,512]{2,1,0:T(8,128)(2,1)} custom-call(bf16[8,192,512]{2,1,0:T(8,128)(2,1)} %all_to_all.20.query_ref.refs_0_.refs_1_, bf16[8,192,512]{2,1,0:T(8,128)(2,1)} %all_to_all.20.query_ref.refs_0_.refs_1_, bf16[8,192,512]{2,1,0:T(8,128)(2,1)} %collective-permute-done.7.refs_1_), custom_call_target="tpu_custom_call" | custom-call | flops 42949672960 | bytes 8388608 | tf_op jit(solution)/shard_map/pallas_call | solution.py:339
  204.5 0.0 all-to-all-done.3.refs_0_
  204.5 5.7 %all-to-all-start.2 = ((bf16[8,64,512]{2,1,0:T(8,128)(2,1)}), bf16[8,64,512]{2,1,0:T(8,128)(2,1)S(1)}, u32[]{:S(2)}, u32[]{:S(2)}) async-start(bf16[8,64,512]{2,1,0:T(8,128)(2,1)} %shard_map.116.refs_1_), calls=%async_computation.2 | async-start | bytes 1048576 | tf_op jit(solution)/shard_map/all_to_all | solution.py:140
  210.3 27.7 %shard_map.119 = bf16[2,64,512]{2,1,0:T(8,128)(2,1)} custom-call(bf16[2,64,512]{2,1,0:T(8,128)(2,1)} %pad_maximum_fusion.1.query_ref, bf16[8,256,512]{2,1,0:T(8,128)(2,1)} %bitcast.18), custom_call_target="tpu_custom_call" | custom-call | flops 10737418240 | bytes 8388608 | tf_op jit(solution)/shard_map/pallas_call | solution.py:339
  238.0 0.9 slice_bitcast_fusion.1
  238.8 0.1 collective-permute-start.9
  238.9 1.2 collective-permute-done.9.far_ref
  240.2 0.0 all-to-all-done.2.first_ref
  240.2 4.8 %shard_map.120 = f32[1,4,128,1280]{3,2,1,0:T(8,128)} custom-call(s32[1]{0:T(128)} %bitcast.core_ref, f32[1,4,128,1280]{3,2,1,0:T(8,128)S(1)} %copy-done.3, f32[1,1280]{1,0:T(1,128)S(1)} %copy-done.8, bf16[8,64,512]{2,1,0:T(8,128)(2,1)S(1)} %all-to-all-done.2.first_ref, bf16[64,512]{1,0:T(8,128)(2,1)S(1)} %get-tuple-element.17.near_ref, ...), custom_call_target="tpu_custom_call" | custom-call | flops 838860800 | bytes 5242880 | tf_op jit(solution)/shard_map/pallas_call | solution.py:393
  (39 shorter events, 0.2 us)
Async XLA Ops:
  3.1 50.7 %all-to-all-start = ((bf16[8,160,1280]{2,1,0:T(8,128)(2,1)}), bf16[8,160,1280]{2,1,0:T(8,128)(2,1)S(1)}, u32[]{:S(2)}, u32[]{:S(2)}) async-start(bf16[8,160,1280]{2,1,0:T(8,128)(2,1)} %shard_map.112), calls=%async_computation | async-start | bytes 6553600 | tf_op jit(solution)/shard_map/all_to_all | solution.py:421
  11.1 1.7 copy-start.2
  12.8 9.6 %copy-start.10 = (f32[1280]{0:T(1024)S(1)}, f32[1280]{0:T(1024)}, u32[]{:S(2)}) copy-start(f32[1280]{0:T(1024)} %param.15) | copy-start | bytes 15364
  12.8 9.6 %copy-start.11 = (f32[1280]{0:T(1024)S(1)}, f32[1280]{0:T(1024)}, u32[]{:S(2)}) copy-start(f32[1280]{0:T(1024)} %param.16) | copy-start | bytes 15364
  12.8 10.2 %copy-start.12 = (f32[1280]{0:T(1024)S(1)}, f32[1280]{0:T(1024)}, u32[]{:S(2)}) copy-start(f32[1280]{0:T(1024)} %param.17) | copy-start | bytes 15364
  12.8 10.8 %copy-start.6 = (f32[320,1280]{1,0:T(8,128)S(1)}, f32[320,1280]{1,0:T(8,128)}, u32[]{:S(2)}) copy-start(f32[320,1280]{1,0:T(8,128)} %time_ref.1) | copy-start | bytes 4915204
  13.4 5.5 %collective-permute-start = (f32[2,1280]{1,0:T(2,128)S(1)}, f32[2,1280]{1,0:T(2,128)S(1)}, u32[]{:S(2)}, u32[]{:S(2)}) collective-permute-start(f32[2,1280]{1,0:T(2,128)S(1)} %shard_map.110), channel_id=1, source_target_pairs={{0,32},{8,40},{16,48},{24,56},{32,64},{40,72},{48,80},{56,88},{64,... | collective-permute-start | bytes 30728 | tf_op jit(solution)/shard_map/ppermute | solution.py:107
  15.0 5.2 %collective-permute-start.1 = (f32[2,1280]{1,0:T(2,128)S(1)}, f32[2,1280]{1,0:T(2,128)S(1)}, u32[]{:S(2)}, u32[]{:S(2)}) collective-permute-start(f32[2,1280]{1,0:T(2,128)S(1)} %shard_map.110), channel_id=1, source_target_pairs={{0,64},{8,72},{16,80},{24,88},{32,96},{40,104},{48,112},{56,120},{... | collective-permute-start | bytes 30728 | tf_op jit(solution)/shard_map/ppermute | solution.py:107
  16.1 4.1 %collective-permute-start.2 = (f32[2,1280]{1,0:T(2,128)S(1)}, f32[2,1280]{1,0:T(2,128)S(1)}, u32[]{:S(2)}, u32[]{:S(2)}) collective-permute-start(f32[2,1280]{1,0:T(2,128)S(1)} %shard_map.110), channel_id=1, source_target_pairs={{0,96},{8,104},{16,112},{24,120},{32,0},{40,8},{48,16},{56,24},{64... | collective-permute-start | bytes 30728 | tf_op jit(solution)/shard_map/ppermute | solution.py:107
  20.3 8.0 %collective-permute-start.3 = (f32[2,1280]{1,0:T(2,128)S(1)}, f32[2,1280]{1,0:T(2,128)S(1)}, u32[]{:S(2)}, u32[]{:S(2)}) collective-permute-start(f32[2,1280]{1,0:T(2,128)S(1)} %pad_maximum_fusion.2), channel_id=1, source_target_pairs={{0,8},{8,0},{16,24},{24,16},{32,40},{40,32},{48,56},{56,48},{64,72... | collective-permute-start | bytes 30728 | tf_op jit(solution)/shard_map/ppermute | solution.py:107
  20.4 27.7 %collective-permute-start.4 = (f32[2,1280]{1,0:T(2,128)S(1)}, f32[2,1280]{1,0:T(2,128)S(1)}, u32[]{:S(2)}, u32[]{:S(2)}) collective-permute-start(f32[2,1280]{1,0:T(2,128)S(1)} %pad_maximum_fusion.2), channel_id=1, source_target_pairs={{0,16},{8,24},{16,0},{24,8},{32,48},{40,56},{48,32},{56,40},{64,80... | collective-permute-start | bytes 30728 | tf_op jit(solution)/shard_map/ppermute | solution.py:107
  21.2 26.9 %collective-permute-start.5 = (f32[2,1280]{1,0:T(2,128)S(1)}, f32[2,1280]{1,0:T(2,128)S(1)}, u32[]{:S(2)}, u32[]{:S(2)}) collective-permute-start(f32[2,1280]{1,0:T(2,128)S(1)} %pad_maximum_fusion.2), channel_id=1, source_target_pairs={{0,24},{8,16},{16,8},{24,0},{32,56},{40,48},{48,40},{56,32},{64,88... | collective-permute-start | bytes 30728 | tf_op jit(solution)/shard_map/ppermute | solution.py:107
  27.9 22.0 %copy-start.7 = (f32[1,1280]{1,0:T(1,128)}, f32[1,1280]{1,0:T(1,128)S(1)}, u32[]{:S(2)}) copy-start(f32[1,1280]{1,0:T(1,128)S(1)} %shard_map.109.shift_ref) | copy-start | bytes 15364
  53.9 1.7 copy-start
  55.6 6.1 %collective-permute-start.6 = (bf16[8,160,1280]{2,1,0:T(8,128)(2,1)}, bf16[8,160,1280]{2,1,0:T(8,128)(2,1)S(1)}, u32[]{:S(2)}, u32[]{:S(2)}) collective-permute-start(bf16[8,160,1280]{2,1,0:T(8,128)(2,1)} %shard_map.113.weight_ref.mine_ref), channel_id=1, source_target_pairs={{0,8},{8,0},{16,24},{24,16},{32,40},{40,32},{48,56},{56,48},{64,72... | collective-permute-start | bytes 9830408 | tf_op jit(solution)/shard_map/ppermute | solution.py:107
  55.8 1.9 copy-start.1
  57.7 1.3 copy-start.4
  61.7 2.6 %copy-start.5 = (bf16[8,160,1280]{2,1,0:T(8,128)(2,1)}, bf16[8,160,1280]{2,1,0:T(8,128)(2,1)S(1)}, u32[]{:S(2)}) copy-start(bf16[8,160,1280]{2,1,0:T(8,128)(2,1)S(1)} %collective-permute-done.6.weight_ref.theirs_ref) | copy-start | bytes 9830404
  89.8 10.8 %collective-permute-start.7 = (bf16[8,192,512]{2,1,0:T(8,128)(2,1)}, bf16[8,192,512]{2,1,0:T(8,128)(2,1)}, u32[]{:S(2)}, u32[]{:S(2)}) collective-permute-start(bf16[8,192,512]{2,1,0:T(8,128)(2,1)} %all_to_all.20.query_ref.refs_0_.refs_1_), channel_id=1, source_target_pairs={{0,8},{8,0},{16,24},{24,16},{32,40},{40,32},{48,56},{56,48},{64,72... | collective-permute-start | bytes 4718600 | tf_op jit(solution)/shard_map/ppermute | solution.py:107
  89.8 3.3 %collective-permute-start.8 = (bf16[192,512]{1,0:T(8,128)(2,1)S(1)}, bf16[192,512]{1,0:T(8,128)(2,1)S(1)}, u32[]{:S(2)}, u32[]{:S(2)}) collective-permute-start(bf16[192,512]{1,0:T(8,128)(2,1)S(1)} %slice.110), channel_id=1, source_target_pairs={{0,8},{8,0},{16,24},{24,16},{32,40},{40,32},{48,56},{56,48},{64,72... | collective-permute-start | bytes 589832 | tf_op jit(solution)/shard_map/ppermute | solution.py:107
  95.3 109.2 %all-to-all-start.3 = ((bf16[8,2,128,512]{3,2,1,0:T(8,128)(2,1)}), bf16[8,2,128,512]{3,2,1,0:T(8,128)(2,1)S(1)}, u32[]{:S(2)}, u32[]{:S(2)}) async-start(bf16[8,2,128,512]{3,2,1,0:T(8,128)(2,1)} %shard_map.117), calls=%async_computation.3 | async-start | bytes 4194304 | tf_op jit(solution)/shard_map/all_to_all | solution.py:140
  204.5 5.7 %copy-start.9 = (bf16[8,2,128,512]{3,2,1,0:T(8,128)(2,1)}, bf16[8,2,128,512]{3,2,1,0:T(8,128)(2,1)S(1)}, u32[]{:S(2)}) copy-start(bf16[8,2,128,512]{3,2,1,0:T(8,128)(2,1)S(1)} %all-to-all-done.3.refs_0_) | copy-start | bytes 6291460
  204.5 35.6 %all-to-all-start.2 = ((bf16[8,64,512]{2,1,0:T(8,128)(2,1)}), bf16[8,64,512]{2,1,0:T(8,128)(2,1)S(1)}, u32[]{:S(2)}, u32[]{:S(2)}) async-start(bf16[8,64,512]{2,1,0:T(8,128)(2,1)} %shard_map.116.refs_1_), calls=%async_computation.2 | async-start | bytes 1048576 | tf_op jit(solution)/shard_map/all_to_all | solution.py:140
  210.3 29.9 %copy-start.3 = (f32[1,4,128,1280]{3,2,1,0:T(8,128)S(1)}, f32[1,4,128,1280]{3,2,1,0:T(8,128)}, u32[]{:S(2)}) copy-start(f32[1,4,128,1280]{3,2,1,0:T(8,128)} %features_ref.5) | copy-start | bytes 7864324
  210.3 29.9 %copy-start.8 = (f32[1,1280]{1,0:T(1,128)S(1)}, f32[1,1280]{1,0:T(1,128)}, u32[]{:S(2)}) copy-start(f32[1,1280]{1,0:T(1,128)} %copy-done.7) | copy-start | bytes 15364
  238.8 1.3 collective-permute-start.9

commit v5 on v4

--- a/solution.py
+++ b/solution.py
@@ -58,7 +58,7 @@
         out_specs=pl.BlockSpec((1, channels), lambda i: (0, 0)),
         out_shape=jax.ShapeDtypeStruct((1, channels), F32),
         scratch_shapes=[pltpu.VMEM((w_emb.shape[0], 8), F32), pltpu.VMEM((8, channels), F32)],
-        compiler_params=pltpu.CompilerParams(vmem_limit_bytes=48 * 2**20),
+        compiler_params=pltpu.CompilerParams(vmem_limit_bytes=20 * 2**20),
         cost_estimate=NO_COST,
     )(table, w_time, w_emb, b_emb[None, :])
 
@@ -75,15 +75,16 @@
     return pl.pallas_call(
         spread_kernel,
         out_shape=jax.ShapeDtypeStruct((2, features.shape[3]), F32),
-        compiler_params=pltpu.CompilerParams(vmem_limit_bytes=48 * 2**20),
+        compiler_params=pltpu.CompilerParams(vmem_limit_bytes=12 * 2**20),
         cost_estimate=NO_COST,
     )(features)
 
 
-def normalise_kernel(features_ref, group_ref, shift_ref, gain_ref, bias_ref, out_ref):
+def normalise_kernel(features_ref, group_ref, shift_ref, gain_ref, bias_ref, out_ref, token_ref):
     lifted = features_ref[0, 0] + shift_ref[...]
     value = (lifted - group_ref[0:1, :]) * (1.0 / group_ref[1:2, :])
     out_ref[...] = (value * gain_ref[...] + bias_ref[...]).astype(BF16)
+    token_ref[...] = jnp.broadcast_to(value[:8, :128], token_ref.shape)
 
 
 def normalise(features, group, *rows):
@@ -97,8 +98,15 @@
             pl.BlockSpec(group.shape, lambda i: (0, 0)),
         ]
         + [row] * len(rows),
-        out_specs=pl.BlockSpec((cols_here, channels), lambda i: (i, 0)),
-        out_shape=jax.ShapeDtypeStruct((rows_here * cols_here, channels), BF16),
+        out_specs=(
+            pl.BlockSpec((cols_here, channels), lambda i: (i, 0)),
+            pl.BlockSpec((8, 128), lambda i: (0, 0)),
+        ),
+        out_shape=(
+            jax.ShapeDtypeStruct((rows_here * cols_here, channels), BF16),
+            jax.ShapeDtypeStruct((8, 128), F32),
+        ),
+        compiler_params=pltpu.CompilerParams(vmem_limit_bytes=8 * 2**20),
         cost_estimate=NO_COST,
     )(features, group, *[value.reshape(1, channels) for value in rows])
 
@@ -119,7 +127,7 @@
     return lambda c: ((c // 2 + step) % 4) * 2 + c % 2
 
 
-def after(value, *others):
+def after(value, *others, vmem=None):
     anywhere = pl.BlockSpec(memory_space=pl.ANY)
     return pl.pallas_call(
         lambda *refs: None,
@@ -127,6 +135,7 @@
         out_specs=anywhere,
         out_shape=jax.ShapeDtypeStruct(value.shape, value.dtype),
         input_output_aliases={0: 0},
+        compiler_params=pltpu.CompilerParams(vmem_limit_bytes=vmem),
         cost_estimate=pl.CostEstimate(flops=0, bytes_accessed=0, transcendentals=0),
     )(value, *others)
 
@@ -195,33 +204,44 @@
     return jnp.where(core == 0, jnp.stack([mine, theirs]), jnp.stack([theirs, mine]))
 
 
-def project_kernel(normed_ref, weight_ref, out_ref):
+def project_kernel(normed_ref, weight_ref, out_ref, last_ref):
     weight = weight_ref[...].reshape(normed_ref.shape[1], weight_ref.shape[2])
-    out_ref[...] = product(normed_ref[...], weight).T.astype(BF16)
+    out = product(normed_ref[...], weight).T.astype(BF16)
+    out_ref[...] = out
+
+    @pl.when(pl.program_id(0) == pl.num_programs(0) - 1)
+    def _():
+        last_ref[...] = out[-last_ref.shape[0] :]
 
 
 def project(normed, weight):
     pixels, channels = normed.shape
     size, depth, width = weight.shape
     rows = HEADS // 2 * 3 * HEAD
+    last = 3 * HEAD
     lanes = 256
     skip = (width - rows) // lanes
-    out = pl.pallas_call(
+    out, last_out = pl.pallas_call(
         project_kernel,
         grid=(width // lanes - skip,),
         in_specs=[
             pl.BlockSpec((pixels, channels), lambda i: (0, 0)),
             pl.BlockSpec((size, depth, lanes), lambda i: (0, 0, i + skip)),
         ],
-        out_specs=pl.BlockSpec((lanes, pixels), lambda i: (i, 0)),
-        out_shape=jax.ShapeDtypeStruct((width - skip * lanes, pixels), BF16),
-        compiler_params=pltpu.CompilerParams(vmem_limit_bytes=48 * 2**20),
+        out_specs=(
+            pl.BlockSpec((lanes, pixels), lambda i: (i, 0)),
+            pl.BlockSpec((last, pixels), lambda i: (0, 0)),
+        ),
+        out_shape=(
+            jax.ShapeDtypeStruct((width - skip * lanes, pixels), BF16),
+            jax.ShapeDtypeStruct((last, pixels), BF16),
+        ),
+        compiler_params=pltpu.CompilerParams(vmem_limit_bytes=16 * 2**20),
         cost_estimate=pl.CostEstimate(
             flops=2 * normed.size * rows, bytes_accessed=2**22, transcendentals=0
         ),
     )(normed, weight)
-    out = out[-rows:]
-    return out[: -3 * HEAD].reshape(HEADS // 2 - 1, 3 * HEAD, pixels), out[-3 * HEAD :]
+    return out[-rows:-last].reshape(HEADS // 2 - 1, last, pixels), last_out
 
 
 def split3(value):
@@ -280,7 +300,7 @@
         accum_ref[...] = accum
 
     query[3 * HEAD :, :] = jnp.zeros((HEAD, width), BF16)
-    run(jnp.max(scores(0, 256), axis=0, keepdims=True), chunk)
+    run(jnp.max(scores(0, 128), axis=0, keepdims=True), chunk)
     small = jnp.max(jnp.where(total_ref[...] < 1e30, 0.0, 1.0))
 
     @pl.when(small > 0.5)
@@ -312,8 +332,9 @@
     )
 
 
-def attend_kernel(stride, query_ref, *refs):
-    sources, (out_ref, query, keys, vals, total, accum) = refs[:-6], refs[-6:]
+def attend_kernel(stride, split, query_low, query_high, *refs):
+    ends = 7 if split else 6
+    sources, outs, (query, keys, vals, total, accum) = refs[:-ends], refs[-ends:-5], refs[-5:]
     chips, rows, pixels = sources[0].shape
 
     @pl.when(pl.program_id(0) == 0)
@@ -326,27 +347,44 @@
                     put_keys(keys, vals, place, key, value)
                     place += pixels
 
-    query_t = jnp.concatenate([query_ref[0], query_ref[1]], axis=1)
-    attended = attend_rows(query, keys, vals, total, accum, query_t, 8192)
+    if split:
+        query_t = jnp.concatenate([query_low[:HEAD], query_high[:HEAD]], axis=1)
+    else:
+        query_t = jnp.concatenate([query_low[0], query_high[0]], axis=1)
+    attended = attend_rows(query, keys, vals, total, accum, query_t, keys.shape[0])
     for at in range(2):
-        out_ref[at] = attended[:, at * pixels : (at + 1) * pixels]
-
-
-def attend(queries, mine, theirs, stride):
+        value = attended[:, at * pixels : (at + 1) * pixels]
+        if split:
+            outs[at][...] = value
+        else:
+            outs[0][at] = value
+
+
+def attend(low, high, mine, theirs, stride):
     sources = [mine] if theirs is None else [mine, theirs]
-    blocks, unused, pixels = queries.shape
+    split = low.ndim == 2
+    pixels = low.shape[-1]
     count = sum(source.shape[0] * source.shape[1] // stride * pixels for source in sources)
-    return pl.pallas_call(
-        functools.partial(attend_kernel, stride),
+    if split:
+        blocks = 2
+        queries = [pl.BlockSpec((HEAD, pixels), lambda i: (0, 0))] * 2
+        out_specs = [pl.BlockSpec((HEAD, pixels), lambda i: (0, 0))] * 2
+        out_shape = [jax.ShapeDtypeStruct((HEAD, pixels), BF16)] * 2
+    else:
+        blocks = low.shape[0]
+        queries = [pl.BlockSpec((1, HEAD, pixels), lambda i, at=at: (2 * i + at, 0, 0)) for at in range(2)]
+        out_specs = pl.BlockSpec((2, HEAD, pixels), lambda i: (i, 0, 0))
+        out_shape = jax.ShapeDtypeStruct((blocks, HEAD, pixels), BF16)
+    return pl.pallas_call(
+        functools.partial(attend_kernel, stride, split),
         grid=(blocks // 2,),
-        in_specs=[pl.BlockSpec((2, HEAD, pixels), lambda i: (i, 0, 0))]
-        + [pl.BlockSpec(source.shape, lambda i: (0, 0, 0)) for source in sources],
-        out_specs=pl.BlockSpec((2, HEAD, pixels), lambda i: (i, 0, 0)),
-        out_shape=jax.ShapeDtypeStruct((blocks, HEAD, pixels), BF16),
+        in_specs=queries + [pl.BlockSpec(source.shape, lambda i: (0, 0, 0)) for source in sources],
+        out_specs=out_specs,
+        out_shape=out_shape,
         scratch_shapes=attention_scratch(count, 2 * pixels),
         compiler_params=pltpu.CompilerParams(vmem_limit_bytes=56 * 2**20),
         cost_estimate=cost(blocks * pixels, count),
-    )(queries, *sources)
+    )(low, high, *sources)
 
 
 def add_attended_kernel(
@@ -429,9 +467,9 @@
     var = spread / (count * per_group)
 
     group = jnp.repeat(jnp.stack([mean, jnp.sqrt(var + 1e-06)]), per_group, axis=1)
-    normed = normalise(features, group, shift, gn_gain, gn_bias)
-
-    mine = after(mine, normed)
+    normed, done = normalise(features, group, shift, gn_gain, gn_bias)
+
+    mine = after(mine, done, vmem=2**20)
     theirs = other_core(mine)
     out_weights = (mine, theirs)
     first_mine, last_mine = project(normed, mine)
@@ -439,15 +477,16 @@
     first = CHIPS * HEAD
     by_head = by_core(first_mine, first_theirs).reshape(CHIPS, 3 * HEAD, pixels)
     mine = across_chips(by_head)
-    rest = jnp.stack([last_mine, other_core(last_theirs)])
-    pairs = jnp.broadcast_to(rest[None, :, HEAD:], (CHIPS, 2, 2 * HEAD, pixels))
+    last_theirs = other_core(last_theirs)
+    pairs = jnp.concatenate([last_mine[HEAD:], last_theirs[HEAD:]], axis=0)
+    pairs = jnp.broadcast_to(pairs[None], (CHIPS,) + pairs.shape)
     theirs = other_core(mine)
     pairs = across_chips(after(pairs, mine))
 
-    attended = attend(mine, mine, theirs, 3 * HEAD)
+    attended = attend(mine, mine, mine, theirs, 3 * HEAD)
     pairs = after(pairs, attended)
     attended = across_chips(attended)
-    near, far = attend(rest[:, :HEAD], pairs.reshape(CHIPS, 4 * HEAD, pixels), None, 2 * HEAD)
+    near, far = attend(last_mine, last_theirs, pairs, None, 2 * HEAD)
     core = (lax.axis_index("row") % 2).astype(jnp.int32).reshape(1)
     return add_attended(core, features, shift, attended, near, other_core(far), *out_weights)
 

time: 246 us -> 244 us (level)
  Pallas kernels: 153 us -> 148 us
  waiting for transfers between devices: 24.9 us -> 27.4 us
    unnamed x26 -> x30, local copies, waits for them, and re-layouts: 6.73 us -> 10.5 us
    pallas_call x1, Pallas kernels: 3.94 us -> 0.55 us  [normalise(): pl.pallas_call(normalise_kernel, grid=(rows_here,), in_specs=[pl.BlockSpe...]
    pallas_call x1, Pallas kernels: 4.21 us -> 1.18 us  [time_shift(): pl.pallas_call(time_shift_kernel, grid=(steps,), in_specs=[pl.BlockSpec(t...]
    ppermute x10, waiting for transfers between devices: 24.9 us -> 27.4 us  [move_row(): return lax.ppermute(value, 'row', [(r, target(r)) for r in range(16)])]
  transfers between devices with their start and end apart: 13 -> 13, of which waited for: 4 -> 5; matrix products, arithmetic and copies ran while one was open for 3% -> 1% of each run, Pallas kernels for 58% -> 56%
where the time goes in v5:
time: 244 us; the launch traced here: 242 us
  Pallas kernels  148 us (61%)
  waiting for transfers between devices  27.4 us (11%)
  starting transfers between devices  26.2 us (11%)
  blocking collectives  25.2 us (10%)
  local copies, waits for them, and re-layouts  13.4 us (5%)
    pallas_call x2, Pallas kernels, attend(): pl.pallas_call(functools.partial(attend_kernel, stride, split), grid=(blo...  131 us
    ppermute x10, waiting for transfers between devices, move_row(): return lax.ppermute(value, 'row', [(r, target(r)) for r in range(16)])  27.4 us
    all_to_all x1, blocking collectives, across_chips(): lax.all_to_all(value, 'row', 0, 0, tiled=True, axis_index_groups=groups)  25.2 us
    all_to_all x2, starting transfers between devices, across_chips(): lax.all_to_all(value, 'row', 0, 0, tiled=True, axis_index_groups=groups)  10.7 us
    unnamed x30, local copies, waits for them, and re-layouts  10.5 us
    all_to_all x1, starting transfers between devices, local(): mine = lax.all_to_all(mine, 'col', 0, 0, tiled=True)  7.96 us
    ppermute x10, starting transfers between devices, move_row(): return lax.ppermute(value, 'row', [(r, target(r)) for r in range(16)])  7.51 us
    pallas_call x2, Pallas kernels, project(): pl.pallas_call(project_kernel, grid=(width // lanes - skip,), in_specs=[p...  6.55 us
  transfers between devices with their start and end apart: 13, of which 5 were waited for; matrix products, arithmetic and copies ran while one was open for 1% of the time, Pallas kernels for 56%

profile of v5, /device:TPU:2, one launch (start us, length us, event | category | flops | bytes accessed | tf_op | source)
XLA Modules:
  0.0 242.3 jit_solution(18361579114467921032)
XLA Ops:
  0.0 3.1 %shard_map.112 = bf16[8,160,1280]{2,1,0:T(8,128)(2,1)} custom-call(s32[1]{0:T(128)} %bitcast.core_ref, bf16[160,640]{1,0:T(8,128)(2,1)} %query_ref.1, bf16[160,640]{1,0:T(8,128)(2,1)} %key_ref.1, bf16[160,640]{1,0:T(8,128)(2,1)} %value_ref.1, bf16[160,640]{1,0:T(8,128)(2,1)} %bitcast.13), custom_call_target="tpu_custom_call" | custom-call | tf_op jit(solution)/shard_map/pallas_call | solution.py:192
  3.1 8.0 %all-to-all-start = ((bf16[8,160,1280]{2,1,0:T(8,128)(2,1)}), bf16[8,160,1280]{2,1,0:T(8,128)(2,1)S(1)}, u32[]{:S(2)}, u32[]{:S(2)}) async-start(bf16[8,160,1280]{2,1,0:T(8,128)(2,1)} %shard_map.112), calls=%async_computation | async-start | bytes 6553600 | tf_op jit(solution)/shard_map/all_to_all | solution.py:459
  11.1 1.7 copy-done.1
  12.8 0.6 shard_map.110
  13.4 1.6 collective-permute-start
  15.0 1.1 collective-permute-start.1
  16.1 2.2 collective-permute-start.2
  19.0 0.0 collective-permute-done
  19.0 1.2 collective-permute-done.1
  20.2 0.1 fusion.3
  20.3 0.1 collective-permute-start.3
  20.4 0.8 collective-permute-start.4
  21.2 1.1 collective-permute-start.5
  22.3 0.1 pad_maximum_fusion.2
  22.3 0.1 broadcast_in_dim.20.table_ref
  22.5 0.0 copy-start.4
  22.5 2.9 %copy-done.4 = f32[1280,1280]{1,0:T(8,128)S(1)} copy-done((f32[1280,1280]{1,0:T(8,128)S(1)}, f32[1280,1280]{1,0:T(8,128)}, u32[]{:S(2)}) %copy-start.4) | copy-done | bytes 6553624
  25.4 1.2 shard_map.109.shift_ref
  26.6 0.1 add.249
  26.7 0.1 squeeze.20
  26.8 0.1 squeeze.21
  26.8 0.1 squeeze.44
  26.9 0.1 squeeze.45
  27.0 0.0 collective-permute-done.3
  27.0 21.1 %collective-permute-done.4 = f32[2,1280]{1,0:T(2,128)S(1)} collective-permute-done((f32[2,1280]{1,0:T(2,128)S(1)}, f32[2,1280]{1,0:T(2,128)S(1)}, u32[]{:S(2)}, u32[]{:S(2)}) %collective-permute-start.4) | collective-permute-done | bytes 10272 | tf_op jit(solution)/shard_map/ppermute | solution.py:115
  48.1 0.0 collective-permute-done.5
  48.1 0.1 slice_reduce_fusion.2
  48.2 0.1 reshape.75
  48.3 0.1 squeeze.46
  48.4 0.1 squeeze.47
  48.5 0.1 squeeze.48
  48.6 0.1 squeeze.49
  48.6 0.1 squeeze.50
  48.7 0.1 squeeze.51
  48.8 0.1 reduce_sum.18
  48.9 0.2 add_reduce_fusion
  49.2 0.1 broadcast_in_dim.18
  49.2 0.1 reshape.76.group_ref
  49.3 0.0 copy-start.2
  49.3 1.7 copy-done.2
  51.1 0.6 shard_map.111
  51.6 0.0 copy-start.8
  51.6 1.0 copy-done.8
  52.7 0.2 collective-permute-start.6
  52.9 2.3 copy-done.9
  55.2 2.6 %shard_map.114 = (bf16[1024,512]{1,0:T(8,128)(2,1)S(1)}, bf16[192,512]{1,0:T(8,128)(2,1)S(1)}) custom-call(bf16[512,1280]{1,0:T(8,128)(2,1)S(1)} %copy-done.9, bf16[8,160,1280]{2,1,0:T(8,128)(2,1)S(1)} %shard_map.113.weight_ref.mine_ref), custom_call_target="tpu_custom_call" | custom-call | flops 1258291200 | bytes 4194304 | tf_op jit(solution)/shard_map/pallas_call | solution.py:224
  57.8 0.1 slice.75
  57.8 0.8 collective-permute-done.6.weight_ref.theirs_ref
  58.7 4.0 %shard_map.115 = (bf16[1024,512]{1,0:T(8,128)(2,1)S(1)}, bf16[192,512]{1,0:T(8,128)(2,1)S(1)}) custom-call(bf16[512,1280]{1,0:T(8,128)(2,1)S(1)} %copy-done.9, bf16[8,160,1280]{2,1,0:T(8,128)(2,1)} %collective-permute-done.6.weight_ref.theirs_ref), custom_call_target="tpu_custom_call" | custom-call | flops 1258291200 | bytes 4194304 | tf_op jit(solution)/shard_map/pallas_call | solution.py:224
  62.7 0.1 slice.76
  62.7 0.3 maximum_select_fusion
  63.0 25.2 %all_to_all.20.query_low.query_high.refs_0_.refs_1_ = bf16[8,192,512]{2,1,0:T(8,128)(2,1)} all-to-all(bf16[8,192,512]{2,1,0:T(8,128)(2,1)S(1)} %bitcast.10), channel_id=1, replica_groups={{0,16,32,48,64,80,96,112},{8,24,40,56,72,88,104,120},{1,17,33,49,65,81,..., dimensions={0} | all-to-all | bytes 3145728 | tf_op jit(solution)/shard_map/all_to_all | solution.py:149
  88.2 0.0 collective-permute-start.7
  88.2 0.5 collective-permute-start.8
  88.7 2.8 %collective-permute-done.8.query_high = bf16[192,512]{1,0:T(8,128)(2,1)S(1)} collective-permute-done((bf16[192,512]{1,0:T(8,128)(2,1)S(1)}, bf16[192,512]{1,0:T(8,128)(2,1)S(1)}, u32[]{:S(2)}, u32[]{:S(2)}) %collective-permute-start.8) | collective-permute-done | bytes 196640 | tf_op jit(solution)/shard_map/ppermute | solution.py:115
  91.5 1.5 broadcast_in_dim.19.refs_0_
  93.0 5.2 %all-to-all-start.3 = ((bf16[8,256,512]{2,1,0:T(8,128)(2,1)}), bf16[8,256,512]{2,1,0:T(8,128)(2,1)S(1)}, u32[]{:S(2)}, u32[]{:S(2)}) async-start(bf16[8,256,512]{2,1,0:T(8,128)(2,1)} %shard_map.117), calls=%async_computation.3 | async-start | bytes 4194304 | tf_op jit(solution)/shard_map/all_to_all | solution.py:149
  98.3 0.0 collective-permute-done.7.refs_1_
  98.3 103.8 %shard_map.116.refs_1_ = bf16[8,64,512]{2,1,0:T(8,128)(2,1)} custom-call(bf16[8,192,512]{2,1,0:T(8,128)(2,1)} %all_to_all.20.query_low.query_high.refs_0_.refs_1_, bf16[8,192,512]{2,1,0:T(8,128)(2,1)} %all_to_all.20.query_low.query_high.refs_0_.refs_1_, bf16[8,192,512]{2,1,0:T(8,128)(2,1)} %all_to_all.20.query_low.query_high.refs_0_.refs_1_, ...), custom_call_target="tpu_custom_call" | custom-call | flops 42949672960 | bytes 8388608 | tf_op jit(solution)/shard_map/pallas_call | solution.py:378
  202.1 5.5 %all-to-all-start.2 = ((bf16[8,64,512]{2,1,0:T(8,128)(2,1)}), bf16[8,64,512]{2,1,0:T(8,128)(2,1)S(1)}, u32[]{:S(2)}, u32[]{:S(2)}) async-start(bf16[8,64,512]{2,1,0:T(8,128)(2,1)} %shard_map.116.refs_1_), calls=%async_computation.2 | async-start | bytes 1048576 | tf_op jit(solution)/shard_map/all_to_all | solution.py:149
  207.6 27.6 %shard_map.119 = (bf16[64,512]{1,0:T(8,128)(2,1)}, bf16[64,512]{1,0:T(8,128)(2,1)}) custom-call(bf16[192,512]{1,0:T(8,128)(2,1)} %copy-done.6, bf16[192,512]{1,0:T(8,128)(2,1)} %copy-done.11, bf16[8,256,512]{2,1,0:T(8,128)(2,1)} %shard_map.118.refs_0_), custom_call_target="tpu_custom_call" | custom-call | flops 10737418240 | bytes 8388608 | tf_op jit(solution)/shard_map/pallas_call | solution.py:378
  235.2 1.5 collective-permute-done.9.far_ref
  236.7 0.8 copy-done.7
  237.5 4.8 %shard_map.120 = f32[1,4,128,1280]{3,2,1,0:T(8,128)} custom-call(s32[1]{0:T(128)} %bitcast.core_ref, f32[1,4,128,1280]{3,2,1,0:T(8,128)S(1)} %copy-done.3, f32[1,1280]{1,0:T(1,128)S(1)} %shard_map.109.shift_ref, bf16[8,64,512]{2,1,0:T(8,128)(2,1)S(1)} %all-to-all-done.2.first_ref, bf16[64,512]{1,0:T(8,128)(2,1)S(1)} %copy-done.7, ...), custom_call_target="tpu_custom_call" | custom-call | flops 838860800 | bytes 5242880 | tf_op jit(solution)/shard_map/pallas_call | solution.py:431
  (41 shorter events, 0.2 us)
Async XLA Ops:
  3.1 49.6 %all-to-all-start = ((bf16[8,160,1280]{2,1,0:T(8,128)(2,1)}), bf16[8,160,1280]{2,1,0:T(8,128)(2,1)S(1)}, u32[]{:S(2)}, u32[]{:S(2)}) async-start(bf16[8,160,1280]{2,1,0:T(8,128)(2,1)} %shard_map.112), calls=%async_computation | async-start | bytes 6553600 | tf_op jit(solution)/shard_map/all_to_all | solution.py:459
  11.1 1.7 copy-start.1
  12.8 9.6 %copy-start.12 = (f32[1280]{0:T(1024)S(1)}, f32[1280]{0:T(1024)}, u32[]{:S(2)}) copy-start(f32[1280]{0:T(1024)} %param.15) | copy-start | bytes 15364
  12.8 9.6 %copy-start.13 = (f32[1280]{0:T(1024)S(1)}, f32[1280]{0:T(1024)}, u32[]{:S(2)}) copy-start(f32[1280]{0:T(1024)} %param.16) | copy-start | bytes 15364
  12.8 9.7 %copy-start.14 = (f32[1280]{0:T(1024)S(1)}, f32[1280]{0:T(1024)}, u32[]{:S(2)}) copy-start(f32[1280]{0:T(1024)} %param.17) | copy-start | bytes 15364
  12.8 9.7 %copy-start.5 = (f32[320,1280]{1,0:T(8,128)S(1)}, f32[320,1280]{1,0:T(8,128)}, u32[]{:S(2)}) copy-start(f32[320,1280]{1,0:T(8,128)} %time_ref.1) | copy-start | bytes 4915204
  13.4 5.5 %collective-permute-start = (f32[2,1280]{1,0:T(2,128)S(1)}, f32[2,1280]{1,0:T(2,128)S(1)}, u32[]{:S(2)}, u32[]{:S(2)}) collective-permute-start(f32[2,1280]{1,0:T(2,128)S(1)} %shard_map.110), channel_id=1, source_target_pairs={{0,32},{8,40},{16,48},{24,56},{32,64},{40,72},{48,80},{56,88},{64,... | collective-permute-start | bytes 30728 | tf_op jit(solution)/shard_map/ppermute | solution.py:115
  15.0 5.2 %collective-permute-start.1 = (f32[2,1280]{1,0:T(2,128)S(1)}, f32[2,1280]{1,0:T(2,128)S(1)}, u32[]{:S(2)}, u32[]{:S(2)}) collective-permute-start(f32[2,1280]{1,0:T(2,128)S(1)} %shard_map.110), channel_id=1, source_target_pairs={{0,64},{8,72},{16,80},{24,88},{32,96},{40,104},{48,112},{56,120},{... | collective-permute-start | bytes 30728 | tf_op jit(solution)/shard_map/ppermute | solution.py:115
  16.1 4.1 %collective-permute-start.2 = (f32[2,1280]{1,0:T(2,128)S(1)}, f32[2,1280]{1,0:T(2,128)S(1)}, u32[]{:S(2)}, u32[]{:S(2)}) collective-permute-start(f32[2,1280]{1,0:T(2,128)S(1)} %shard_map.110), channel_id=1, source_target_pairs={{0,96},{8,104},{16,112},{24,120},{32,0},{40,8},{48,16},{56,24},{64... | collective-permute-start | bytes 30728 | tf_op jit(solution)/shard_map/ppermute | solution.py:115
  20.3 6.7 %collective-permute-start.3 = (f32[2,1280]{1,0:T(2,128)S(1)}, f32[2,1280]{1,0:T(2,128)S(1)}, u32[]{:S(2)}, u32[]{:S(2)}) collective-permute-start(f32[2,1280]{1,0:T(2,128)S(1)} %pad_maximum_fusion.1), channel_id=1, source_target_pairs={{0,8},{8,0},{16,24},{24,16},{32,40},{40,32},{48,56},{56,48},{64,72... | collective-permute-start | bytes 30728 | tf_op jit(solution)/shard_map/ppermute | solution.py:115
  20.4 27.7 %collective-permute-start.4 = (f32[2,1280]{1,0:T(2,128)S(1)}, f32[2,1280]{1,0:T(2,128)S(1)}, u32[]{:S(2)}, u32[]{:S(2)}) collective-permute-start(f32[2,1280]{1,0:T(2,128)S(1)} %pad_maximum_fusion.1), channel_id=1, source_target_pairs={{0,16},{8,24},{16,0},{24,8},{32,48},{40,56},{48,32},{56,40},{64,80... | collective-permute-start | bytes 30728 | tf_op jit(solution)/shard_map/ppermute | solution.py:115
  21.2 26.9 %collective-permute-start.5 = (f32[2,1280]{1,0:T(2,128)S(1)}, f32[2,1280]{1,0:T(2,128)S(1)}, u32[]{:S(2)}, u32[]{:S(2)}) collective-permute-start(f32[2,1280]{1,0:T(2,128)S(1)} %pad_maximum_fusion.1), channel_id=1, source_target_pairs={{0,24},{8,16},{16,8},{24,0},{32,56},{40,48},{48,40},{56,32},{64,88... | collective-permute-start | bytes 30728 | tf_op jit(solution)/shard_map/ppermute | solution.py:115
  22.5 2.9 %copy-start.4 = (f32[1280,1280]{1,0:T(8,128)S(1)}, f32[1280,1280]{1,0:T(8,128)}, u32[]{:S(2)}) copy-start(f32[1280,1280]{1,0:T(8,128)} %emb_ref.1) | copy-start | bytes 19660804
  49.3 1.7 copy-start.2
  51.6 1.1 copy-start.8
  52.7 5.1 %copy-start = (bf16[8,160,1280]{2,1,0:T(8,128)(2,1)}, bf16[8,160,1280]{2,1,0:T(8,128)(2,1)S(1)}, u32[]{:S(2)}) copy-start(bf16[8,160,1280]{2,1,0:T(8,128)(2,1)S(1)} %shard_map.113.weight_ref.mine_ref) | copy-start | bytes 9830404
  52.7 6.0 %collective-permute-start.6 = (bf16[8,160,1280]{2,1,0:T(8,128)(2,1)S(1)}, bf16[8,160,1280]{2,1,0:T(8,128)(2,1)}, u32[]{:S(2)}, u32[]{:S(2)}) collective-permute-start(bf16[8,160,1280]{2,1,0:T(8,128)(2,1)S(1)} %shard_map.113.weight_ref.mine_ref), channel_id=1, source_target_pairs={{0,8},{8,0},{16,24},{24,16},{32,40},{40,32},{48,56},{56,48},{64,72... | collective-permute-start | bytes 9830408 | tf_op jit(solution)/shard_map/ppermute | solution.py:115
  52.9 2.3 copy-start.9
  57.8 30.9 %copy-start.6 = (bf16[192,512]{1,0:T(8,128)(2,1)}, bf16[192,512]{1,0:T(8,128)(2,1)S(1)}, u32[]{:S(2)}) copy-start(bf16[192,512]{1,0:T(8,128)(2,1)S(1)} %get-tuple-element.17.query_low) | copy-start | bytes 589828
  88.2 10.1 %collective-permute-start.7 = (bf16[8,192,512]{2,1,0:T(8,128)(2,1)}, bf16[8,192,512]{2,1,0:T(8,128)(2,1)}, u32[]{:S(2)}, u32[]{:S(2)}) collective-permute-start(bf16[8,192,512]{2,1,0:T(8,128)(2,1)} %all_to_all.20.query_low.query_high.refs_0_.refs_1_), channel_id=1, source_target_pairs={{0,8},{8,0},{16,24},{24,16},{32,40},{40,32},{48,56},{56,48},{64,72... | collective-permute-start | bytes 4718600 | tf_op jit(solution)/shard_map/ppermute | solution.py:115
  88.2 3.3 %collective-permute-start.8 = (bf16[192,512]{1,0:T(8,128)(2,1)S(1)}, bf16[192,512]{1,0:T(8,128)(2,1)S(1)}, u32[]{:S(2)}, u32[]{:S(2)}) collective-permute-start(bf16[192,512]{1,0:T(8,128)(2,1)S(1)} %get-tuple-element.18), channel_id=1, source_target_pairs={{0,8},{8,0},{16,24},{24,16},{32,40},{40,32},{48,56},{56,48},{64,72... | collective-permute-start | bytes 589832 | tf_op jit(solution)/shard_map/ppermute | solution.py:115
  91.5 1.5 copy-start.11
  93.0 109.1 %all-to-all-start.3 = ((bf16[8,256,512]{2,1,0:T(8,128)(2,1)}), bf16[8,256,512]{2,1,0:T(8,128)(2,1)S(1)}, u32[]{:S(2)}, u32[]{:S(2)}) async-start(bf16[8,256,512]{2,1,0:T(8,128)(2,1)} %shard_map.117), calls=%async_computation.3 | async-start | bytes 4194304 | tf_op jit(solution)/shard_map/all_to_all | solution.py:149
  202.1 5.5 %copy-start.10 = (bf16[8,256,512]{2,1,0:T(8,128)(2,1)}, bf16[8,256,512]{2,1,0:T(8,128)(2,1)S(1)}, u32[]{:S(2)}) copy-start(bf16[8,256,512]{2,1,0:T(8,128)(2,1)S(1)} %all-to-all-done.3.refs_0_) | copy-start | bytes 6291460
  202.1 34.6 %all-to-all-start.2 = ((bf16[8,64,512]{2,1,0:T(8,128)(2,1)}), bf16[8,64,512]{2,1,0:T(8,128)(2,1)S(1)}, u32[]{:S(2)}, u32[]{:S(2)}) async-start(bf16[8,64,512]{2,1,0:T(8,128)(2,1)} %shard_map.116.refs_1_), calls=%async_computation.2 | async-start | bytes 1048576 | tf_op jit(solution)/shard_map/all_to_all | solution.py:149
  207.6 29.1 %copy-start.3 = (f32[1,4,128,1280]{3,2,1,0:T(8,128)S(1)}, f32[1,4,128,1280]{3,2,1,0:T(8,128)}, u32[]{:S(2)}) copy-start(f32[1,4,128,1280]{3,2,1,0:T(8,128)} %features_ref.5) | copy-start | bytes 7864324
  235.2 1.5 collective-permute-start.9
  236.7 0.8 copy-start.7

commit v6 on v5

--- a/solution.py
+++ b/solution.py
@@ -469,7 +469,7 @@
     group = jnp.repeat(jnp.stack([mean, jnp.sqrt(var + 1e-06)]), per_group, axis=1)
     normed, done = normalise(features, group, shift, gn_gain, gn_bias)
 
-    mine = after(mine, done, vmem=2**20)
+    mine = after(mine, group, shift, vmem=2**20)
     theirs = other_core(mine)
     out_weights = (mine, theirs)
     first_mine, last_mine = project(normed, mine)

time: 244 us -> 243 us (level)
  the two profiles are of different devices: /device:TPU:2 before, /device:TPU:1 now
where the time goes in v6:
time: 243 us
  Pallas kernels  131 us (54%)
  starting transfers between devices  48.5 us (20%)
  waiting for transfers between devices  26.4 us (11%)
  blocking collectives  23.5 us (10%)
  local copies, waits for them, and re-layouts  10.7 us (4%)
    pallas_call x2, Pallas kernels, attend(): pl.pallas_call(functools.partial(attend_kernel, stride, split), grid=(blo...  114 us
    all_to_all x2, starting transfers between devices, across_chips(): lax.all_to_all(value, 'row', 0, 0, tiled=True, axis_index_groups=groups)  25.7 us
    ppermute x10, waiting for transfers between devices, move_row(): return lax.ppermute(value, 'row', [(r, target(r)) for r in range(16)])  25.2 us
    all_to_all x1, blocking collectives, across_chips(): lax.all_to_all(value, 'row', 0, 0, tiled=True, axis_index_groups=groups)  23.5 us
    ppermute x10, starting transfers between devices, move_row(): return lax.ppermute(value, 'row', [(r, target(r)) for r in range(16)])  14.3 us
    all_to_all x1, starting transfers between devices, local(): mine = lax.all_to_all(mine, 'col', 0, 0, tiled=True)  8.51 us
    unnamed x26, local copies, waits for them, and re-layouts  7.88 us
    pallas_call x2, Pallas kernels, project(): pl.pallas_call(project_kernel, grid=(width // lanes - skip,), in_specs=[p...  6.55 us
  transfers between devices with their start and end apart: 13, of which 7 were waited for; matrix products, arithmetic and copies ran while one was open for 1% of the time, Pallas kernels for 49%

profile of v6, /device:TPU:1, one launch (start us, length us, event | category | flops | bytes accessed | tf_op | source)
XLA Modules:
  0.0 242.5 jit_solution(1058226964114525172)
XLA Ops:
  0.0 3.1 %shard_map.112 = bf16[8,160,1280]{2,1,0:T(8,128)(2,1)} custom-call(s32[1]{0:T(128)} %bitcast.core_ref, bf16[160,640]{1,0:T(8,128)(2,1)} %query_ref.1, bf16[160,640]{1,0:T(8,128)(2,1)} %key_ref.1, bf16[160,640]{1,0:T(8,128)(2,1)} %value_ref.1, bf16[160,640]{1,0:T(8,128)(2,1)} %bitcast.13), custom_call_target="tpu_custom_call" | custom-call | tf_op jit(solution)/shard_map/pallas_call | solution.py:192
  3.1 8.5 %all-to-all-start = ((bf16[8,160,1280]{2,1,0:T(8,128)(2,1)}), bf16[8,160,1280]{2,1,0:T(8,128)(2,1)S(1)}, u32[]{:S(2)}, u32[]{:S(2)}) async-start(bf16[8,160,1280]{2,1,0:T(8,128)(2,1)} %shard_map.112), calls=%async_computation | async-start | bytes 6553600 | tf_op jit(solution)/shard_map/all_to_all | solution.py:459
  11.7 1.7 copy-done.1
  13.4 0.6 shard_map.110
  14.0 1.3 collective-permute-start
  15.3 2.5 %collective-permute-start.1 = (f32[2,1280]{1,0:T(2,128)S(1)}, f32[2,1280]{1,0:T(2,128)S(1)}, u32[]{:S(2)}, u32[]{:S(2)}) collective-permute-start(f32[2,1280]{1,0:T(2,128)S(1)} %shard_map.110), channel_id=1, source_target_pairs={{0,64},{8,72},{16,80},{24,88},{32,96},{40,104},{48,112},{56,120},{... | collective-permute-start | bytes 30728 | tf_op jit(solution)/shard_map/ppermute | solution.py:115
  17.7 1.2 collective-permute-start.2
  19.6 0.9 collective-permute-done.2
  20.5 0.1 fusion.3
  20.7 2.4 %collective-permute-start.3 = (f32[2,1280]{1,0:T(2,128)S(1)}, f32[2,1280]{1,0:T(2,128)S(1)}, u32[]{:S(2)}, u32[]{:S(2)}) collective-permute-start(f32[2,1280]{1,0:T(2,128)S(1)} %pad_maximum_fusion.1), channel_id=1, source_target_pairs={{0,8},{8,0},{16,24},{24,16},{32,40},{40,32},{48,56},{56,48},{64,72... | collective-permute-start | bytes 30728 | tf_op jit(solution)/shard_map/ppermute | solution.py:115
  23.1 0.4 collective-permute-start.4
  23.5 1.3 collective-permute-start.5
  24.8 0.1 pad_maximum_fusion.2
  24.9 0.1 broadcast_in_dim.20.table_ref
  25.0 0.0 copy-start.4
  25.1 2.9 %copy-done.4 = f32[1280,1280]{1,0:T(8,128)S(1)} copy-done((f32[1280,1280]{1,0:T(8,128)S(1)}, f32[1280,1280]{1,0:T(8,128)}, u32[]{:S(2)}) %copy-start.4) | copy-done | bytes 6553624
  27.9 1.2 shard_map.109.shift_ref.refs_2_
  29.1 0.1 add.249
  29.2 0.1 squeeze.20
  29.3 0.1 squeeze.21
  29.4 0.1 squeeze.44
  29.4 0.1 squeeze.45
  29.5 18.4 %collective-permute-done.4 = f32[2,1280]{1,0:T(2,128)S(1)} collective-permute-done((f32[2,1280]{1,0:T(2,128)S(1)}, f32[2,1280]{1,0:T(2,128)S(1)}, u32[]{:S(2)}, u32[]{:S(2)}) %collective-permute-start.4) | collective-permute-done | bytes 10272 | tf_op jit(solution)/shard_map/ppermute | solution.py:115
  48.0 1.4 collective-permute-done.5
  49.3 0.1 slice_reduce_fusion.2
  49.4 0.1 reshape.75
  49.5 0.1 squeeze.46
  49.6 0.1 squeeze.47
  49.7 0.1 squeeze.48
  49.8 0.1 squeeze.49
  49.9 0.1 squeeze.50
  49.9 0.1 squeeze.51
  50.0 0.1 reduce_sum.18
  50.1 0.2 add_reduce_fusion
  50.4 0.1 broadcast_in_dim.18
  50.4 0.1 reshape.76.group_ref.refs_1_
  50.5 0.0 copy-start.11
  50.6 0.0 copy-start.12
  50.6 1.3 all-to-all-done.refs_0_
  51.8 2.1 collective-permute-start.6
  53.9 0.0 copy-start.2
  54.0 1.7 copy-done.2
  55.7 1.0 shard_map.111
  56.7 2.6 %shard_map.114 = (bf16[1024,512]{1,0:T(8,128)(2,1)S(1)}, bf16[192,512]{1,0:T(8,128)(2,1)S(1)}) custom-call(bf16[512,1280]{1,0:T(8,128)(2,1)S(1)} %get-tuple-element.12.normed_ref, bf16[8,160,1280]{2,1,0:T(8,128)(2,1)S(1)} %shard_map.113.weight_ref.mine_ref), custom_call_target="tpu_custom_call" | custom-call | flops 1258291200 | bytes 4194304 | tf_op jit(solution)/shard_map/pallas_call | solution.py:224
  59.3 0.1 slice.75
  59.4 0.2 collective-permute-done.6.weight_ref.theirs_ref
  59.5 4.0 %shard_map.115 = (bf16[1024,512]{1,0:T(8,128)(2,1)S(1)}, bf16[192,512]{1,0:T(8,128)(2,1)S(1)}) custom-call(bf16[512,1280]{1,0:T(8,128)(2,1)S(1)} %get-tuple-element.12.normed_ref, bf16[8,160,1280]{2,1,0:T(8,128)(2,1)} %collective-permute-done.6.weight_ref.theirs_ref), custom_call_target="tpu_custom_call" | custom-call | flops 1258291200 | bytes 4194304 | tf_op jit(solution)/shard_map/pallas_call | solution.py:224
  63.5 0.1 slice.76
  63.6 0.3 maximum_select_fusion
  63.9 23.5 %all_to_all.20.query_low.query_high.refs_0_.refs_1_ = bf16[8,192,512]{2,1,0:T(8,128)(2,1)} all-to-all(bf16[8,192,512]{2,1,0:T(8,128)(2,1)S(1)} %bitcast.10), channel_id=1, replica_groups={{0,16,32,48,64,80,96,112},{8,24,40,56,72,88,104,120},{1,17,33,49,65,81,..., dimensions={0} | all-to-all | bytes 3145728 | tf_op jit(solution)/shard_map/all_to_all | solution.py:149
  87.3 2.5 %collective-permute-start.7 = (bf16[8,192,512]{2,1,0:T(8,128)(2,1)}, bf16[8,192,512]{2,1,0:T(8,128)(2,1)}, u32[]{:S(2)}, u32[]{:S(2)}) collective-permute-start(bf16[8,192,512]{2,1,0:T(8,128)(2,1)} %all_to_all.20.query_low.query_high.refs_0_.refs_1_), channel_id=1, source_target_pairs={{0,8},{8,0},{16,24},{24,16},{32,40},{40,32},{48,56},{56,48},{64,72... | collective-permute-start | bytes 4718600 | tf_op jit(solution)/shard_map/ppermute | solution.py:115
  89.8 0.0 collective-permute-start.8
  89.8 3.2 %collective-permute-done.8.query_high = bf16[192,512]{1,0:T(8,128)(2,1)S(1)} collective-permute-done((bf16[192,512]{1,0:T(8,128)(2,1)S(1)}, bf16[192,512]{1,0:T(8,128)(2,1)S(1)}, u32[]{:S(2)}, u32[]{:S(2)}) %collective-permute-start.8) | collective-permute-done | bytes 196640 | tf_op jit(solution)/shard_map/ppermute | solution.py:115
  93.0 0.7 copy-done.9
  93.7 1.5 broadcast_in_dim.19.refs_0_
  95.2 3.8 %all-to-all-start.3 = ((bf16[8,256,512]{2,1,0:T(8,128)(2,1)}), bf16[8,256,512]{2,1,0:T(8,128)(2,1)S(1)}, u32[]{:S(2)}, u32[]{:S(2)}) async-start(bf16[8,256,512]{2,1,0:T(8,128)(2,1)} %shard_map.117), calls=%async_computation.3 | async-start | bytes 4194304 | tf_op jit(solution)/shard_map/all_to_all | solution.py:149
  99.0 86.5 %shard_map.116.refs_1_ = bf16[8,64,512]{2,1,0:T(8,128)(2,1)} custom-call(bf16[8,192,512]{2,1,0:T(8,128)(2,1)} %all_to_all.20.query_low.query_high.refs_0_.refs_1_, bf16[8,192,512]{2,1,0:T(8,128)(2,1)} %all_to_all.20.query_low.query_high.refs_0_.refs_1_, bf16[8,192,512]{2,1,0:T(8,128)(2,1)} %all_to_all.20.query_low.query_high.refs_0_.refs_1_, ...), custom_call_target="tpu_custom_call" | custom-call | flops 42949672960 | bytes 8388608 | tf_op jit(solution)/shard_map/pallas_call | solution.py:378
  185.6 21.9 %all-to-all-start.2 = ((bf16[8,64,512]{2,1,0:T(8,128)(2,1)}), bf16[8,64,512]{2,1,0:T(8,128)(2,1)S(1)}, u32[]{:S(2)}, u32[]{:S(2)}) async-start(bf16[8,64,512]{2,1,0:T(8,128)(2,1)} %shard_map.116.refs_1_), calls=%async_computation.2 | async-start | bytes 1048576 | tf_op jit(solution)/shard_map/all_to_all | solution.py:149
  207.5 0.0 copy-start.3
  207.5 27.6 %shard_map.119 = (bf16[64,512]{1,0:T(8,128)(2,1)}, bf16[64,512]{1,0:T(8,128)(2,1)}) custom-call(bf16[192,512]{1,0:T(8,128)(2,1)} %copy-done.6, bf16[192,512]{1,0:T(8,128)(2,1)} %copy-done.9, bf16[8,256,512]{2,1,0:T(8,128)(2,1)} %shard_map.118.refs_0_), custom_call_target="tpu_custom_call" | custom-call | flops 10737418240 | bytes 8388608 | tf_op jit(solution)/shard_map/pallas_call | solution.py:378
  235.1 0.7 collective-permute-start.9
  235.8 1.1 collective-permute-done.9.far_ref
  236.9 0.8 copy-done.7
  237.8 4.8 %shard_map.120 = f32[1,4,128,1280]{3,2,1,0:T(8,128)} custom-call(s32[1]{0:T(128)} %bitcast.core_ref, f32[1,4,128,1280]{3,2,1,0:T(8,128)S(1)} %copy-done.3, f32[1,1280]{1,0:T(1,128)S(1)} %shard_map.109.shift_ref.refs_2_, bf16[8,64,512]{2,1,0:T(8,128)(2,1)S(1)} %all-to-all-done.2.first_ref, bf16[64,512]{1,0:T(8,128)(2,1)S(1)} %copy-done.7, ...), custom_call_target="tpu_custom_call" | custom-call | flops 838860800 | bytes 5242880 | tf_op jit(solution)/shard_map/pallas_call | solution.py:431
  (37 shorter events, 0.2 us)
Async XLA Ops:
  3.1 48.7 %all-to-all-start = ((bf16[8,160,1280]{2,1,0:T(8,128)(2,1)}), bf16[8,160,1280]{2,1,0:T(8,128)(2,1)S(1)}, u32[]{:S(2)}, u32[]{:S(2)}) async-start(bf16[8,160,1280]{2,1,0:T(8,128)(2,1)} %shard_map.112), calls=%async_computation | async-start | bytes 6553600 | tf_op jit(solution)/shard_map/all_to_all | solution.py:459
  11.7 1.7 copy-start.1
  13.4 11.6 %copy-start.10 = (f32[1280]{0:T(1024)S(1)}, f32[1280]{0:T(1024)}, u32[]{:S(2)}) copy-start(f32[1280]{0:T(1024)} %param.15) | copy-start | bytes 15364
  13.4 11.6 %copy-start.5 = (f32[320,1280]{1,0:T(8,128)S(1)}, f32[320,1280]{1,0:T(8,128)}, u32[]{:S(2)}) copy-start(f32[320,1280]{1,0:T(8,128)} %time_ref.1) | copy-start | bytes 4915204
  14.0 5.6 %collective-permute-start = (f32[2,1280]{1,0:T(2,128)S(1)}, f32[2,1280]{1,0:T(2,128)S(1)}, u32[]{:S(2)}, u32[]{:S(2)}) collective-permute-start(f32[2,1280]{1,0:T(2,128)S(1)} %shard_map.110), channel_id=1, source_target_pairs={{0,32},{8,40},{16,48},{24,56},{32,64},{40,72},{48,80},{56,88},{64,... | collective-permute-start | bytes 30728 | tf_op jit(solution)/shard_map/ppermute | solution.py:115
  15.3 4.3 %collective-permute-start.1 = (f32[2,1280]{1,0:T(2,128)S(1)}, f32[2,1280]{1,0:T(2,128)S(1)}, u32[]{:S(2)}, u32[]{:S(2)}) collective-permute-start(f32[2,1280]{1,0:T(2,128)S(1)} %shard_map.110), channel_id=1, source_target_pairs={{0,64},{8,72},{16,80},{24,88},{32,96},{40,104},{48,112},{56,120},{... | collective-permute-start | bytes 30728 | tf_op jit(solution)/shard_map/ppermute | solution.py:115
  17.7 2.8 %collective-permute-start.2 = (f32[2,1280]{1,0:T(2,128)S(1)}, f32[2,1280]{1,0:T(2,128)S(1)}, u32[]{:S(2)}, u32[]{:S(2)}) collective-permute-start(f32[2,1280]{1,0:T(2,128)S(1)} %shard_map.110), channel_id=1, source_target_pairs={{0,96},{8,104},{16,112},{24,120},{32,0},{40,8},{48,16},{56,24},{64... | collective-permute-start | bytes 30728 | tf_op jit(solution)/shard_map/ppermute | solution.py:115
  20.7 8.9 %collective-permute-start.3 = (f32[2,1280]{1,0:T(2,128)S(1)}, f32[2,1280]{1,0:T(2,128)S(1)}, u32[]{:S(2)}, u32[]{:S(2)}) collective-permute-start(f32[2,1280]{1,0:T(2,128)S(1)} %pad_maximum_fusion.1), channel_id=1, source_target_pairs={{0,8},{8,0},{16,24},{24,16},{32,40},{40,32},{48,56},{56,48},{64,72... | collective-permute-start | bytes 30728 | tf_op jit(solution)/shard_map/ppermute | solution.py:115
  23.1 24.9 %collective-permute-start.4 = (f32[2,1280]{1,0:T(2,128)S(1)}, f32[2,1280]{1,0:T(2,128)S(1)}, u32[]{:S(2)}, u32[]{:S(2)}) collective-permute-start(f32[2,1280]{1,0:T(2,128)S(1)} %pad_maximum_fusion.1), channel_id=1, source_target_pairs={{0,16},{8,24},{16,0},{24,8},{32,48},{40,56},{48,32},{56,40},{64,80... | collective-permute-start | bytes 30728 | tf_op jit(solution)/shard_map/ppermute | solution.py:115
  23.5 25.8 %collective-permute-start.5 = (f32[2,1280]{1,0:T(2,128)S(1)}, f32[2,1280]{1,0:T(2,128)S(1)}, u32[]{:S(2)}, u32[]{:S(2)}) collective-permute-start(f32[2,1280]{1,0:T(2,128)S(1)} %pad_maximum_fusion.1), channel_id=1, source_target_pairs={{0,24},{8,16},{16,8},{24,0},{32,56},{40,48},{48,40},{56,32},{64,88... | collective-permute-start | bytes 30728 | tf_op jit(solution)/shard_map/ppermute | solution.py:115
  25.0 2.9 %copy-start.4 = (f32[1280,1280]{1,0:T(8,128)S(1)}, f32[1280,1280]{1,0:T(8,128)}, u32[]{:S(2)}) copy-start(f32[1280,1280]{1,0:T(8,128)} %emb_ref.1) | copy-start | bytes 19660804
  50.5 3.4 %copy-start.11 = (f32[1280]{0:T(1024)S(1)}, f32[1280]{0:T(1024)}, u32[]{:S(2)}) copy-start(f32[1280]{0:T(1024)} %param.16) | copy-start | bytes 15364
  50.6 3.4 %copy-start.12 = (f32[1280]{0:T(1024)S(1)}, f32[1280]{0:T(1024)}, u32[]{:S(2)}) copy-start(f32[1280]{0:T(1024)} %param.17) | copy-start | bytes 15364
  51.8 7.4 %copy-start = (bf16[8,160,1280]{2,1,0:T(8,128)(2,1)}, bf16[8,160,1280]{2,1,0:T(8,128)(2,1)S(1)}, u32[]{:S(2)}) copy-start(bf16[8,160,1280]{2,1,0:T(8,128)(2,1)S(1)} %shard_map.113.weight_ref.mine_ref) | copy-start | bytes 9830404
  51.8 7.7 %collective-permute-start.6 = (bf16[8,160,1280]{2,1,0:T(8,128)(2,1)S(1)}, bf16[8,160,1280]{2,1,0:T(8,128)(2,1)}, u32[]{:S(2)}, u32[]{:S(2)}) collective-permute-start(bf16[8,160,1280]{2,1,0:T(8,128)(2,1)S(1)} %shard_map.113.weight_ref.mine_ref), channel_id=1, source_target_pairs={{0,8},{8,0},{16,24},{24,16},{32,40},{40,32},{48,56},{56,48},{64,72... | collective-permute-start | bytes 9830408 | tf_op jit(solution)/shard_map/ppermute | solution.py:115
  53.9 1.7 copy-start.2
  59.3 30.5 %copy-start.6 = (bf16[192,512]{1,0:T(8,128)(2,1)}, bf16[192,512]{1,0:T(8,128)(2,1)S(1)}, u32[]{:S(2)}) copy-start(bf16[192,512]{1,0:T(8,128)(2,1)S(1)} %get-tuple-element.15.query_low) | copy-start | bytes 589828
  87.3 11.7 %collective-permute-start.7 = (bf16[8,192,512]{2,1,0:T(8,128)(2,1)}, bf16[8,192,512]{2,1,0:T(8,128)(2,1)}, u32[]{:S(2)}, u32[]{:S(2)}) collective-permute-start(bf16[8,192,512]{2,1,0:T(8,128)(2,1)} %all_to_all.20.query_low.query_high.refs_0_.refs_1_), channel_id=1, source_target_pairs={{0,8},{8,0},{16,24},{24,16},{32,40},{40,32},{48,56},{56,48},{64,72... | collective-permute-start | bytes 4718600 | tf_op jit(solution)/shard_map/ppermute | solution.py:115
  89.8 3.2 %collective-permute-start.8 = (bf16[192,512]{1,0:T(8,128)(2,1)S(1)}, bf16[192,512]{1,0:T(8,128)(2,1)S(1)}, u32[]{:S(2)}, u32[]{:S(2)}) collective-permute-start(bf16[192,512]{1,0:T(8,128)(2,1)S(1)} %get-tuple-element.16), channel_id=1, source_target_pairs={{0,8},{8,0},{16,24},{24,16},{32,40},{40,32},{48,56},{56,48},{64,72... | collective-permute-start | bytes 589832 | tf_op jit(solution)/shard_map/ppermute | solution.py:115
  93.0 0.7 copy-start.9
  95.2 90.3 %all-to-all-start.3 = ((bf16[8,256,512]{2,1,0:T(8,128)(2,1)}), bf16[8,256,512]{2,1,0:T(8,128)(2,1)S(1)}, u32[]{:S(2)}, u32[]{:S(2)}) async-start(bf16[8,256,512]{2,1,0:T(8,128)(2,1)} %shard_map.117), calls=%async_computation.3 | async-start | bytes 4194304 | tf_op jit(solution)/shard_map/all_to_all | solution.py:149
  185.5 21.9 %copy-start.8 = (bf16[8,256,512]{2,1,0:T(8,128)(2,1)}, bf16[8,256,512]{2,1,0:T(8,128)(2,1)S(1)}, u32[]{:S(2)}) copy-start(bf16[8,256,512]{2,1,0:T(8,128)(2,1)S(1)} %all-to-all-done.3.refs_0_) | copy-start | bytes 6291460
  185.6 51.4 %all-to-all-start.2 = ((bf16[8,64,512]{2,1,0:T(8,128)(2,1)}), bf16[8,64,512]{2,1,0:T(8,128)(2,1)S(1)}, u32[]{:S(2)}, u32[]{:S(2)}) async-start(bf16[8,64,512]{2,1,0:T(8,128)(2,1)} %shard_map.116.refs_1_), calls=%async_computation.2 | async-start | bytes 1048576 | tf_op jit(solution)/shard_map/all_to_all | solution.py:149
  207.5 29.5 %copy-start.3 = (f32[1,4,128,1280]{3,2,1,0:T(8,128)S(1)}, f32[1,4,128,1280]{3,2,1,0:T(8,128)}, u32[]{:S(2)}) copy-start(f32[1,4,128,1280]{3,2,1,0:T(8,128)} %features_ref.5) | copy-start | bytes 7864324
  235.1 1.8 collective-permute-start.9
  236.9 0.8 copy-start.7
